TPU v7x, 512 devices: a whole 4x8x8 slice. The times are simulated.
512 devices in a mesh: tm: 32 (over z, x), series: 16 (over y, core).
Axes of the slice: x: 4, y: 8, z: 8, core: 2. Of those that a mesh axis runs over, the one named last changes fastest.
Arguments:
- readings: bfloat16 [512, 16384], P('tm', 'series'), may hold values from -8 to 8
- present: int32 [512, 16384], P('tm', 'series'), may hold values 0 or 1
- loadings: bfloat16 [16384, 128], P('series'), may hold values from -1 to 1
- noise_precision: float32 [16384], P('series'), may hold values from 0.5 to 2
- update_gain: float32 [128], replicated, may hold values from 7.8125e-06 to 0.0078125
- factor_rate: float32 [128], replicated, may hold values from 0.0001 to 0.01
- smooth_rate: float32 [128], replicated, may hold values from 0.0001 to 0.05
- regions: int32 [16384], P('series'), may hold values from 0 to 15
Outputs:
- smoothed: float32 [512, 128], P('tm')
- histogram: float32 [16, 20], replicated
All inputs are finite; a program needn't handle non-finite values. No bound on the sum of `present` on one device may be relied on, other than what follows from the above.
Results may differ from a plain program's by a relative error of at most 0.0004.
Values sent between devices are 32-bit elements; how exact they have to be, the bound alone decides.
No kernel may reach another device: no remote copies, remote signals or barrier semaphores. Data moves between devices by JAX's collectives and lax.ppermute only.
A program may use at most 64 MiB of HBM per device.

v0:
```python
import jax
import jax.numpy as jnp
from jax import lax
from jax.sharding import Mesh
from jax.sharding import PartitionSpec as P

BINS = 20
GROUPS = 16
SERIES = ("series_0", "series_1")
TM = ("tm_0", "tm_1")


highest = lax.Precision.HIGHEST


def in_blocks(shard, dim, count):
    before, after = (shard.shape[:dim], shard.shape[dim + 1 :])
    return jnp.moveaxis(shard.reshape(*before, count, -1, *after), dim, 0)


def sent_and_summed(shard, axis, dim):
    count = lax.axis_size(axis)
    tiles = lax.all_to_all(in_blocks(shard, dim, count), axis, 0, 0, tiled=True)
    return jnp.sum(tiles, axis=0)


def summed_rows(shard, axes, dim):
    far, near = axes
    tiles = in_blocks(shard, dim, lax.axis_size(far))
    nearer = sent_and_summed(tiles, near, dim + 1)
    arrived = lax.all_to_all(nearer, far, split_axis=0, concat_axis=0, tiled=True)
    return arrived.sum(axis=0)


def rows_for(lines, count):
    spare = -lines.shape[0] % count
    if not spare:
        return lines
    return jnp.concatenate([lines, jnp.zeros((spare, *lines.shape[1:]), lines.dtype)])


def sent_to_all(shard, axis):
    count = lax.axis_size(axis)
    return lax.all_to_all(
        jnp.broadcast_to(shard[None], (count, *shard.shape)), axis, 0, 0, tiled=True
    )


def in_order(tiles, dim):
    shape = list(tiles.shape[1:])
    shape[dim] *= tiles.shape[0]
    return jnp.moveaxis(tiles, 0, dim).reshape(shape)


def gather_axes(shard, axes, dim):
    far, near = axes
    tiles = sent_to_all(sent_to_all(shard, far), near)
    return in_order(tiles.swapaxes(0, 1).reshape(-1, *shard.shape), dim)


def total_of(shard, axes):
    own = summed_rows(rows_for(shard, lax.axis_size(axes[0]) * lax.axis_size(axes[1])), axes, 0)
    whole = gather_axes(own, axes, 0)
    return whole[: len(shard)].reshape(shard.shape)


def in_one(arrays, axis):
    ravelled, at, finished = (jnp.concatenate([a.reshape(-1) for a in arrays]), 0, [])
    subtotal = total_of(ravelled, axis)
    for a in arrays:
        finished.append(subtotal[at : at + a.size].reshape(a.shape))
        at += a.size
    return tuple(finished)


def filled_with(shard, identity):
    return jax.tree.map(
        lambda part, zero: jnp.zeros_like(part) + jnp.asarray(zero, part.dtype), shard, identity
    )


def gathered_once(shard, axis):
    leaves = jax.tree.leaves(shard)
    sequence = sorted(range(len(leaves)), key=lambda k: -leaves[k].size)
    width = (1, *leaves[sequence[0]].shape)[-1]
    lines = [
        jnp.pad(leaves[k].reshape(-1), (0, -leaves[k].size % width)).reshape(-1, width)
        for k in sequence
    ]
    both, at, found = (lax.all_gather(jnp.concatenate(lines), axis), 0, {})
    for k, line in zip(sequence, lines):
        section = both[:, at : at + len(line)].reshape(len(both), -1)
        found[k] = section[:, : leaves[k].size].reshape(-1, *leaves[k].shape)
        at += len(line)
    numbers = iter(range(len(leaves)))
    return jax.tree.map(lambda _: found[next(numbers)], shard)


def prefix_by_axis(shard, axes, combine, identity):
    before = start = filled_with(shard, identity)
    subtotal = shard
    for axis in reversed(axes):
        count, position = (lax.axis_size(axis), lax.axis_index(axis))
        pieces = gathered_once(subtotal, axis)
        inside, subtotal = (start, start)
        for k in range(count):
            passed = k < position
            subtotal = combine(subtotal, jax.tree.map(lambda part: part[k], pieces))
            inside = jax.tree.map(lambda new, old: jnp.where(passed, new, old), subtotal, inside)
        before = combine(inside, before)
    return before


def gathered_once_2(shard, axis):
    leaves = jax.tree.leaves(shard)
    sequence = sorted(range(len(leaves)), key=lambda k: -leaves[k].size)
    width = (1, *leaves[sequence[0]].shape)[-1]
    lines = [
        jnp.pad(leaves[k].reshape(-1), (0, -leaves[k].size % width)).reshape(-1, width)
        for k in sequence
    ]
    both, at, found = (sent_to_all(jnp.concatenate(lines), axis), 0, {})
    for k, line in zip(sequence, lines):
        section = both[:, at : at + len(line)].reshape(len(both), -1)
        found[k] = section[:, : leaves[k].size].reshape(-1, *leaves[k].shape)
        at += len(line)
    numbers = iter(range(len(leaves)))
    return jax.tree.map(lambda _: found[next(numbers)], shard)


def once_a_type(shard, axis):
    leaves, found = (jax.tree.leaves(shard), {})
    for initial, a in enumerate(leaves):
        if initial not in found:
            alike = [k for k, b in enumerate(leaves) if b.dtype == a.dtype]
            got = (
                gathered_once_2([leaves[k] for k in alike], axis)
                if len(alike) > 1
                else [sent_to_all(a, axis)]
            )
            for k, b in zip(alike, got):
                found[k] = b
    numbers = iter(range(len(leaves)))
    return jax.tree.map(lambda _: found[next(numbers)], shard)


def joined_by_halves(pieces, combine):
    while len(jax.tree.leaves(pieces)[0]) > 1:
        pieces = jax.vmap(combine)(
            *(jax.tree.map(lambda part: part[side::2], pieces) for side in (0, 1))
        )
    return jax.tree.map(lambda part: part[0], pieces)


def carried_in(shard, axis, combine, identity):
    count, position = (lax.axis_size(axis), lax.axis_index(axis))
    passed = jnp.arange(count) > position

    def kept(part, zero, own):
        part = jnp.where(
            passed.reshape(-1, *(1 for _ in own.shape)), part, jnp.asarray(zero, own.dtype)
        )
        return part[::-1]

    pieces = once_a_type(shard, axis)
    return joined_by_halves(jax.tree.map(kept, pieces, identity, shard), combine)


def taken_together(shard, axis):
    return sent_to_all(shard, axis).sum(axis=0)


def over_axes(shard, axes):
    far, near = axes
    return taken_together(taken_together(shard, near), far)


def normal_cdf(values):
    return 0.5 * (1.0 + lax.erf(values * 0.7071067811865476))


def compose_pair(earlier, later):
    return (
        jnp.dot(later[0], earlier[0], precision=highest),
        jnp.dot(later[0], earlier[1], precision=highest) + later[1],
    )


def scale_pair(earlier, later):
    return (later[0] * earlier[0], later[0] * earlier[1] + later[1])


def local_information(readings, weight, loadings):

    def per_hour(hour):
        scaled = (loadings * weight[hour][:, None]).astype(jnp.bfloat16)
        inform = lax.dot_general(
            scaled, loadings, (((0,), (0,)), ((), ())), preferred_element_type=jnp.float32
        )
        scores = jnp.dot(readings[hour], scaled, preferred_element_type=jnp.float32)
        return (inform, scores)

    return lax.map(per_hour, jnp.arange(readings.shape[0]))


def block_element(inform, scores, update_gain, decays):
    factors = inform.shape[1]
    identity = jnp.eye(factors, dtype=jnp.float32)
    transit = (identity[None] - update_gain[None, :, None] * inform) * decays[None, None, :]
    forcing = update_gain[None, :] * scores

    def block_step(running, stepped):
        return (compose_pair(running, stepped), None)

    (composed, shifted), _ = lax.scan(
        block_step, (identity, jnp.zeros((factors,), jnp.float32)), (transit, forcing)
    )
    return (transit, forcing, composed, shifted)


def run_filter(transit, forcing, start):

    def run_step(current, stepped):
        current = jnp.dot(stepped[0], current, precision=highest) + stepped[1]
        return (current, current)

    _, filtered = lax.scan(run_step, start, (transit, forcing))
    return filtered


def smoother_parts(filtered, decays, retain, smooth_rate):

    def smoother_step(following, filter_row):
        smooth_row = (1.0 - retain * decays) * filter_row + retain * following
        return (smooth_row, smooth_row)

    _, partial_value = lax.scan(smoother_step, jnp.zeros_like(filtered[0]), filtered, reverse=True)
    length = filtered.shape[0]
    distance = (length - jnp.arange(length)).astype(jnp.float32)
    powers = jnp.exp(-distance[:, None] * smooth_rate[None, :])
    boundary = decays * filtered[-1]
    return (partial_value, powers, boundary)


def end_element(partial_value, powers, boundary, at_end):
    element_gain = jnp.where(at_end, jnp.zeros_like(powers[0]), powers[0])
    element_shift = jnp.where(at_end, partial_value[0] + powers[0] * boundary, partial_value[0])
    return (element_gain, element_shift)


def body(
    readings, present, loadings, noise_precision, update_gain, factor_rate, smooth_rate, regions
):
    decays = jnp.exp(-factor_rate)
    retain = jnp.exp(-smooth_rate)
    weight = present.astype(jnp.float32) * noise_precision[None, :]
    inform, scores = local_information(readings, weight, loadings)
    factors = loadings.shape[1]
    identity = jnp.eye(factors, dtype=jnp.float32)
    nothing = jnp.zeros((factors,), jnp.float32)
    all_ones = jnp.ones((factors,), jnp.float32)
    inform, scores = in_one((inform, scores), ("series_0", "series_1"))
    transit, forcing, composed, shifted = block_element(inform, scores, update_gain, decays)
    leading = prefix_by_axis((composed, shifted), TM, compose_pair, (identity, nothing))
    filtered = run_filter(transit, forcing, leading[1])
    partial_value, powers, boundary = smoother_parts(filtered, decays, retain, smooth_rate)
    at_end = lax.axis_index(TM) == lax.axis_size(TM) - 1
    element_gain, element_shift = end_element(partial_value, powers, boundary, at_end)
    trailing = carried_in((element_gain, element_shift), TM, scale_pair, (all_ones, nothing))
    smoothed = partial_value + powers * (trailing[0] * boundary + trailing[1])[None, :]
    fitted = lax.dot_general(
        smoothed.astype(jnp.bfloat16),
        loadings,
        (((1,), (1,)), ((), ())),
        preferred_element_type=jnp.float32,
    )
    standard = (readings.astype(jnp.float32) - fitted) * jnp.sqrt(noise_precision)[None, :]
    probab = normal_cdf(standard)
    observed = present.astype(jnp.float32)
    member = (regions[:, None] == jnp.arange(GROUPS)[None, :]).astype(jnp.float32)
    binned = []
    for bin_index in range(BINS):
        kernel = jnp.maximum(0.0, 1.0 - BINS * jnp.abs(probab - (bin_index + 0.5) / BINS))
        binned.append(jnp.sum(observed * kernel, axis=0))
    bin_table = jnp.stack(binned)
    tallies = jnp.dot(bin_table, member, precision=highest)
    hours_all = readings.shape[0] * lax.axis_size(TM)
    series_all = readings.shape[1] * lax.axis_size(SERIES)
    local_hist = tallies.T * (BINS * GROUPS / (hours_all * series_all))
    histogram = over_axes(local_hist, ("tm_0", ("tm_1", "series_0", "series_1")))
    return (smoothed, histogram)


def solution(mesh):
    split = Mesh(mesh.devices.reshape(8, 4, 8, 2), ("tm_0", "tm_1", "series_0", "series_1"))
    in_specs = (P(TM, SERIES), P(TM, SERIES), P(SERIES, None), P(SERIES), P(), P(), P(), P(SERIES))
    out_specs = (P(TM, None), P())
    return jax.shard_map(body, mesh=split, in_specs=in_specs, out_specs=out_specs, check_vma=False)
```

profile of v0, /device:TPU:1, one launch (start us, length us, event | category | flops | bytes accessed | tf_op | source)
XLA Modules:
  0.0 255.8 jit_solution(17537365856544556412)
XLA Ops:
  1.5 85.4 %while.54 = (s32[]{:T(128)}, f32[16,128,128]{2,1,0:T(8,128)S(1)}, f32[16,128]{1,0:T(8,128)S(1)}, bf16[1024,128]{1,0:T(8,128)(2,1)}, s32[16]{0:T(128)S(1)}, /*ind...) while((s32[]{:T(128)}, f32[16,128,128]{2,1,0:T(8,128)S(1)}, ...), condition=%wide.region_1.2_spmd, body=%wide.region_0.1_spmd.sunk | while | flops 34603012 | bytes 874155 | solution.py:203
  4.1 1.3 fusion.116
  5.4 1.5 fusion.115
  9.4 1.3 fusion.116
  10.7 1.5 fusion.115
  14.7 1.3 fusion.116
  16.1 1.5 fusion.115
  20.1 1.3 fusion.116
  21.4 1.5 fusion.115
  25.4 1.3 fusion.116
  26.7 1.5 fusion.115
  30.8 1.3 fusion.116
  32.1 1.5 fusion.115
  36.1 1.3 fusion.116
  37.4 1.5 fusion.115
  41.4 1.3 fusion.116
  42.7 1.5 fusion.115
  46.8 1.3 fusion.116
  48.1 1.5 fusion.115
  52.1 1.3 fusion.116
  53.4 1.5 fusion.115
  57.4 1.3 fusion.116
  58.7 1.5 fusion.115
  62.8 1.3 fusion.116
  64.1 1.5 fusion.115
  68.1 1.3 fusion.116
  69.4 1.5 fusion.115
  73.4 1.3 fusion.116
  74.7 1.5 fusion.115
  78.8 1.3 fusion.116
  80.1 1.5 fusion.115
  84.1 1.3 fusion.116
  85.4 1.5 fusion.115
  87.7 11.1 %all_to_all.41 = f32[2,8,16512]{2,1,0:T(8,128)S(1)} all-to-all(f32[2,8,16512]{2,1,0:T(8,128)S(1)} %copy.28), channel_id=1, replica_groups=mesh['tm_0'=8,'tm_1'=4,'series_0'=8,'series_1'=2] {'series_1'}, dimensions={0} | all-to-all | bytes 2113536 | tf_op jit(solution)/shard_map/all_to_all | solution.py:23
  99.2 20.4 %all_to_all.42 = f32[8,1,16512]{2,1,0:T(1,128)S(1)} all-to-all(f32[8,1,16512]{2,1,0:T(1,128)S(1)} %all_to_all.26), channel_id=1, replica_groups=mesh['tm_0'=8,'tm_1'=4,'series_0'=8,'series_1'=2] {'series_0'}, dimensions={0} | all-to-all | bytes 1056768 | tf_op jit(solution)/shard_map/all_to_all | solution.py:31
  120.1 1.1 broadcast_in_dim.85
  121.1 3.5 %all-to-all-start.2 = ((f32[8,1,16512]{2,1,0:T(1,128)}), f32[8,1,16512]{2,1,0:T(1,128)S(1)}, u32[]{:S(2)}, u32[]{:S(2)}) async-start(f32[8,1,16512]{2,1,0:T(1,128)} %broadcast_in_dim.85), calls=%async_computation.2 | async-start | bytes 1056768 | tf_op jit(solution)/shard_map/all_to_all | solution.py:44
  124.9 17.7 %all-to-all-done.2 = f32[8,1,16512]{2,1,0:T(1,128)S(1)} async-done(((f32[8,1,16512]{2,1,0:T(1,128)}), f32[8,1,16512]{2,1,0:T(1,128)S(1)}, u32[]{:S(2)}, u32[]{:S(2)}) %all-to-all-start.2) | async-done | bytes 528416 | tf_op jit(solution)/shard_map/all_to_all | solution.py:44
  142.7 4.7 %all_to_all.40 = f32[2,8,16512]{2,1,0:T(8,128)S(1)} all-to-all(f32[2,8,16512]{2,1,0:T(8,128)S(1)} %broadcast_in_dim.87), channel_id=1, replica_groups=mesh['tm_0'=8,'tm_1'=4,'series_0'=8,'series_1'=2] {'series_1'}, dimensions={0} | all-to-all | bytes 2113536 | tf_op jit(solution)/shard_map/all_to_all | solution.py:44
  150.6 7.7 %while.56 = (s32[]{:T(128)}, f32[128,128]{1,0:T(8,128)S(1)}, f32[128]{0:T(128)S(1)}, f32[16,128,128]{2,1,0:T(8,128)S(1)}, f32[16,128]{1,0:T(8,128)S(1)}, /*index=5*/s32[]{:T(128)}, s32[]{:T(128)}) while((s32[]{:T(128)}, f32[128,128]{1,0:T(8,128)S(1)}, f32[128]{0:T(128)S(1)}, f32[16,128,128]{2,1,0:T(8,128)S(1)}, ...), condition=%wide.region_5.6_spmd.clone, body=%wide.region_4.5_spmd.clone.sunk | while | flops 25362688 | bytes 397410 | solution.py:215
  158.3 9.4 %all-gather.2 = f32[4,129,128]{2,1,0:T(8,128)S(1)} all-gather(f32[1,129,128]{2,1,0:T(8,128)S(1)} %maximum_bitcast_fusion), channel_id=2, replica_groups=mesh['tm_0'=8,'tm_1'=4,'series_0'=8,'series_1'=2] {'tm_1'}, dimensions={0}, use_global_device_ids=true | all-gather | bytes 330240 | tf_op jit(solution)/shard_map/all_gather | solution.py:90
  169.4 24.5 %all-gather.3 = f32[8,129,128]{2,1,0:T(8,128)S(1)} all-gather(f32[1,129,128]{2,1,0:T(8,128)S(1)} %maximum_bitcast_fusion.1), channel_id=3, replica_groups=mesh['tm_0'=8,'tm_1'=4,'series_0'=8,'series_1'=2] {'tm_0'}, dimensions={0}, use_global_device_ids=true | all-gather | bytes 594432 | tf_op jit(solution)/shard_map/all_gather | solution.py:90
  196.3 4.4 %while.55 = (s32[]{:T(128)}, f32[128]{0:T(128)S(1)}, f32[16,128]{1,0:T(8,128)S(1)}, f32[16,128,128]{2,1,0:T(8,128)S(1)}, f32[16,128]{1,0:T(8,128)S(1)}, /*index=5*/s32[]{:T(128)}, s32[]{:T(128)}) while((s32[]{:T(128)}, f32[128]{0:T(128)S(1)}, f32[16,128]{1,0:T(8,128)S(1)}, f32[16,128,128]{2,1,0:T(8,128)S(1)}, f32[16,128]{1,0:T(8,128)S(1)}, ...), condition=%wide.region_7.8_spmd, body=%wide.region_6.7_spmd.sunk | while | flops 196738 | bytes 70233 | solution.py:227
  200.7 1.2 while.57
  202.6 5.5 %all-to-all-start.4 = ((f32[32,2,128]{2,1,0:T(2,128)}), f32[32,2,128]{2,1,0:T(2,128)S(1)}, u32[]{:S(2)}, u32[]{:S(2)}) async-start(f32[32,2,128]{2,1,0:T(2,128)} %broadcast_in_dim.89), calls=%async_computation.4 | async-start | bytes 65536 | tf_op jit(solution)/shard_map/all_to_all | solution.py:44
  208.1 8.7 %all-to-all-done.4 = f32[32,2,128]{2,1,0:T(2,128)S(1)} async-done(((f32[32,2,128]{2,1,0:T(2,128)}), f32[32,2,128]{2,1,0:T(2,128)S(1)}, u32[]{:S(2)}, u32[]{:S(2)}) %all-to-all-start.4) | async-done | bytes 32800 | tf_op jit(solution)/shard_map/all_to_all | solution.py:44
  219.2 24.3 %all_to_all.43 = f32[64,1,320]{2,1,0:T(1,128)S(1)} all-to-all(f32[64,1,320]{2,1,0:T(1,128)S(1)} %reshape.156), channel_id=1, replica_groups=mesh['tm_0'=8,'tm_1'=4,'series_0'=8,'series_1'=2] {'tm_1','series_0','se..., dimensions={0} | all-to-all | bytes 163840 | tf_op jit(solution)/shard_map/all_to_all | solution.py:44
  245.4 9.0 %all_to_all.44 = f32[8,1,320]{2,1,0:T(1,128)S(1)} all-to-all(f32[8,1,320]{2,1,0:T(1,128)S(1)} %reshape.158), channel_id=1, replica_groups=mesh['tm_0'=8,'tm_1'=4,'series_0'=8,'series_1'=2] {'tm_0'}, dimensions={0} | all-to-all | bytes 20480 | tf_op jit(solution)/shard_map/all_to_all | solution.py:44
  (305 shorter events, 37.9 us)
Async XLA Ops:
  119.7 5.1 %copy-start.2 = (f32[1024]{0:T(1024)S(1)}, f32[1024]{0:T(1024)}, u32[]{:S(2)}) copy-start(f32[1024]{0:T(1024)} %param.19) | copy-start | bytes 12292
  119.7 5.1 %copy-start.4 = (f32[128]{0:T(128)S(1)}, f32[128]{0:T(128)}, u32[]{:S(2)}) copy-start(f32[128]{0:T(128)} %param.22) | copy-start | bytes 1540
  119.7 5.1 %copy-start.5 = (f32[128]{0:T(128)S(1)}, f32[128]{0:T(128)}, u32[]{:S(2)}) copy-start(f32[128]{0:T(128)} %param.21) | copy-start | bytes 1540
  121.1 21.5 %all-to-all-start.2 = ((f32[8,1,16512]{2,1,0:T(1,128)}), f32[8,1,16512]{2,1,0:T(1,128)S(1)}, u32[]{:S(2)}, u32[]{:S(2)}) async-start(f32[8,1,16512]{2,1,0:T(1,128)} %broadcast_in_dim.85), calls=%async_computation.2 | async-start | bytes 1056768 | tf_op jit(solution)/shard_map/all_to_all | solution.py:44
  149.7 0.7 copy-start.6
  194.6 22.7 %copy-start = (bf16[1024,128]{1,0:T(8,128)(2,1)S(1)}, bf16[1024,128]{1,0:T(8,128)(2,1)}, u32[]{:S(2)}) copy-start(bf16[1024,128]{1,0:T(8,128)(2,1)} %get-tuple-element.587) | copy-start | bytes 786436
  194.6 22.7 %copy-start.1 = (s32[16,1024]{1,0:T(8,128)S(1)}, s32[16,1024]{1,0:T(8,128)}, u32[]{:S(2)}) copy-start(s32[16,1024]{1,0:T(8,128)} %param.17) | copy-start | bytes 196612
  194.6 22.7 %copy-start.7 = (bf16[16,1024]{1,0:T(8,128)(2,1)S(1)}, bf16[16,1024]{1,0:T(8,128)(2,1)}, u32[]{:S(2)}) copy-start(bf16[16,1024]{1,0:T(8,128)(2,1)} %get-tuple-element.593) | copy-start | bytes 98308
  202.6 14.2 %all-to-all-start.4 = ((f32[32,2,128]{2,1,0:T(2,128)}), f32[32,2,128]{2,1,0:T(2,128)S(1)}, u32[]{:S(2)}, u32[]{:S(2)}) async-start(f32[32,2,128]{2,1,0:T(2,128)} %broadcast_in_dim.89), calls=%async_computation.4 | async-start | bytes 65536 | tf_op jit(solution)/shard_map/all_to_all | solution.py:44
  217.3 0.7 copy-start.3
  217.3 0.8 copy-start.8
where the time goes:
time: 258 us; the launch traced here: 256 us
  blocking collectives  103 us (40%)
  matrix products  58.9 us (23%)
  loops' own time  33 us (13%)
  waiting for transfers between devices  26.4 us (10%)
  local copies, waits for them, and re-layouts  19.4 us (8%)
  starting transfers between devices  9.02 us (3%)
  other arithmetic  4.53 us (2%)
    all_to_all x3, blocking collectives, sent_to_all(): lax.all_to_all(jnp.broadcast_to(shard[None], (count, *shard.shape)), axis...  37.9 us
    all_gather x2, blocking collectives, gathered_once(): both, at, found = (lax.all_gather(jnp.concatenate(lines), axis), 0, {})  33.9 us
    another operation x1, loops' own time, local_information(): return lax.map(per_hour, jnp.arange(readings.shape[0]))  31.6 us
    all_to_all x2, waiting for transfers between devices, sent_to_all(): lax.all_to_all(jnp.broadcast_to(shard[None], (count, *shard.shape)), axis...  26.4 us
    dot_general x16, matrix products, per_hour(): lax.dot_general(scaled, loadings, (((0,), (0,)), ((), ())), preferred_ele...  23.2 us
    dot_general x16, matrix products, per_hour(): scores = jnp.dot(readings[hour], scaled, preferred_element_type=jnp.float32)  20.6 us
    all_to_all x1, blocking collectives, summed_rows(): lax.all_to_all(nearer, far, split_axis=0, concat_axis=0, tiled=True)  20.4 us
    all_to_all x1, blocking collectives, sent_and_summed(): tiles = lax.all_to_all(in_blocks(shard, dim, count), axis, 0, 0, tiled=True)  11.1 us
  transfers between devices with their start and end apart: 2, of which 2 were waited for; matrix products, arithmetic and copies ran while one was open for 0% of the time, Pallas kernels for 0%

commit v1 on v0

v1 whole, which is shorter than its diff:
```python
import jax
import jax.numpy as jnp
from jax import lax
from jax.experimental import pallas as pl
from jax.experimental.pallas import tpu as pltpu
from jax.sharding import Mesh
from jax.sharding import PartitionSpec as P

BINS = 20
GROUPS = 16
SERIES = ("y", "c")
TM = ("z", "x")
F32 = jnp.float32
BF16 = jnp.bfloat16
VM = pl.BlockSpec(memory_space=pltpu.VMEM)
SM = pl.BlockSpec(memory_space=pltpu.SMEM)
PARAMS = pltpu.CompilerParams(vmem_limit_bytes=40 * 1024 * 1024)


def iotas(rows, lanes):
    shape = (rows, lanes)
    return lax.broadcasted_iota(jnp.int32, shape, 0), lax.broadcasted_iota(jnp.int32, shape, 1)


def halves(a):
    high = a.astype(BF16)
    return high, (a - high.astype(F32)).astype(BF16)


def bdot(a, b):
    return jnp.dot(a, b, preferred_element_type=F32)


def dot3(a, b):
    ah, al = halves(a)
    bh, bl = halves(b)
    return bdot(ah, bh) + (bdot(ah, bl) + bdot(al, bh))


def across(a, b):
    return lax.dot_general(a, b, (((1,), (1,)), ((), ())), preferred_element_type=F32)


def joined(earlier, later):
    k = later.shape[1]
    product = dot3(earlier, later[:k])
    return jnp.concatenate([product[:k], product[k:] + later[k:]], axis=0)


def information_kernel(readings, present, loadings, noise, out):
    hours = readings.shape[0]
    load = loadings[...]
    k = load.shape[1]
    half = k // 2
    scaled = (jnp.transpose(load.astype(F32)) * noise[...]).astype(BF16)
    seen = present[...].astype(F32).astype(BF16)
    scores = across(readings[...] * seen, scaled)
    row, lane = iotas(half, k)
    row_k, lane_k = iotas(k, k)
    for h in range(hours):
        inform = bdot(scaled * seen[h : h + 1, :], load)
        folded = pltpu.roll(inform[half:], half, 1)
        out[h, :half] = jnp.where(lane >= row, inform[:half], folded)
        diagonal = jnp.sum(jnp.where(row_k == lane_k, inform, 0.0), axis=0, keepdims=True)
        out[h, half:] = jnp.concatenate(
            [diagonal, scores[h : h + 1], jnp.zeros((6, k), F32)], axis=0
        )


def block_kernel(packed, gain, factor_rate, leaves, pairs, quads, eighths, total):
    hours = packed.shape[0]
    k = packed.shape[2]
    half = k // 2
    gain_row = gain[...]
    decay_col = jnp.transpose(jnp.broadcast_to(jnp.exp(-factor_rate[...]), (k, k)))
    row, lane = iotas(half, k)
    row_k, lane_k = iotas(k, k)
    on_diag = row_k == lane_k
    identity = on_diag.astype(F32)
    maps = []
    for h in range(hours):
        page = packed[h]
        top = page[:half]
        upper = jnp.where(lane >= row, top, 0.0)
        lower = pltpu.roll(jnp.where(lane < row, top, 0.0), half, 1)
        part = jnp.concatenate([upper, lower], axis=0)
        inform = jnp.where(on_diag, page[half : half + 1], part + jnp.transpose(part))
        matrix = (identity - inform * gain_row) * decay_col
        shift = gain_row * page[half + 1 : half + 2]
        one = jnp.concatenate([matrix, shift, jnp.zeros((7, k), F32)], axis=0)
        leaves[h] = one
    for i in range(hours // 2):
        pairs[i] = joined(leaves[2 * i], leaves[2 * i + 1])
    for i in range(hours // 4):
        quads[i] = joined(pairs[2 * i], pairs[2 * i + 1])
    for i in range(hours // 8):
        eighths[i] = joined(quads[2 * i], quads[2 * i + 1])
    total[...] = joined(eighths[0], eighths[1])


def four_kernel(blocks, total):
    total[...] = joined(joined(blocks[0], blocks[1]), joined(blocks[2], blocks[3]))


def applied(current, one):
    k = one.shape[1]
    return dot3(current, one[:k]) + one[k : k + 1]


def filter_kernel(
    place, planes, blocks, leaves, pairs, quads, eighths, factor_rate, smooth_rate, partial, sent, last
):
    k = factor_rate.shape[1]
    z, x, at_end = place[0], place[1], place[2]
    current = jnp.zeros((8, k), F32)
    for i in range(planes.shape[0] - 1):
        current = jnp.where(i < z, applied(current, planes[i]), current)
    for i in range(blocks.shape[0] - 1):
        current = jnp.where(i < x, applied(current, blocks[i]), current)
    after = {-1: current}
    after[7] = applied(current, eighths[0])
    after[3] = applied(current, quads[0])
    after[11] = applied(after[7], quads[2])
    after[15] = applied(after[7], eighths[1])
    for i in range(4):
        after[4 * i + 1] = applied(after[4 * i - 1], pairs[2 * i])
    for i in range(8):
        after[2 * i] = applied(after[2 * i - 1], leaves[2 * i])
    hours = leaves.shape[0]
    decays = jnp.exp(-factor_rate[...])
    rate = smooth_rate[...]
    retain = jnp.exp(-rate)
    own = 1.0 - retain * decays
    following = jnp.zeros((1, k), F32)
    for h in reversed(range(hours)):
        following = own * after[h][:1] + retain * following
        partial[h : h + 1] = following
    boundary = jnp.where(at_end == 1, decays * after[hours - 1][:1], 0.0)
    last[...] = boundary
    sent[...] = following + jnp.exp(-hours * rate) * boundary


def histogram_kernel(
    place, partial, last, later, smooth_rate, readings, present, loadings, noise, regions, scale, smoothed, out
):
    hours, k = partial.shape
    count = later.shape[0]
    own = place[3]
    rate = smooth_rate[...]
    row, _ = iotas(count, k)
    steps = row - own - 1
    weight = jnp.exp(-(jnp.maximum(steps, 0) * hours).astype(F32) * rate)
    trailing = jnp.sum(jnp.where(steps >= 0, weight * later[...], 0.0), axis=0, keepdims=True)
    trailing = trailing + last[...]
    hour, _ = iotas(hours, k)
    powers = jnp.exp(-(hours - hour).astype(F32) * rate)
    smooth = partial[...] + powers * trailing
    smoothed[...] = smooth
    fitted = across(smooth.astype(BF16), loadings[...])
    standard = (readings[...].astype(F32) - fitted) * jnp.sqrt(noise[...])
    probab = 0.5 * (1.0 + lax.erf(standard * 0.7071067811865476))
    seen = present[...].astype(F32)
    rows = []
    for b in range(BINS):
        kernel = jnp.maximum(0.0, 1.0 - BINS * jnp.abs(probab - (b + 0.5) / BINS))
        rows.append(jnp.sum(seen * kernel, axis=0, keepdims=True))
    rows.append(jnp.zeros((4, probab.shape[1]), F32))
    table = jnp.concatenate(rows, axis=0)
    slot, _ = iotas(128, probab.shape[1])
    member = (lax.rem(slot, GROUPS) == regions[...]).astype(F32).astype(BF16)
    high, low = halves(table)
    lowest = (table - high.astype(F32) - low.astype(F32)).astype(BF16)
    wide = across(high, member) + (across(low, member) + across(lowest, member))
    brow, blane = iotas(24, 128)
    kept = jnp.where(lax.div(blane, GROUPS) == lax.rem(brow, 8), wide, 0.0) * scale[0]
    out[...] = jnp.concatenate(
        [jnp.sum(kept[8 * r : 8 * r + 8], axis=0, keepdims=True) for r in range(3)], axis=0
    )


def sent_to_all(shard, axis):
    count = lax.axis_size(axis)
    return lax.all_to_all(
        jnp.broadcast_to(shard[None], (count, *shard.shape)), axis, 0, 0, tiled=True
    )


def shape_of(*sizes):
    return jax.ShapeDtypeStruct(sizes, F32)


def body(
    readings, present, loadings, noise_precision, update_gain, factor_rate, smooth_rate, regions
):
    hours, series = readings.shape
    k = loadings.shape[1]
    noise = noise_precision.reshape(1, series)
    gain, factor, smooth = (a.reshape(1, k) for a in (update_gain, factor_rate, smooth_rate))
    z, x = lax.axis_index("z"), lax.axis_index("x")
    nz, nx = lax.axis_size("z"), lax.axis_size("x")
    own = z * nx + x
    place = jnp.stack([z, x, (own == nz * nx - 1).astype(jnp.int32), own]).astype(jnp.int32)

    packed = pl.pallas_call(
        information_kernel,
        out_shape=shape_of(hours, k // 2 + 8, k),
        in_specs=[VM] * 4,
        out_specs=VM,
        compiler_params=PARAMS,
        name="information",
    )(readings, present, loadings, noise)

    height = k // 2 + 8
    cores, ny = lax.axis_size("c"), lax.axis_size("y")
    packed = packed.reshape(cores, hours // cores, height, k)
    packed = lax.all_to_all(packed, "c", 0, 0, tiled=True).sum(axis=0)
    packed = lax.all_to_all(packed, "y", 0, 0, tiled=True).sum(axis=0)
    packed = sent_to_all(packed, "y")
    packed = lax.all_gather(packed, "c").reshape(hours, height, k)

    tall = k + 8
    leaves, pairs, quads, eighths, total = pl.pallas_call(
        block_kernel,
        out_shape=[
            shape_of(hours, tall, k),
            shape_of(hours // 2, tall, k),
            shape_of(hours // 4, tall, k),
            shape_of(hours // 8, tall, k),
            shape_of(tall, k),
        ],
        in_specs=[VM] * 3,
        out_specs=[VM] * 5,
        compiler_params=PARAMS,
        name="block",
    )(packed, gain, factor)

    blocks = lax.all_gather(total, "x")
    plane = pl.pallas_call(
        four_kernel,
        out_shape=shape_of(tall, k),
        in_specs=[VM],
        out_specs=VM,
        compiler_params=PARAMS,
        name="four",
    )(blocks)
    planes = sent_to_all(plane, "z")

    partial, sent, last = pl.pallas_call(
        filter_kernel,
        out_shape=[shape_of(hours, k), shape_of(1, k), shape_of(1, k)],
        in_specs=[SM] + [VM] * 8,
        out_specs=[VM] * 3,
        compiler_params=PARAMS,
        name="filter",
    )(place, planes, blocks, leaves, pairs, quads, eighths, factor, smooth)

    later = sent_to_all(sent, TM).reshape(nz * nx, k)
    hours_all = hours * nz * nx
    series_all = series * ny * cores
    scale = jnp.full((1,), BINS * GROUPS / (hours_all * series_all), F32)
    smoothed, local = pl.pallas_call(
        histogram_kernel,
        out_shape=[shape_of(hours, k), shape_of(3, 128)],
        in_specs=[SM] + [VM] * 9 + [SM],
        out_specs=[VM] * 2,
        compiler_params=PARAMS,
        name="histogram",
    )(place, partial, last, later, smooth, readings, present, loadings, noise, regions.reshape(1, series), scale)

    local = lax.all_gather(local, "c").sum(axis=0)
    local = sent_to_all(local, ("x", "y")).sum(axis=0)
    local = sent_to_all(local, "z").sum(axis=0)
    histogram = local.reshape(24, GROUPS)[:BINS].T
    return (smoothed, histogram)


def solution(mesh):
    split = Mesh(mesh.devices.reshape(8, 4, 8, 2), ("z", "x", "y", "c"))
    in_specs = (P(TM, SERIES), P(TM, SERIES), P(SERIES, None), P(SERIES), P(), P(), P(), P(SERIES))
    out_specs = (P(TM, None), P())
    return jax.shard_map(body, mesh=split, in_specs=in_specs, out_specs=out_specs, check_vma=False)
```

time: 258 us -> 131 us (0.51)
  matrix products: 58.9 us -> 0 us
  loops' own time: 33 us -> 0 us
  local copies, waits for them, and re-layouts: 19.4 us -> 4.93 us
  waiting for transfers between devices: 26.4 us -> 15.2 us
  blocking collectives: 103 us -> 92.1 us
  Pallas kernels: 0 us -> 7.87 us
  other arithmetic: 4.53 us -> 0.2 us
    dot_general x101 -> x0, matrix products: 58.9 us -> none  [the longest x16 23.2 us: per_hour(): lax.dot_general(scaled, loadings, (((0,), (0,)), ((), ())), preferred_ele...]
    another operation x4 -> x0, loops' own time: 33 us -> none  [the longest x1 31.6 us: local_information(): return lax.map(per_hour, jnp.arange(readings.shape[0]))]
    all_gather x2 -> x3, blocking collectives: 33.9 us -> 20.3 us  [the longest x1 9.4 us: body(): blocks = lax.all_gather(total, 'x')]
    all_to_all x2 -> x1, waiting for transfers between devices: 26.4 us -> 15.2 us  [sent_to_all(): lax.all_to_all(jnp.broadcast_to(shard[None], (count, *shard.shape)), axis...]
    dynamic_slice x32 -> x0, local copies, waits for them, and re-layouts: 9.57 us -> none  [the longest x16 9.38 us: local_information(): return lax.map(per_hour, jnp.arange(readings.shape[0]))]
    all_to_all x3 -> x4, blocking collectives: 37.9 us -> 46 us  [sent_to_all(): lax.all_to_all(jnp.broadcast_to(shard[None], (count, *shard.shape)), axis...]
    pallas_call x0 -> x5, Pallas kernels: none -> 7.87 us  [the longest x1 2.56 us: body(): pl.pallas_call(filter_kernel, out_shape=[shape_of(hours, k), shape_of(1,...]
    all_to_all x2, blocking collectives: 31.5 us -> 25.8 us  [the longest x1 15 us: body(): packed = lax.all_to_all(packed, 'y', 0, 0, tiled=True).sum(axis=0)]
  transfers between devices with their start and end apart: 2 -> 1, of which waited for: 2 -> 1; matrix products, arithmetic and copies ran while one was open for 0% -> 0% of each run, Pallas kernels for 0% -> 0%
where the time goes in v1:
time: 131 us; the launch traced here: 130 us
  blocking collectives  92.1 us (70%)
  waiting for transfers between devices  15.2 us (12%)
  starting transfers between devices  9.34 us (7%)
  Pallas kernels  7.87 us (6%)
  local copies, waits for them, and re-layouts  4.93 us (4%)
    all_to_all x4, blocking collectives, sent_to_all(): lax.all_to_all(jnp.broadcast_to(shard[None], (count, *shard.shape)), axis...  46 us
    all_to_all x1, waiting for transfers between devices, sent_to_all(): lax.all_to_all(jnp.broadcast_to(shard[None], (count, *shard.shape)), axis...  15.2 us
    all_to_all x1, blocking collectives, body(): packed = lax.all_to_all(packed, 'y', 0, 0, tiled=True).sum(axis=0)  15 us
    all_to_all x1, blocking collectives, body(): packed = lax.all_to_all(packed, 'c', 0, 0, tiled=True).sum(axis=0)  10.7 us
    all_gather x1, blocking collectives, body(): blocks = lax.all_gather(total, 'x')  9.4 us
    all_to_all x1, starting transfers between devices, sent_to_all(): lax.all_to_all(jnp.broadcast_to(shard[None], (count, *shard.shape)), axis...  9.34 us
    all_gather x1, blocking collectives, body(): local = lax.all_gather(local, 'c').sum(axis=0)  6.6 us
    all_gather x1, blocking collectives, body(): packed = lax.all_gather(packed, 'c').reshape(hours, height, k)  4.33 us
  transfers between devices with their start and end apart: 1, of which 1 were waited for; matrix products, arithmetic and copies ran while one was open for 0% of the time, Pallas kernels for 0%

profile of v1, /device:TPU:1, one launch (start us, length us, event | category | flops | bytes accessed | tf_op | source)
XLA Modules:
  0.0 130.4 jit_solution(2814285386457306523)
XLA Ops:
  0.6 0.0 copy-start
  0.6 0.9 copy-done
  1.6 0.0 copy-start.2
  1.6 0.8 copy-done.2
  2.4 0.0 copy-start.4
  2.4 0.8 copy-done.4
  3.2 0.0 copy-start.6
  3.2 0.7 copy-done.6
  3.9 1.4 %information.1 = f32[16,72,128]{2,1,0:T(8,128)S(1)} custom-call(bf16[16,1024]{1,0:T(8,128)(2,1)S(1)} %copy-done.4, s32[16,1024]{1,0:T(8,128)S(1)} %copy-done.2, bf16[1024,128]{1,0:T(8,128)(2,1)S(1)} %copy-done, f32[1,1024]{1,0:T(1,128)S(1)} %bitcast.20), custom_call_target="tpu_custom_call" | custom-call | tf_op jit(solution)/shard_map/information/pallas_call | solution.py:204
  5.3 10.7 %all_to_all.35 = f32[2,8,72,128]{3,2,1,0:T(8,128)S(1)} all-to-all(f32[2,8,72,128]{3,2,1,0:T(8,128)S(1)} %bitcast.18), channel_id=1, replica_groups=mesh['z'=8,'x'=4,'y'=8,'c'=2] {'c'}, dimensions={0} | all-to-all | bytes 1179648 | tf_op jit(solution)/shard_map/all_to_all | solution.py:216
  16.1 15.0 %all_to_all.36 = f32[8,72,128]{2,1,0:T(8,128)S(1)} all-to-all(f32[8,72,128]{2,1,0:T(8,128)S(1)} %reduce_sum.45), channel_id=1, replica_groups=mesh['z'=8,'x'=4,'y'=8,'c'=2] {'y'}, dimensions={0} | all-to-all | bytes 589824 | tf_op jit(solution)/shard_map/all_to_all | solution.py:217
  31.1 0.0 copy-start.9
  31.1 0.0 copy-start.11
  31.2 13.4 %all_to_all.37 = f32[8,72,128]{2,1,0:T(8,128)S(1)} all-to-all(f32[8,72,128]{2,1,0:T(8,128)S(1)} %broadcast_in_dim.12), channel_id=1, replica_groups=mesh['z'=8,'x'=4,'y'=8,'c'=2] {'y'}, dimensions={0} | all-to-all | bytes 589824 | tf_op jit(solution)/shard_map/all_to_all | solution.py:183
  44.6 4.3 %all-gather.packed = f32[16,72,128]{2,1,0:T(8,128)S(1)} all-gather(f32[8,72,128]{2,1,0:T(8,128)S(1)} %all_to_all.37), channel_id=2, replica_groups=mesh['z'=8,'x'=4,'y'=8,'c'=2] {'c'}, dimensions={0}, use_global_device_ids=true | all-gather | bytes 884736 | tf_op jit(solution)/shard_map/all_gather | solution.py:219
  48.9 0.0 copy-done.9
  48.9 0.0 copy-done.11
  48.9 1.6 %block.1 = (f32[16,136,128]{2,1,0:T(8,128)S(1)}, f32[8,136,128]{2,1,0:T(8,128)S(1)}, f32[4,136,128]{2,1,0:T(8,128)S(1)}, f32[2,136,128]{2,1,0:T(8,128)S(1)}, f32[136,128]{1,0:T(8,128)S(1)}) custom-call(f32[16,72,128]{2,1,0:T(8,128)S(1)} %all-gather.packed, f32[1,128]{1,0:T(1,128)S(1)} %bitcast.28, f32[1,128]{1,0:T(1,128)S(1)} %bitcast.23), custom_call_target="tpu_custom_call" | custom-call | tf_op jit(solution)/shard_map/block/pallas_call | solution.py:222
  50.5 9.4 %all-gather.1 = f32[544,128]{1,0:T(8,128)S(1)} all-gather(f32[136,128]{1,0:T(8,128)S(1)} %get-tuple-element.12), channel_id=3, replica_groups=mesh['z'=8,'x'=4,'y'=8,'c'=2] {'x'}, dimensions={0}, use_global_device_ids=true | all-gather | bytes 348160 | tf_op jit(solution)/shard_map/all_gather | solution.py:237
  59.9 0.0 copy-start.10
  59.9 0.5 four.1
  60.5 0.8 broadcast_in_dim.13
  61.3 9.3 %all-to-all-start.3 = ((f32[8,136,128]{2,1,0:T(8,128)}), f32[8,136,128]{2,1,0:T(8,128)S(1)}, u32[]{:S(2)}, u32[]{:S(2)}) async-start(f32[8,136,128]{2,1,0:T(8,128)} %broadcast_in_dim.13), calls=%async_computation.3 | async-start | bytes 1114112 | tf_op jit(solution)/shard_map/all_to_all | solution.py:183
  70.7 0.1 pad_add_fusion.place
  70.7 15.2 %all-to-all-done.3.planes = f32[8,136,128]{2,1,0:T(8,128)S(1)} async-done(((f32[8,136,128]{2,1,0:T(8,128)}), f32[8,136,128]{2,1,0:T(8,128)S(1)}, u32[]{:S(2)}, u32[]{:S(2)}) %all-to-all-start.3) | async-done | bytes 557088 | tf_op jit(solution)/shard_map/all_to_all | solution.py:183
  85.9 0.0 copy-done.10
  85.9 0.0 copy-start.1
  85.9 0.0 copy-start.3
  85.9 0.0 copy-start.5
  86.0 0.0 copy-start.7
  86.0 0.0 copy-start.8
  86.0 2.6 %filter.1 = (f32[16,128]{1,0:T(8,128)S(1)}, f32[1,128]{1,0:T(1,128)S(1)}, f32[1,128]{1,0:T(1,128)S(1)}) custom-call(s32[4]{0:T(128)S(1)} %pad_add_fusion.place, f32[8,136,128]{2,1,0:T(8,128)S(1)} %all-to-all-done.3.planes, f32[4,136,128]{2,1,0:T(8,128)S(1)} %bitcast.17, f32[16,136,128]{2,1,0:T(8,128)S(1)} %get-tuple-element.13.leaves, ...), custom_call_target="tpu_custom_call" | custom-call | tf_op jit(solution)/shard_map/filter/pallas_call | solution.py:248
  88.6 11.8 %all_to_all.38 = f32[32,1,128]{2,1,0:T(1,128)S(1)} all-to-all(f32[32,1,128]{2,1,0:T(1,128)S(1)} %broadcast_in_dim.15), channel_id=1, replica_groups=mesh['z'=8,'x'=4,'y'=8,'c'=2] {'z','x'}, dimensions={0} | all-to-all | bytes 32768 | tf_op jit(solution)/shard_map/all_to_all | solution.py:183
  100.4 0.0 copy-done.1
  100.4 0.0 copy-done.3
  100.4 0.0 copy-done.5
  100.4 0.0 copy-done.7
  100.4 0.0 copy-done.8
  100.4 1.7 %histogram.1 = (f32[16,128]{1,0:T(8,128)}, f32[3,128]{1,0:T(4,128)S(1)}) custom-call(s32[4]{0:T(128)S(1)} %pad_add_fusion.place, f32[16,128]{1,0:T(8,128)S(1)} %get-tuple-element.17.partial, f32[1,128]{1,0:T(1,128)S(1)} %get-tuple-element.18.last, f32[32,128]{1,0:T(8,128)S(1)} %bitcast.19, f32[1,128]{1,0:T(1,128)S(1)} %bitcast.26, ...), custom_call_target="tpu_custom_call" | custom-call | tf_op jit(solution)/shard_map/histogram/pallas_call | solution.py:261
  102.1 6.6 %all-gather.3 = f32[2,3,128]{2,1,0:T(4,128)S(1)} all-gather(f32[1,3,128]{2,1,0:T(4,128)S(1)} %bitcast.27), channel_id=4, replica_groups=mesh['z'=8,'x'=4,'y'=8,'c'=2] {'c'}, dimensions={0}, use_global_device_ids=true | all-gather | bytes 4608 | tf_op jit(solution)/shard_map/all_gather | solution.py:270
  108.7 11.8 %all_to_all.39 = f32[32,3,128]{2,1,0:T(4,128)S(1)} all-to-all(f32[32,3,128]{2,1,0:T(4,128)S(1)} %broadcast_in_dim.16), channel_id=1, replica_groups=mesh['z'=8,'x'=4,'y'=8,'c'=2] {'x','y'}, dimensions={0} | all-to-all | bytes 98304 | tf_op jit(solution)/shard_map/all_to_all | solution.py:183
  120.6 9.0 %all_to_all.40 = f32[8,3,128]{2,1,0:T(4,128)S(1)} all-to-all(f32[8,3,128]{2,1,0:T(4,128)S(1)} %broadcast_in_dim.17), channel_id=1, replica_groups=mesh['z'=8,'x'=4,'y'=8,'c'=2] {'z'}, dimensions={0} | all-to-all | bytes 24576 | tf_op jit(solution)/shard_map/all_to_all | solution.py:183
  129.6 0.1 reshape.46
  129.7 0.7 copy.15
  (10 shorter events, 0.2 us)
Async XLA Ops:
  0.6 1.0 copy-start
  1.6 0.8 copy-start.2
  2.4 0.8 copy-start.4
  3.2 0.7 copy-start.6
  31.1 17.8 %copy-start.9 = (f32[128]{0:T(128)S(1)}, f32[128]{0:T(128)}, u32[]{:S(2)}) copy-start(f32[128]{0:T(128)} %param.13) | copy-start | bytes 1540
  31.1 17.8 %copy-start.11 = (f32[128]{0:T(128)S(1)}, f32[128]{0:T(128)}, u32[]{:S(2)}) copy-start(f32[128]{0:T(128)} %param.12) | copy-start | bytes 1540
  59.9 26.0 %copy-start.10 = (f32[128]{0:T(128)S(1)}, f32[128]{0:T(128)}, u32[]{:S(2)}) copy-start(f32[128]{0:T(128)} %param.14) | copy-start | bytes 1540
  61.3 24.6 %all-to-all-start.3 = ((f32[8,136,128]{2,1,0:T(8,128)}), f32[8,136,128]{2,1,0:T(8,128)S(1)}, u32[]{:S(2)}, u32[]{:S(2)}) async-start(f32[8,136,128]{2,1,0:T(8,128)} %broadcast_in_dim.13), calls=%async_computation.3 | async-start | bytes 1114112 | tf_op jit(solution)/shard_map/all_to_all | solution.py:183
  85.9 14.4 %copy-start.1 = (bf16[1024,128]{1,0:T(8,128)(2,1)S(1)}, bf16[1024,128]{1,0:T(8,128)(2,1)}, u32[]{:S(2)}) copy-start(bf16[1024,128]{1,0:T(8,128)(2,1)} %loadings.3) | copy-start | bytes 786436
  85.9 14.4 %copy-start.3 = (s32[16,1024]{1,0:T(8,128)S(1)}, s32[16,1024]{1,0:T(8,128)}, u32[]{:S(2)}) copy-start(s32[16,1024]{1,0:T(8,128)} %present.3) | copy-start | bytes 196612
  85.9 14.4 %copy-start.5 = (bf16[16,1024]{1,0:T(8,128)(2,1)S(1)}, bf16[16,1024]{1,0:T(8,128)(2,1)}, u32[]{:S(2)}) copy-start(bf16[16,1024]{1,0:T(8,128)(2,1)} %readings.3) | copy-start | bytes 98308
  86.0 14.4 %copy-start.7 = (f32[1024]{0:T(1024)S(1)}, f32[1024]{0:T(1024)}, u32[]{:S(2)}) copy-start(f32[1024]{0:T(1024)} %param.11) | copy-start | bytes 12292
  86.0 14.4 %copy-start.8 = (s32[1024]{0:T(1024)S(1)}, s32[1024]{0:T(1024)}, u32[]{:S(2)}) copy-start(s32[1024]{0:T(1024)} %param.15) | copy-start | bytes 12292

commit v2 on v1

v2 whole, which is shorter than its diff:
```python
import jax
import jax.numpy as jnp
from jax import lax
from jax.experimental import pallas as pl
from jax.experimental.pallas import tpu as pltpu
from jax.sharding import Mesh
from jax.sharding import PartitionSpec as P

BINS = 20
GROUPS = 16
SERIES = ("y", "c")
TM = ("z", "x")
F32 = jnp.float32
BF16 = jnp.bfloat16
VM = pl.BlockSpec(memory_space=pltpu.VMEM)
SM = pl.BlockSpec(memory_space=pltpu.SMEM)
HB = pl.BlockSpec(memory_space=pltpu.HBM)
PARAMS = pltpu.CompilerParams(vmem_limit_bytes=40 * 1024 * 1024)


def iotas(rows, lanes):
    shape = (rows, lanes)
    return lax.broadcasted_iota(jnp.int32, shape, 0), lax.broadcasted_iota(jnp.int32, shape, 1)


def halves(a):
    high = a.astype(BF16)
    return high, (a - high.astype(F32)).astype(BF16)


def bdot(a, b):
    return jnp.dot(a, b, preferred_element_type=F32)


def dot3(a, b):
    ah, al = halves(a)
    bh, bl = halves(b)
    return bdot(ah, bh) + (bdot(ah, bl) + bdot(al, bh))


def across(a, b):
    return lax.dot_general(a, b, (((1,), (1,)), ((), ())), preferred_element_type=F32)


def joined(earlier, later, fade):
    k = fade.shape[1]
    wide = jnp.concatenate([later[0][:k], later[1][:k]], axis=1)
    product = dot3(earlier[0], wide)
    maps = jnp.concatenate([product[:k, :k], product[k:, :k] + later[0][k:]], axis=0)
    gives = jnp.concatenate([product[:k, k:], product[k:, k:] + later[1][k:]], axis=0)
    return maps, earlier[1] + fade * gives


def information_kernel(
    place, readings_hbm, present_hbm, loadings_hbm, noise_hbm, kept, sent,
    readings, present, loadings, noise, seen, scores, sems,
):
    pairs = (
        (loadings_hbm, loadings),
        (noise_hbm, noise),
        (present_hbm, present),
        (readings_hbm, readings),
    )
    copies = [pltpu.make_async_copy(a, b, sems.at[i]) for i, (a, b) in enumerate(pairs)]
    for copy in copies:
        copy.start()
    for copy in copies:
        copy.wait()
    count = kept.shape[0]
    core = place[2]
    load = loadings[...]
    k = load.shape[1]
    half = k // 2
    scaled = (jnp.transpose(load.astype(F32)) * noise[...]).astype(BF16)
    seen[...] = present[...].astype(F32)
    scores[...] = across(readings[...] * seen[...].astype(BF16), scaled)
    row, lane = iotas(half, k)
    row_k, lane_k = iotas(k, k)
    for slot, out in enumerate((kept, sent)):
        first = (core if slot == 0 else 1 - core) * count
        for i in range(count):
            observed = seen[pl.ds(first + i, 1), :].astype(BF16)
            inform = bdot(scaled * observed, load)
            folded = pltpu.roll(inform[half:], half, 1)
            out[i, :half] = jnp.where(lane >= row, inform[:half], folded)
            diagonal = jnp.sum(jnp.where(row_k == lane_k, inform, 0.0), axis=0, keepdims=True)
            out[i, half:] = jnp.concatenate(
                [diagonal, scores[pl.ds(first + i, 1), :], jnp.zeros((6, k), F32)], axis=0
            )


def block_kernel(
    place, packed, gain, factor_rate, smooth_rate, leaves, pairs, quads, eighths, half_total,
    given1, given2, given4, given8,
):
    hours = packed.shape[0]
    k = packed.shape[2]
    half = k // 2
    gain_row = gain[...]
    decay_row = jnp.exp(-factor_rate[...])
    decay_col = jnp.transpose(jnp.broadcast_to(decay_row, (k, k)))
    rate = smooth_rate[...]
    weight = 1.0 - jnp.exp(-rate) * decay_row
    row, lane = iotas(half, k)
    row_k, lane_k = iotas(k, k)
    on_diag = row_k == lane_k
    identity = on_diag.astype(F32)
    for h in range(hours):
        page = packed[h]
        top = page[:half]
        upper = jnp.where(lane >= row, top, 0.0)
        lower = pltpu.roll(jnp.where(lane < row, top, 0.0), half, 1)
        part = jnp.concatenate([upper, lower], axis=0)
        inform = jnp.where(on_diag, page[half : half + 1], part + jnp.transpose(part))
        matrix = (identity - inform * gain_row) * decay_col
        shift = gain_row * page[half + 1 : half + 2]
        one = jnp.concatenate([matrix, shift, jnp.zeros((7, k), F32)], axis=0)
        leaves[h] = one
        given1[h] = one * weight
    below, given = leaves, given1
    for span, above, gives in ((1, pairs, given2), (2, quads, given4), (4, eighths, given8)):
        fade = jnp.exp(-span * rate)
        for i in range(hours // (2 * span)):
            above[i], gives[i] = joined(
                (below[2 * i], given[2 * i]), (below[2 * i + 1], given[2 * i + 1]), fade
            )
        below, given = above, gives
    total = joined((below[0], given[0]), (below[1], given[1]), jnp.exp(-8.0 * rate))
    half_total[...] = jnp.where(place[2] == 0, total[0], total[1])


def four_kernel(place, blocks, smooth_rate, half_total):
    rate = smooth_rate[...]
    short, long = jnp.exp(-16.0 * rate), jnp.exp(-32.0 * rate)
    one = joined((blocks[0, 0], blocks[1, 0]), (blocks[0, 1], blocks[1, 1]), short)
    two = joined((blocks[0, 2], blocks[1, 2]), (blocks[0, 3], blocks[1, 3]), short)
    total = joined(one, two, long)
    half_total[...] = jnp.where(place[2] == 0, total[0], total[1])


def applied(current, one):
    k = one.shape[1]
    return dot3(current, one[:k]) + one[k : k + 1]


def walked(nodes, start, own):
    k = nodes.shape[3]
    current = found = start
    gives = []
    for i in range(nodes.shape[1]):
        found = jnp.where(i == own, current, found)
        wide = jnp.concatenate([nodes[0, i, :k], nodes[1, i, :k]], axis=1)
        product = dot3(current, wide)
        gives.append(product[:1, k:] + nodes[1, i, k : k + 1])
        current = product[:, :k] + nodes[0, i, k : k + 1]
    return found, current, gives


def followed(gives, after, own, fade):
    found = following = after
    for i in reversed(range(len(gives))):
        found = jnp.where(i == own, following, found)
        following = gives[i] + fade * following
    return found


def final_kernel(
    place, planes, blocks, leaves, pairs, quads, eighths, factor_rate, smooth_rate,
    readings, present, loadings, noise, regions, scale, smoothed, out,
):
    hours, _, k = leaves.shape
    z, x = place[0], place[1]
    decays = jnp.exp(-factor_rate[...])
    rate = smooth_rate[...]
    retain = jnp.exp(-rate)
    start, final, plane_gives = walked(planes, jnp.zeros((8, k), F32), z)
    span = hours * blocks.shape[1]
    behind_plane = followed(plane_gives, decays * final[:1], z, jnp.exp(-span * rate))
    start, _, block_gives = walked(blocks, start, x)
    following = followed(block_gives, behind_plane, x, jnp.exp(-hours * rate))
    after = {-1: start}
    after[7] = applied(start, eighths[0])
    after[3] = applied(start, quads[0])
    after[11] = applied(after[7], quads[2])
    after[15] = applied(after[7], eighths[1])
    for i in range(4):
        after[4 * i + 1] = applied(after[4 * i - 1], pairs[2 * i])
    for i in range(8):
        after[2 * i] = applied(after[2 * i - 1], leaves[2 * i])
    weight = 1.0 - retain * decays
    for h in reversed(range(hours)):
        following = weight * after[h][:1] + retain * following
        smoothed[h : h + 1] = following
    fitted = across(smoothed[...].astype(BF16), loadings[...])
    standard = (readings[...].astype(F32) - fitted) * jnp.sqrt(noise[...])
    probab = 0.5 * (1.0 + lax.erf(standard * 0.7071067811865476))
    seen = present[...].astype(F32)
    rows = []
    for b in range(BINS):
        kernel = jnp.maximum(0.0, 1.0 - BINS * jnp.abs(probab - (b + 0.5) / BINS))
        rows.append(jnp.sum(seen * kernel, axis=0, keepdims=True))
    rows.append(jnp.zeros((4, probab.shape[1]), F32))
    table = jnp.concatenate(rows, axis=0)
    slot, _ = iotas(128, probab.shape[1])
    member = (lax.rem(slot, GROUPS) == regions[...]).astype(F32).astype(BF16)
    high, low = halves(table)
    lowest = (table - high.astype(F32) - low.astype(F32)).astype(BF16)
    wide = across(high, member) + (across(low, member) + across(lowest, member))
    brow, blane = iotas(24, 128)
    kept = jnp.where(lax.div(blane, GROUPS) == lax.rem(brow, 8), wide, 0.0) * scale[0]
    out[...] = jnp.concatenate(
        [jnp.sum(kept[8 * r : 8 * r + 8], axis=0, keepdims=True) for r in range(3)], axis=0
    )


def sent_to_all(shard, axis):
    count = lax.axis_size(axis)
    return lax.all_to_all(
        jnp.broadcast_to(shard[None], (count, *shard.shape)), axis, 0, 0, tiled=True
    )


def shape_of(*sizes):
    return jax.ShapeDtypeStruct(sizes, F32)


def body(
    readings, present, loadings, noise_precision, update_gain, factor_rate, smooth_rate, regions
):
    hours, series = readings.shape
    k = loadings.shape[1]
    height, tall = k // 2 + 8, k + 8
    noise = noise_precision.reshape(1, series)
    gain, factor, smooth = (a.reshape(1, k) for a in (update_gain, factor_rate, smooth_rate))
    z, x, core = (lax.axis_index(a) for a in ("z", "x", "c"))
    nz, nx, ny, cores = (lax.axis_size(a) for a in ("z", "x", "y", "c"))
    place = jnp.stack([z, x, core]).astype(jnp.int32)
    share = hours // cores

    kept, sent = pl.pallas_call(
        information_kernel,
        out_shape=[shape_of(share, height, k)] * 2,
        in_specs=[SM] + [HB] * 4,
        out_specs=[VM] * 2,
        scratch_shapes=[
            pltpu.VMEM((hours, series), BF16),
            pltpu.VMEM((hours, series), jnp.int32),
            pltpu.VMEM((series, k), BF16),
            pltpu.VMEM((1, series), F32),
            pltpu.VMEM((hours, series), F32),
            pltpu.VMEM((hours, k), F32),
            pltpu.SemaphoreType.DMA((4,)),
        ],
        compiler_params=PARAMS,
        name="information",
    )(place, readings, present, loadings, noise)
    arrived = lax.dynamic_index_in_dim(lax.all_gather(sent, "c"), 1 - core, 0, keepdims=False)
    packed = lax.all_to_all(kept + arrived, "y", 0, 0, tiled=True).sum(axis=0)
    packed = sent_to_all(packed, "y")
    packed = lax.all_gather(packed, "c").reshape(hours, height, k)

    nodes = [shape_of(hours // n, tall, k) for n in (1, 2, 4, 8)]
    leaves, pairs, quads, eighths, half_total = pl.pallas_call(
        block_kernel,
        out_shape=nodes + [shape_of(tall, k)],
        in_specs=[SM] + [VM] * 4,
        out_specs=[VM] * 5,
        scratch_shapes=[pltpu.VMEM((hours // n, tall, k), F32) for n in (1, 2, 4, 8)],
        compiler_params=PARAMS,
        name="block",
    )(place, packed, gain, factor, smooth)
    blocks = lax.all_gather(sent_to_all(half_total, "x"), "c")

    half_total = pl.pallas_call(
        four_kernel,
        out_shape=shape_of(tall, k),
        in_specs=[SM] + [VM] * 2,
        out_specs=VM,
        compiler_params=PARAMS,
        name="four",
    )(place, blocks, smooth)
    planes = lax.all_gather(sent_to_all(half_total, "z"), "c")

    hours_all = hours * nz * nx
    series_all = series * ny * cores
    scale = jnp.full((1,), BINS * GROUPS / (hours_all * series_all), F32)
    smoothed, local = pl.pallas_call(
        final_kernel,
        out_shape=[shape_of(hours, k), shape_of(3, 128)],
        in_specs=[SM] + [VM] * 13 + [SM],
        out_specs=[VM] * 2,
        compiler_params=PARAMS,
        name="final",
    )(
        place, planes, blocks, leaves, pairs, quads, eighths, factor, smooth,
        readings, present, loadings, noise, regions.reshape(1, series), scale,
    )

    local = sent_to_all(local, SERIES).sum(axis=0)
    local = sent_to_all(local, TM).sum(axis=0)
    histogram = local.reshape(24, GROUPS)[:BINS].T
    return (smoothed, histogram)


def solution(mesh):
    split = Mesh(mesh.devices.reshape(8, 4, 8, 2), ("z", "x", "y", "c"))
    in_specs = (P(TM, SERIES), P(TM, SERIES), P(SERIES, None), P(SERIES), P(), P(), P(), P(SERIES))
    out_specs = (P(TM, None), P())
    return jax.shard_map(body, mesh=split, in_specs=in_specs, out_specs=out_specs, check_vma=False)
```

time: 131 us -> 151 us (1.15)
  blocking collectives: 92.1 us -> 113 us
  between operations: 0.75 us -> 14.2 us
  starting transfers between devices: 9.34 us -> 0.04 us
  waiting for transfers between devices: 15.2 us -> 8.71 us
    all_to_all x4 -> x5, blocking collectives: 46 us -> 81.5 us  [sent_to_all(): lax.all_to_all(jnp.broadcast_to(shard[None], (count, *shard.shape)), axis...]
    all_to_all x1 -> x0, waiting for transfers between devices: 15.2 us -> none  [sent_to_all(): lax.all_to_all(jnp.broadcast_to(shard[None], (count, *shard.shape)), axis...]
    all_to_all x2 -> x1, blocking collectives: 25.8 us -> 15 us  [body(): packed = lax.all_to_all(kept + arrived, 'y', 0, 0, tiled=True).sum(axis=0)]
    all_to_all x1 -> x0, starting transfers between devices: 9.34 us -> none  [sent_to_all(): lax.all_to_all(jnp.broadcast_to(shard[None], (count, *shard.shape)), axis...]
    all_gather x0 -> x1, waiting for transfers between devices: none -> 8.7 us  [body(): planes = lax.all_gather(sent_to_all(half_total, 'z'), 'c')]
    all_gather x2, blocking collectives: 16 us -> 11.9 us  [the longest x1 8.73 us: body(): lax.all_gather(sent, 'c')]
    pallas_call x5 -> x4, Pallas kernels: 7.87 us -> 9.21 us  [the longest x1 3.75 us: body(): pl.pallas_call(final_kernel, out_shape=[shape_of(hours, k), shape_of(3, 1...]
    unnamed x25 -> x27, local copies, waits for them, and re-layouts: 3.95 us -> 5.2 us
where the time goes in v2:
time: 151 us
  blocking collectives  113 us (75%)
  between operations  14.2 us (9%)
  Pallas kernels  9.21 us (6%)
  waiting for transfers between devices  8.71 us (6%)
  local copies, waits for them, and re-layouts  5.38 us (4%)
    all_to_all x5, blocking collectives, sent_to_all(): lax.all_to_all(jnp.broadcast_to(shard[None], (count, *shard.shape)), axis...  81.5 us
    all_to_all x1, blocking collectives, body(): packed = lax.all_to_all(kept + arrived, 'y', 0, 0, tiled=True).sum(axis=0)  15 us
    all_gather x1, blocking collectives, body(): lax.all_gather(sent, 'c')  8.73 us
    all_gather x1, waiting for transfers between devices, body(): planes = lax.all_gather(sent_to_all(half_total, 'z'), 'c')  8.7 us
    unnamed x27, local copies, waits for them, and re-layouts  5.2 us
    all_gather x1, blocking collectives, body(): packed = lax.all_gather(packed, 'c').reshape(hours, height, k)  4.33 us
    pallas_call x1, Pallas kernels, body(): pl.pallas_call(final_kernel, out_shape=[shape_of(hours, k), shape_of(3, 1...  3.75 us
    all_gather x1, blocking collectives, body(): blocks = lax.all_gather(sent_to_all(half_total, 'x'), 'c')  3.18 us
  transfers between devices with their start and end apart: 1, of which 1 were waited for; matrix products, arithmetic and copies ran while one was open for 0% of the time, Pallas kernels for 0%

profile of v2, /device:TPU:1, one launch (start us, length us, event | category | flops | bytes accessed | tf_op | source)
XLA Modules:
  0.0 150.5 jit_solution(8815395552425028557)
XLA Ops:
  7.2 0.0 all-gather.6.cloned.1.call-start
  7.2 0.1 pad_add_fusion.place
  7.3 0.0 copy-start.1
  7.3 0.9 copy-done.1
  8.2 0.0 copy-start.3
  8.2 0.8 copy-done.3
  9.1 0.0 copy-start.5
  9.1 0.8 copy-done.5
  9.8 0.0 copy-start.7
  9.8 0.7 copy-done.7
  10.5 2.2 %information.1 = (f32[8,72,128]{2,1,0:T(8,128)S(1)}, f32[8,72,128]{2,1,0:T(8,128)S(1)}) custom-call(s32[3]{0:T(128)S(1)} %pad_add_fusion.place, bf16[16,1024]{1,0:T(8,128)(2,1)S(1)} %copy-done.5, s32[16,1024]{1,0:T(8,128)S(1)} %copy-done.3, bf16[1024,128]{1,0:T(8,128)(2,1)S(1)} %copy-done.1, f32[1,1024]{1,0:T(1,128)S(1)} %bitcast.18), custom_call_target="tpu_custom_call" | custom-call | tf_op jit(solution)/shard_map/information/pallas_call | solution.py:240
  12.7 8.7 %all-gather = f32[16,72,128]{2,1,0:T(8,128)S(1)} all-gather(f32[8,72,128]{2,1,0:T(8,128)S(1)} %get-tuple-element.12), channel_id=2, replica_groups=mesh['z'=8,'x'=4,'y'=8,'c'=2] {'c'}, dimensions={0}, use_global_device_ids=true | all-gather | bytes 884736 | tf_op jit(solution)/shard_map/all_gather | solution.py:257
  21.5 15.0 %all_to_all.30 = f32[8,72,128]{2,1,0:T(8,128)S(1)} all-to-all(f32[8,72,128]{2,1,0:T(8,128)S(1)} %bitcast_add_fusion), channel_id=1, replica_groups=mesh['z'=8,'x'=4,'y'=8,'c'=2] {'y'}, dimensions={0} | all-to-all | bytes 589824 | tf_op jit(solution)/shard_map/all_to_all | solution.py:258
  36.5 0.0 copy-start.9
  36.5 0.0 copy-start.11
  36.5 0.0 copy-start.12
  36.6 13.4 %all_to_all.31 = f32[8,72,128]{2,1,0:T(8,128)S(1)} all-to-all(f32[8,72,128]{2,1,0:T(8,128)S(1)} %broadcast_in_dim.10), channel_id=1, replica_groups=mesh['z'=8,'x'=4,'y'=8,'c'=2] {'y'}, dimensions={0} | all-to-all | bytes 589824 | tf_op jit(solution)/shard_map/all_to_all | solution.py:218
  50.0 4.3 %all-gather.1.packed = f32[16,72,128]{2,1,0:T(8,128)S(1)} all-gather(f32[8,72,128]{2,1,0:T(8,128)S(1)} %all_to_all.31), channel_id=3, replica_groups=mesh['z'=8,'x'=4,'y'=8,'c'=2] {'c'}, dimensions={0}, use_global_device_ids=true | all-gather | bytes 884736 | tf_op jit(solution)/shard_map/all_gather | solution.py:260
  54.3 0.0 copy-done.9
  54.3 0.0 copy-done.11
  54.3 0.0 copy-done.12
  54.3 2.2 %block.1 = (f32[16,136,128]{2,1,0:T(8,128)S(1)}, f32[8,136,128]{2,1,0:T(8,128)S(1)}, f32[4,136,128]{2,1,0:T(8,128)S(1)}, f32[2,136,128]{2,1,0:T(8,128)S(1)}, f32[136,128]{1,0:T(8,128)S(1)}) custom-call(s32[3]{0:T(128)S(1)} %pad_add_fusion.place, f32[16,72,128]{2,1,0:T(8,128)S(1)} %all-gather.1.packed, f32[1,128]{1,0:T(1,128)S(1)} %bitcast.26, ...), custom_call_target="tpu_custom_call" | custom-call | tf_op jit(solution)/shard_map/block/pallas_call | solution.py:263
  56.6 8.8 %all_to_all.32 = f32[4,136,128]{2,1,0:T(8,128)S(1)} all-to-all(f32[4,136,128]{2,1,0:T(8,128)S(1)} %broadcast_in_dim.11), channel_id=1, replica_groups=mesh['z'=8,'x'=4,'y'=8,'c'=2] {'x'}, dimensions={0} | all-to-all | bytes 557056 | tf_op jit(solution)/shard_map/all_to_all | solution.py:218
  65.4 3.2 %all-gather.2 = f32[8,136,128]{2,1,0:T(8,128)S(1)} all-gather(f32[4,136,128]{2,1,0:T(8,128)S(1)} %all_to_all.32), channel_id=4, replica_groups=mesh['z'=8,'x'=4,'y'=8,'c'=2] {'c'}, dimensions={0}, use_global_device_ids=true | all-gather | bytes 835584 | tf_op jit(solution)/shard_map/all_gather | solution.py:272
  68.5 1.1 four.1
  69.6 0.0 copy-start.2
  69.7 0.0 copy-start.4
  69.7 0.0 copy-start.6
  69.7 0.0 copy-start.8
  69.7 0.0 copy-start.10
  69.8 27.7 %all_to_all.33 = f32[8,136,128]{2,1,0:T(8,128)} all-to-all(f32[8,136,128]{2,1,0:T(8,128)S(1)} %broadcast_in_dim.12), channel_id=1, replica_groups=mesh['z'=8,'x'=4,'y'=8,'c'=2] {'z'}, dimensions={0} | all-to-all | bytes 1114112 | tf_op jit(solution)/shard_map/all_to_all | solution.py:218
  97.4 0.0 all-gather.6.cloned.1.call-update
  97.4 8.7 %all-gather.6.cloned.1.call-done = f32[16,136,128]{2,1,0:T(8,128)} async-done(((f32[8,136,128]{2,1,0:T(8,128)}), f32[16,136,128]{2,1,0:T(8,128)}) %all-gather.6.cloned.1.call-update) | async-done | bytes 1114128 | tf_op jit(solution)/shard_map/all_gather | solution.py:282
  106.1 0.0 copy-done.2
  106.1 0.0 copy-done.4
  106.1 0.0 copy-done.6
  106.1 0.0 copy-done.8
  106.1 0.0 copy-done.10
  106.2 0.0 copy-start
  106.2 1.2 copy-done
  107.4 3.7 %final.1 = (f32[16,128]{1,0:T(8,128)}, f32[3,128]{1,0:T(4,128)S(1)}) custom-call(s32[3]{0:T(128)S(1)} %pad_add_fusion.place, f32[2,8,136,128]{3,2,1,0:T(8,128)S(1)} %bitcast.17, f32[2,4,136,128]{3,2,1,0:T(8,128)S(1)} %bitcast.16, f32[16,136,128]{2,1,0:T(8,128)S(1)} %get-tuple-element.14.leaves, f32[8,136,128]{2,1,0:T(8,128)S(1)} %get-tuple-element.15.pairs, ...), custom_call_target="tpu_custom_call" | custom-call | tf_op jit(solution)/shard_map/final/pallas_call | solution.py:287
  111.2 13.1 %all_to_all.34 = f32[16,3,128]{2,1,0:T(4,128)S(1)} all-to-all(f32[16,3,128]{2,1,0:T(4,128)S(1)} %broadcast_in_dim.13), channel_id=1, replica_groups=mesh['z'=8,'x'=4,'y'=8,'c'=2] {'y','c'}, dimensions={0} | all-to-all | bytes 49152 | tf_op jit(solution)/shard_map/all_to_all | solution.py:218
  124.3 18.5 %all_to_all.35 = f32[32,3,128]{2,1,0:T(4,128)S(1)} all-to-all(f32[32,3,128]{2,1,0:T(4,128)S(1)} %broadcast_in_dim.14), channel_id=1, replica_groups=mesh['z'=8,'x'=4,'y'=8,'c'=2] {'z','x'}, dimensions={0} | all-to-all | bytes 98304 | tf_op jit(solution)/shard_map/all_to_all | solution.py:218
  142.9 0.1 reshape.36
  143.0 0.7 copy.15
  (10 shorter events, 0.2 us)
Async XLA Ops:
  7.2 99.0 %all-gather.6.cloned.1.call-start = ((), (), s32[]{:S(2)}) async-start(), calls=%async_computation.6 | async-start | bytes 1671168 | tf_op jit(solution)/shard_map/all_gather | solution.py:282
  7.3 1.0 copy-start.1
  8.2 0.8 copy-start.3
  9.1 0.8 copy-start.5
  9.8 0.7 copy-start.7
  36.5 17.8 %copy-start.9 = (f32[128]{0:T(128)S(1)}, f32[128]{0:T(128)}, u32[]{:S(2)}) copy-start(f32[128]{0:T(128)} %param.14) | copy-start | bytes 1540
  36.5 17.8 %copy-start.11 = (f32[128]{0:T(128)S(1)}, f32[128]{0:T(128)}, u32[]{:S(2)}) copy-start(f32[128]{0:T(128)} %param.13) | copy-start | bytes 1540
  36.5 17.8 %copy-start.12 = (f32[128]{0:T(128)S(1)}, f32[128]{0:T(128)}, u32[]{:S(2)}) copy-start(f32[128]{0:T(128)} %param.12) | copy-start | bytes 1540
  69.6 36.5 %copy-start.2 = (bf16[1024,128]{1,0:T(8,128)(2,1)S(1)}, bf16[1024,128]{1,0:T(8,128)(2,1)}, u32[]{:S(2)}) copy-start(bf16[1024,128]{1,0:T(8,128)(2,1)} %loadings.1) | copy-start | bytes 786436
  69.7 36.5 %copy-start.4 = (s32[16,1024]{1,0:T(8,128)S(1)}, s32[16,1024]{1,0:T(8,128)}, u32[]{:S(2)}) copy-start(s32[16,1024]{1,0:T(8,128)} %present.1) | copy-start | bytes 196612
  69.7 36.5 %copy-start.6 = (bf16[16,1024]{1,0:T(8,128)(2,1)S(1)}, bf16[16,1024]{1,0:T(8,128)(2,1)}, u32[]{:S(2)}) copy-start(bf16[16,1024]{1,0:T(8,128)(2,1)} %readings.1) | copy-start | bytes 98308
  69.7 36.5 %copy-start.8 = (f32[1024]{0:T(1024)S(1)}, f32[1024]{0:T(1024)}, u32[]{:S(2)}) copy-start(f32[1024]{0:T(1024)} %param.11) | copy-start | bytes 12292
  69.7 36.4 %copy-start.10 = (s32[1024]{0:T(1024)S(1)}, s32[1024]{0:T(1024)}, u32[]{:S(2)}) copy-start(s32[1024]{0:T(1024)} %param.15) | copy-start | bytes 12292
  106.2 1.2 copy-start
Sparse Core Ops, SparseCore 0:
  97.5 8.5 all-gather.5

commit v3 on v2

--- a/solution.py
+++ b/solution.py
@@ -144,15 +144,15 @@
 
 
 def walked(nodes, start, own):
-    k = nodes.shape[3]
+    k = start.shape[1]
     current = found = start
     gives = []
-    for i in range(nodes.shape[1]):
+    for i, (group, at) in enumerate((n, j) for n in nodes for j in range(n.shape[1])):
         found = jnp.where(i == own, current, found)
-        wide = jnp.concatenate([nodes[0, i, :k], nodes[1, i, :k]], axis=1)
+        wide = jnp.concatenate([group[0, at, :k], group[1, at, :k]], axis=1)
         product = dot3(current, wide)
-        gives.append(product[:1, k:] + nodes[1, i, k : k + 1])
-        current = product[:, :k] + nodes[0, i, k : k + 1]
+        gives.append(product[:1, k:] + group[1, at, k : k + 1])
+        current = product[:, :k] + group[0, at, k : k + 1]
     return found, current, gives
 
 
@@ -165,7 +165,7 @@
 
 
 def final_kernel(
-    place, planes, blocks, leaves, pairs, quads, eighths, factor_rate, smooth_rate,
+    place, planes_low, planes_high, blocks, leaves, pairs, quads, eighths, factor_rate, smooth_rate,
     readings, present, loadings, noise, regions, scale, smoothed, out,
 ):
     hours, _, k = leaves.shape
@@ -173,10 +173,10 @@
     decays = jnp.exp(-factor_rate[...])
     rate = smooth_rate[...]
     retain = jnp.exp(-rate)
-    start, final, plane_gives = walked(planes, jnp.zeros((8, k), F32), z)
+    start, final, plane_gives = walked((planes_low, planes_high), jnp.zeros((8, k), F32), z)
     span = hours * blocks.shape[1]
     behind_plane = followed(plane_gives, decays * final[:1], z, jnp.exp(-span * rate))
-    start, _, block_gives = walked(blocks, start, x)
+    start, _, block_gives = walked((blocks,), start, x)
     following = followed(block_gives, behind_plane, x, jnp.exp(-hours * rate))
     after = {-1: start}
     after[7] = applied(start, eighths[0])
@@ -251,7 +251,7 @@
             pltpu.VMEM((hours, k), F32),
             pltpu.SemaphoreType.DMA((4,)),
         ],
-        compiler_params=PARAMS,
+        compiler_params=pltpu.CompilerParams(vmem_limit_bytes=60 * 1024 * 1024),
         name="information",
     )(place, readings, present, loadings, noise)
     arrived = lax.dynamic_index_in_dim(lax.all_gather(sent, "c"), 1 - core, 0, keepdims=False)
@@ -279,7 +279,8 @@
         compiler_params=PARAMS,
         name="four",
     )(place, blocks, smooth)
-    planes = lax.all_gather(sent_to_all(half_total, "z"), "c")
+    half_planes = sent_to_all(half_total, "z")
+    planes = [lax.all_gather(half_planes[at : at + 4], "c") for at in range(0, nz, 4)]
 
     hours_all = hours * nz * nx
     series_all = series * ny * cores
@@ -287,12 +288,12 @@
     smoothed, local = pl.pallas_call(
         final_kernel,
         out_shape=[shape_of(hours, k), shape_of(3, 128)],
-        in_specs=[SM] + [VM] * 13 + [SM],
+        in_specs=[SM] + [VM] * 14 + [SM],
         out_specs=[VM] * 2,
         compiler_params=PARAMS,
         name="final",
     )(
-        place, planes, blocks, leaves, pairs, quads, eighths, factor, smooth,
+        place, *planes, blocks, leaves, pairs, quads, eighths, factor, smooth,
         readings, present, loadings, noise, regions.reshape(1, series), scale,
     )
 

time: 151 us -> 124 us (0.82)
  between operations: 14.2 us -> 0.77 us
  waiting for transfers between devices: 8.71 us -> 0 us
  local copies, waits for them, and re-layouts: 5.38 us -> 0.95 us
  blocking collectives: 113 us -> 109 us
  Pallas kernels: 9.21 us -> 10.9 us
  other arithmetic: 0.2 us -> 1.73 us
    all_to_all x5, blocking collectives: 81.5 us -> 71.7 us  [sent_to_all(): lax.all_to_all(jnp.broadcast_to(shard[None], (count, *shard.shape)), axis...]
    all_gather x1 -> x0, waiting for transfers between devices: 8.7 us -> none  [body(): planes = lax.all_gather(sent_to_all(half_total, 'z'), 'c')]
    all_gather x0 -> x2, blocking collectives: none -> 5.59 us  [body(): lax.all_gather(half_planes[at:at + 4], 'c')]
    unnamed x27 -> x19, local copies, waits for them, and re-layouts: 5.2 us -> 0.73 us
    pallas_call x1, Pallas kernels: 2.17 us -> 3.81 us  [body(): pl.pallas_call(information_kernel, out_shape=[shape_of(share, height, k)]...]
  transfers between devices with their start and end apart: 1 -> 0, of which waited for: 1 -> 0; matrix products, arithmetic and copies ran while one was open for 0% -> 0% of each run, Pallas kernels for 0% -> 0%
where the time goes in v3:
time: 124 us; the launch traced here: 123 us
  blocking collectives  109 us (88%)
  Pallas kernels  10.9 us (9%)
  other arithmetic  1.73 us (1%)
    all_to_all x5, blocking collectives, sent_to_all(): lax.all_to_all(jnp.broadcast_to(shard[None], (count, *shard.shape)), axis...  71.7 us
    all_to_all x1, blocking collectives, body(): packed = lax.all_to_all(kept + arrived, 'y', 0, 0, tiled=True).sum(axis=0)  15 us
    all_gather x1, blocking collectives, body(): lax.all_gather(sent, 'c')  8.95 us
    all_gather x2, blocking collectives, body(): lax.all_gather(half_planes[at:at + 4], 'c')  5.59 us
    all_gather x1, blocking collectives, body(): packed = lax.all_gather(packed, 'c').reshape(hours, height, k)  4.33 us
    pallas_call x1, Pallas kernels, body(): pl.pallas_call(information_kernel, out_shape=[shape_of(share, height, k)]...  3.81 us
    pallas_call x1, Pallas kernels, body(): pl.pallas_call(final_kernel, out_shape=[shape_of(hours, k), shape_of(3, 1...  3.76 us
    all_gather x1, blocking collectives, body(): blocks = lax.all_gather(sent_to_all(half_total, 'x'), 'c')  3.19 us

profile of v3, /device:TPU:1, one launch (start us, length us, event | category | flops | bytes accessed | tf_op | source)
XLA Modules:
  0.0 123.1 jit_solution(8630025227426585115)
XLA Ops:
  0.6 0.6 pad_add_fusion.place
  1.3 3.8 %information.1 = (f32[8,72,128]{2,1,0:T(8,128)}, f32[8,72,128]{2,1,0:T(8,128)}) custom-call(s32[3]{0:T(128)} %pad_add_fusion.place, bf16[16,1024]{1,0:T(8,128)(2,1)} %readings.1, s32[16,1024]{1,0:T(8,128)} %present.1, bf16[1024,128]{1,0:T(8,128)(2,1)} %loadings.1, f32[1,1024]{1,0:T(1,128)} %bitcast.20), custom_call_target="tpu_custom_call" | custom-call | tf_op jit(solution)/shard_map/information/pallas_call | solution.py:240
  5.1 8.9 %all-gather = f32[16,72,128]{2,1,0:T(8,128)S(1)} all-gather(f32[8,72,128]{2,1,0:T(8,128)} %get-tuple-element.12), channel_id=2, replica_groups=mesh['z'=8,'x'=4,'y'=8,'c'=2] {'c'}, dimensions={0}, use_global_device_ids=true | all-gather | bytes 884736 | tf_op jit(solution)/shard_map/all_gather | solution.py:257
  14.0 1.0 bitcast_add_fusion
  15.0 15.0 %all_to_all.30 = f32[8,72,128]{2,1,0:T(8,128)S(1)} all-to-all(f32[8,72,128]{2,1,0:T(8,128)S(1)} %bitcast_add_fusion), channel_id=1, replica_groups=mesh['z'=8,'x'=4,'y'=8,'c'=2] {'y'}, dimensions={0} | all-to-all | bytes 589824 | tf_op jit(solution)/shard_map/all_to_all | solution.py:258
  30.1 0.0 copy-start.4
  30.1 0.0 copy-start.5
  30.1 0.0 copy-start.7
  30.1 0.0 copy-start.8
  30.2 13.4 %all_to_all.31 = f32[8,72,128]{2,1,0:T(8,128)S(1)} all-to-all(f32[8,72,128]{2,1,0:T(8,128)S(1)} %broadcast_in_dim.10), channel_id=1, replica_groups=mesh['z'=8,'x'=4,'y'=8,'c'=2] {'y'}, dimensions={0} | all-to-all | bytes 589824 | tf_op jit(solution)/shard_map/all_to_all | solution.py:218
  43.6 4.3 %all-gather.1.packed = f32[16,72,128]{2,1,0:T(8,128)S(1)} all-gather(f32[8,72,128]{2,1,0:T(8,128)S(1)} %all_to_all.31), channel_id=3, replica_groups=mesh['z'=8,'x'=4,'y'=8,'c'=2] {'c'}, dimensions={0}, use_global_device_ids=true | all-gather | bytes 884736 | tf_op jit(solution)/shard_map/all_gather | solution.py:260
  47.9 0.0 copy-done.4
  47.9 0.0 copy-done.5
  47.9 0.0 copy-done.7
  47.9 0.0 copy-done.8
  47.9 2.2 %block.1 = (f32[16,136,128]{2,1,0:T(8,128)S(1)}, f32[8,136,128]{2,1,0:T(8,128)S(1)}, f32[4,136,128]{2,1,0:T(8,128)S(1)}, f32[2,136,128]{2,1,0:T(8,128)S(1)}, f32[136,128]{1,0:T(8,128)S(1)}) custom-call(s32[3]{0:T(128)S(1)} %copy-done.4, f32[16,72,128]{2,1,0:T(8,128)S(1)} %all-gather.1.packed, f32[1,128]{1,0:T(1,128)S(1)} %bitcast.28, f32[1,128]{1,0:T(1,128)S(1)} %bitcast.26, ...), custom_call_target="tpu_custom_call" | custom-call | tf_op jit(solution)/shard_map/block/pallas_call | solution.py:263
  50.2 8.8 %all_to_all.32 = f32[4,136,128]{2,1,0:T(8,128)S(1)} all-to-all(f32[4,136,128]{2,1,0:T(8,128)S(1)} %broadcast_in_dim.11), channel_id=1, replica_groups=mesh['z'=8,'x'=4,'y'=8,'c'=2] {'x'}, dimensions={0} | all-to-all | bytes 557056 | tf_op jit(solution)/shard_map/all_to_all | solution.py:218
  58.9 3.2 %all-gather.2 = f32[8,136,128]{2,1,0:T(8,128)S(1)} all-gather(f32[4,136,128]{2,1,0:T(8,128)S(1)} %all_to_all.32), channel_id=4, replica_groups=mesh['z'=8,'x'=4,'y'=8,'c'=2] {'c'}, dimensions={0}, use_global_device_ids=true | all-gather | bytes 835584 | tf_op jit(solution)/shard_map/all_gather | solution.py:272
  62.1 1.1 four.1
  63.3 27.4 %all_to_all.33 = f32[8,136,128]{2,1,0:T(8,128)S(1)} all-to-all(f32[8,136,128]{2,1,0:T(8,128)S(1)} %broadcast_in_dim.12), channel_id=1, replica_groups=mesh['z'=8,'x'=4,'y'=8,'c'=2] {'z'}, dimensions={0} | all-to-all | bytes 1114112 | tf_op jit(solution)/shard_map/all_to_all | solution.py:218
  90.7 0.0 copy-start
  90.7 0.0 copy-start.1
  90.8 0.0 copy-start.2
  90.8 0.0 copy-start.3
  90.8 0.0 copy-start.6
  90.8 3.4 %all-gather.4 = f32[8,136,128]{2,1,0:T(8,128)S(1)} all-gather(f32[4,136,128]{2,1,0:T(8,128)S(1)} %get-tuple-element.28), channel_id=6, replica_groups=mesh['z'=8,'x'=4,'y'=8,'c'=2] {'c'}, dimensions={0}, use_global_device_ids=true | all-gather | bytes 835584 | tf_op jit(solution)/shard_map/all_gather | solution.py:283
  94.2 2.2 %all-gather.3 = f32[8,136,128]{2,1,0:T(8,128)S(1)} all-gather(f32[4,136,128]{2,1,0:T(8,128)S(1)} %get-tuple-element.29), channel_id=5, replica_groups=mesh['z'=8,'x'=4,'y'=8,'c'=2] {'c'}, dimensions={0}, use_global_device_ids=true | all-gather | bytes 835584 | tf_op jit(solution)/shard_map/all_gather | solution.py:283
  96.4 0.0 copy-done
  96.4 0.0 copy-done.1
  96.4 0.0 copy-done.2
  96.4 0.0 copy-done.3
  96.4 0.0 copy-done.6
  96.4 3.8 %final.1 = (f32[16,128]{1,0:T(8,128)}, f32[3,128]{1,0:T(4,128)S(1)}) custom-call(s32[3]{0:T(128)S(1)} %copy-done.4, f32[2,4,136,128]{3,2,1,0:T(8,128)S(1)} %bitcast.19, f32[2,4,136,128]{3,2,1,0:T(8,128)S(1)} %bitcast.18, f32[2,4,136,128]{3,2,1,0:T(8,128)S(1)} %bitcast.17, f32[16,136,128]{2,1,0:T(8,128)S(1)} %get-tuple-element.14.leaves, ...), custom_call_target="tpu_custom_call" | custom-call | tf_op jit(solution)/shard_map/final/pallas_call | solution.py:288
  100.2 10.2 %all_to_all.34 = f32[16,3,128]{2,1,0:T(4,128)S(1)} all-to-all(f32[16,3,128]{2,1,0:T(4,128)S(1)} %broadcast_in_dim.13), channel_id=1, replica_groups=mesh['z'=8,'x'=4,'y'=8,'c'=2] {'y','c'}, dimensions={0} | all-to-all | bytes 49152 | tf_op jit(solution)/shard_map/all_to_all | solution.py:218
  110.4 11.8 %all_to_all.35 = f32[32,3,128]{2,1,0:T(4,128)S(1)} all-to-all(f32[32,3,128]{2,1,0:T(4,128)S(1)} %broadcast_in_dim.14), channel_id=1, replica_groups=mesh['z'=8,'x'=4,'y'=8,'c'=2] {'z','x'}, dimensions={0} | all-to-all | bytes 98304 | tf_op jit(solution)/shard_map/all_to_all | solution.py:218
  122.3 0.1 reshape.36
  122.4 0.7 copy.15
  (10 shorter events, 0.2 us)
Async XLA Ops:
  30.1 17.8 %copy-start.4 = (s32[3]{0:T(128)S(1)}, s32[3]{0:T(128)}, u32[]{:S(2)}) copy-start(s32[3]{0:T(128)} %pad_add_fusion.place) | copy-start | bytes 40
  30.1 17.8 %copy-start.5 = (f32[128]{0:T(128)S(1)}, f32[128]{0:T(128)}, u32[]{:S(2)}) copy-start(f32[128]{0:T(128)} %param.14) | copy-start | bytes 1540
  30.1 17.8 %copy-start.7 = (f32[128]{0:T(128)S(1)}, f32[128]{0:T(128)}, u32[]{:S(2)}) copy-start(f32[128]{0:T(128)} %param.13) | copy-start | bytes 1540
  30.1 17.8 %copy-start.8 = (f32[128]{0:T(128)S(1)}, f32[128]{0:T(128)}, u32[]{:S(2)}) copy-start(f32[128]{0:T(128)} %param.12) | copy-start | bytes 1540
  90.7 5.7 %copy-start = (bf16[1024,128]{1,0:T(8,128)(2,1)S(1)}, bf16[1024,128]{1,0:T(8,128)(2,1)}, u32[]{:S(2)}) copy-start(bf16[1024,128]{1,0:T(8,128)(2,1)} %loadings.1) | copy-start | bytes 786436
  90.7 5.6 %copy-start.1 = (s32[16,1024]{1,0:T(8,128)S(1)}, s32[16,1024]{1,0:T(8,128)}, u32[]{:S(2)}) copy-start(s32[16,1024]{1,0:T(8,128)} %present.1) | copy-start | bytes 196612
  90.8 5.6 %copy-start.2 = (bf16[16,1024]{1,0:T(8,128)(2,1)S(1)}, bf16[16,1024]{1,0:T(8,128)(2,1)}, u32[]{:S(2)}) copy-start(bf16[16,1024]{1,0:T(8,128)(2,1)} %readings.1) | copy-start | bytes 98308
  90.8 5.6 %copy-start.3 = (f32[1024]{0:T(1024)S(1)}, f32[1024]{0:T(1024)}, u32[]{:S(2)}) copy-start(f32[1024]{0:T(1024)} %param.11) | copy-start | bytes 12292
  90.8 5.6 %copy-start.6 = (s32[1024]{0:T(1024)S(1)}, s32[1024]{0:T(1024)}, u32[]{:S(2)}) copy-start(s32[1024]{0:T(1024)} %param.15) | copy-start | bytes 12292

commit v4 on v2

--- a/solution.py
+++ b/solution.py
@@ -33,9 +33,11 @@
 
 
 def dot3(a, b):
+    rows = a.shape[0]
     ah, al = halves(a)
     bh, bl = halves(b)
-    return bdot(ah, bh) + (bdot(ah, bl) + bdot(al, bh))
+    both = bdot(jnp.concatenate([ah, al], axis=0), bh)
+    return both[:rows] + (both[rows:] + bdot(ah, bl))
 
 
 def across(a, b):
@@ -52,7 +54,7 @@
 
 
 def information_kernel(
-    place, readings_hbm, present_hbm, loadings_hbm, noise_hbm, kept, sent,
+    readings_hbm, present_hbm, loadings_hbm, noise_hbm, kept, sent,
     readings, present, loadings, noise, seen, scores, sems,
 ):
     pairs = (
@@ -64,15 +66,21 @@
     copies = [pltpu.make_async_copy(a, b, sems.at[i]) for i, (a, b) in enumerate(pairs)]
     for copy in copies:
         copy.start()
-    for copy in copies:
-        copy.wait()
-    count = kept.shape[0]
-    core = place[2]
+    core = lax.axis_index("c")
+    count, _, k = kept.shape
+    half = k // 2
+    copies[0].wait()
+    copies[1].wait()
     load = loadings[...]
-    k = load.shape[1]
-    half = k // 2
-    scaled = (jnp.transpose(load.astype(F32)) * noise[...]).astype(BF16)
+    turned = jnp.transpose(load.astype(F32))
+    scaled_wide = turned * noise[...]
+    scaled = scaled_wide.astype(BF16)
+    turned = turned.astype(BF16)
+    columns = jnp.concatenate([load, jnp.transpose(scaled.astype(F32)).astype(BF16)], axis=0)
+    lines = jnp.concatenate([scaled, turned], axis=1)
+    copies[2].wait()
     seen[...] = present[...].astype(F32)
+    copies[3].wait()
     scores[...] = across(readings[...] * seen[...].astype(BF16), scaled)
     row, lane = iotas(half, k)
     row_k, lane_k = iotas(k, k)
@@ -80,7 +88,7 @@
         first = (core if slot == 0 else 1 - core) * count
         for i in range(count):
             observed = seen[pl.ds(first + i, 1), :].astype(BF16)
-            inform = bdot(scaled * observed, load)
+            inform = 0.5 * bdot(lines * jnp.concatenate([observed, observed], axis=1), columns)
             folded = pltpu.roll(inform[half:], half, 1)
             out[i, :half] = jnp.where(lane >= row, inform[:half], folded)
             diagonal = jnp.sum(jnp.where(row_k == lane_k, inform, 0.0), axis=0, keepdims=True)
@@ -90,7 +98,7 @@
 
 
 def block_kernel(
-    place, packed, gain, factor_rate, smooth_rate, leaves, pairs, quads, eighths, half_total,
+    packed, gain, factor_rate, smooth_rate, leaves, pairs, quads, eighths, half_total,
     given1, given2, given4, given8,
 ):
     hours = packed.shape[0]
@@ -126,16 +134,16 @@
             )
         below, given = above, gives
     total = joined((below[0], given[0]), (below[1], given[1]), jnp.exp(-8.0 * rate))
-    half_total[...] = jnp.where(place[2] == 0, total[0], total[1])
-
-
-def four_kernel(place, blocks, smooth_rate, half_total):
+    half_total[...] = jnp.where(lax.axis_index("c") == 0, total[0], total[1])
+
+
+def four_kernel(blocks, smooth_rate, half_total):
     rate = smooth_rate[...]
     short, long = jnp.exp(-16.0 * rate), jnp.exp(-32.0 * rate)
     one = joined((blocks[0, 0], blocks[1, 0]), (blocks[0, 1], blocks[1, 1]), short)
     two = joined((blocks[0, 2], blocks[1, 2]), (blocks[0, 3], blocks[1, 3]), short)
     total = joined(one, two, long)
-    half_total[...] = jnp.where(place[2] == 0, total[0], total[1])
+    half_total[...] = jnp.where(lax.axis_index("c") == 0, total[0], total[1])
 
 
 def applied(current, one):
@@ -143,16 +151,19 @@
     return dot3(current, one[:k]) + one[k : k + 1]
 
 
-def walked(nodes, start, own):
-    k = nodes.shape[3]
-    current = found = start
+def walked(nodes, current, own):
+    k = current.shape[1]
+    found = current
     gives = []
-    for i in range(nodes.shape[1]):
+    for i, (maps, given) in enumerate(nodes):
         found = jnp.where(i == own, current, found)
-        wide = jnp.concatenate([nodes[0, i, :k], nodes[1, i, :k]], axis=1)
-        product = dot3(current, wide)
-        gives.append(product[:1, k:] + nodes[1, i, k : k + 1])
-        current = product[:, :k] + nodes[0, i, k : k + 1]
+        if maps.shape[0] < k:
+            gives.append(None)
+            current = current + maps[:1]
+            continue
+        product = dot3(current, jnp.concatenate([maps[:k], given[:k]], axis=1))
+        gives.append(product[:1, k:] + given[k : k + 1])
+        current = product[:, :k] + maps[k : k + 1]
     return found, current, gives
 
 
@@ -160,23 +171,29 @@
     found = following = after
     for i in reversed(range(len(gives))):
         found = jnp.where(i == own, following, found)
-        following = gives[i] + fade * following
+        if gives[i] is not None:
+            following = gives[i] + fade * following
     return found
 
 
 def final_kernel(
-    place, planes, blocks, leaves, pairs, quads, eighths, factor_rate, smooth_rate,
+    planes, blocks, leaves, pairs, quads, eighths, factor_rate, smooth_rate,
     readings, present, loadings, noise, regions, scale, smoothed, out,
 ):
     hours, _, k = leaves.shape
-    z, x = place[0], place[1]
+    z, x = lax.axis_index("z"), lax.axis_index("x")
     decays = jnp.exp(-factor_rate[...])
     rate = smooth_rate[...]
     retain = jnp.exp(-rate)
-    start, final, plane_gives = walked(planes, jnp.zeros((8, k), F32), z)
+    tall = blocks.shape[2]
+    plane_nodes = [(planes[0, : tall - k], planes[1, : tall - k])]
+    for at in range(tall - k, planes.shape[1], tall):
+        plane_nodes.append((planes[0, at : at + tall], planes[1, at : at + tall]))
+    start, final, plane_gives = walked(plane_nodes, jnp.zeros((8, k), F32), z)
     span = hours * blocks.shape[1]
     behind_plane = followed(plane_gives, decays * final[:1], z, jnp.exp(-span * rate))
-    start, _, block_gives = walked(blocks, start, x)
+    block_nodes = [(blocks[0, i], blocks[1, i]) for i in range(blocks.shape[1])]
+    start, _, block_gives = walked(block_nodes, start, x)
     following = followed(block_gives, behind_plane, x, jnp.exp(-hours * rate))
     after = {-1: start}
     after[7] = applied(start, eighths[0])
@@ -213,6 +230,21 @@
     )
 
 
+def tail_kernel(parts, out):
+    total = jnp.sum(parts[...], axis=0)
+    slots = 128 // GROUPS
+    group, lane = iotas(GROUPS, 128)
+    slot, column = iotas(128, 128)
+    found = jnp.zeros((GROUPS, 128), F32)
+    for r in range(3):
+        spread = jnp.where(lax.rem(lane, GROUPS) == group, total[r : r + 1], 0.0)
+        chosen = (lax.div(slot, GROUPS) + slots * r == column).astype(F32).astype(BF16)
+        high, low = halves(spread)
+        lowest = (spread - high.astype(F32) - low.astype(F32)).astype(BF16)
+        found = found + (bdot(high, chosen) + (bdot(low, chosen) + bdot(lowest, chosen)))
+    out[...] = found[:, :BINS]
+
+
 def sent_to_all(shard, axis):
     count = lax.axis_size(axis)
     return lax.all_to_all(
@@ -232,15 +264,14 @@
     height, tall = k // 2 + 8, k + 8
     noise = noise_precision.reshape(1, series)
     gain, factor, smooth = (a.reshape(1, k) for a in (update_gain, factor_rate, smooth_rate))
-    z, x, core = (lax.axis_index(a) for a in ("z", "x", "c"))
+    core = lax.axis_index("c")
     nz, nx, ny, cores = (lax.axis_size(a) for a in ("z", "x", "y", "c"))
-    place = jnp.stack([z, x, core]).astype(jnp.int32)
     share = hours // cores
 
     kept, sent = pl.pallas_call(
         information_kernel,
         out_shape=[shape_of(share, height, k)] * 2,
-        in_specs=[SM] + [HB] * 4,
+        in_specs=[HB] * 4,
         out_specs=[VM] * 2,
         scratch_shapes=[
             pltpu.VMEM((hours, series), BF16),
@@ -253,7 +284,7 @@
         ],
         compiler_params=PARAMS,
         name="information",
-    )(place, readings, present, loadings, noise)
+    )(*(pltpu.with_memory_space_constraint(a, pltpu.HBM) for a in (readings, present, loadings, noise)))
     arrived = lax.dynamic_index_in_dim(lax.all_gather(sent, "c"), 1 - core, 0, keepdims=False)
     packed = lax.all_to_all(kept + arrived, "y", 0, 0, tiled=True).sum(axis=0)
     packed = sent_to_all(packed, "y")
@@ -263,23 +294,24 @@
     leaves, pairs, quads, eighths, half_total = pl.pallas_call(
         block_kernel,
         out_shape=nodes + [shape_of(tall, k)],
-        in_specs=[SM] + [VM] * 4,
+        in_specs=[VM] * 4,
         out_specs=[VM] * 5,
         scratch_shapes=[pltpu.VMEM((hours // n, tall, k), F32) for n in (1, 2, 4, 8)],
         compiler_params=PARAMS,
         name="block",
-    )(place, packed, gain, factor, smooth)
+    )(packed, gain, factor, smooth)
     blocks = lax.all_gather(sent_to_all(half_total, "x"), "c")
 
     half_total = pl.pallas_call(
         four_kernel,
         out_shape=shape_of(tall, k),
-        in_specs=[SM] + [VM] * 2,
+        in_specs=[VM] * 2,
         out_specs=VM,
         compiler_params=PARAMS,
         name="four",
-    )(place, blocks, smooth)
-    planes = lax.all_gather(sent_to_all(half_total, "z"), "c")
+    )(blocks, smooth)
+    half_planes = sent_to_all(half_total, "z").reshape(nz * tall, k)
+    planes = lax.all_gather(half_planes[k:], "c")
 
     hours_all = hours * nz * nx
     series_all = series * ny * cores
@@ -287,18 +319,24 @@
     smoothed, local = pl.pallas_call(
         final_kernel,
         out_shape=[shape_of(hours, k), shape_of(3, 128)],
-        in_specs=[SM] + [VM] * 13 + [SM],
+        in_specs=[VM] * 13 + [SM],
         out_specs=[VM] * 2,
         compiler_params=PARAMS,
         name="final",
     )(
-        place, planes, blocks, leaves, pairs, quads, eighths, factor, smooth,
+        planes, blocks, leaves, pairs, quads, eighths, factor, smooth,
         readings, present, loadings, noise, regions.reshape(1, series), scale,
     )
 
     local = sent_to_all(local, SERIES).sum(axis=0)
-    local = sent_to_all(local, TM).sum(axis=0)
-    histogram = local.reshape(24, GROUPS)[:BINS].T
+    histogram = pl.pallas_call(
+        tail_kernel,
+        out_shape=shape_of(GROUPS, BINS),
+        in_specs=[VM],
+        out_specs=VM,
+        compiler_params=PARAMS,
+        name="tail",
+    )(sent_to_all(local, TM))
     return (smoothed, histogram)
 
 

time: 151 us -> 118 us (0.78)
  between operations: 14.2 us -> 0.73 us
  waiting for transfers between devices: 8.71 us -> 0 us
  blocking collectives: 113 us -> 107 us
  local copies, waits for them, and re-layouts: 5.38 us -> 0.16 us
    all_to_all x5, blocking collectives: 81.5 us -> 71.7 us  [sent_to_all(): lax.all_to_all(jnp.broadcast_to(shard[None], (count, *shard.shape)), axis...]
    all_gather x1 -> x0, waiting for transfers between devices: 8.7 us -> none  [body(): planes = lax.all_gather(sent_to_all(half_total, 'z'), 'c')]
    unnamed x27 -> x16, local copies, waits for them, and re-layouts: 5.2 us -> 0.03 us
    all_gather x0 -> x1, blocking collectives: none -> 3.69 us  [body(): planes = lax.all_gather(half_planes[k:], 'c')]
  transfers between devices with their start and end apart: 1 -> 0, of which waited for: 1 -> 0; matrix products, arithmetic and copies ran while one was open for 0% -> 0% of each run, Pallas kernels for 0% -> 0%
where the time goes in v4:
time: 118 us; the launch traced here: 117 us
  blocking collectives  107 us (91%)
  Pallas kernels  9.67 us (8%)
    all_to_all x5, blocking collectives, sent_to_all(): lax.all_to_all(jnp.broadcast_to(shard[None], (count, *shard.shape)), axis...  71.7 us
    all_to_all x1, blocking collectives, body(): packed = lax.all_to_all(kept + arrived, 'y', 0, 0, tiled=True).sum(axis=0)  15 us
    all_gather x1, blocking collectives, body(): lax.all_gather(sent, 'c')  8.73 us
    all_gather x1, blocking collectives, body(): packed = lax.all_gather(packed, 'c').reshape(hours, height, k)  4.33 us
    all_gather x1, blocking collectives, body(): planes = lax.all_gather(half_planes[k:], 'c')  3.69 us
    pallas_call x1, Pallas kernels, body(): pl.pallas_call(information_kernel, out_shape=[shape_of(share, height, k)]...  3.68 us
    all_gather x1, blocking collectives, body(): blocks = lax.all_gather(sent_to_all(half_total, 'x'), 'c')  3.18 us
    pallas_call x1, Pallas kernels, body(): pl.pallas_call(final_kernel, out_shape=[shape_of(hours, k), shape_of(3, 1...  2.85 us

profile of v4, /device:TPU:1, one launch (start us, length us, event | category | flops | bytes accessed | tf_op | source)
XLA Modules:
  0.0 117.3 jit_solution(13181788566213326358)
XLA Ops:
  0.6 3.7 %information.1 = (f32[8,72,128]{2,1,0:T(8,128)S(1)}, f32[8,72,128]{2,1,0:T(8,128)S(1)}) custom-call(bf16[16,1024]{1,0:T(8,128)(2,1)} %readings.1, s32[16,1024]{1,0:T(8,128)} %present.1, bf16[1024,128]{1,0:T(8,128)(2,1)} %loadings.1, f32[1,1024]{1,0:T(1,128)} %bitcast.14), custom_call_target="tpu_custom_call" | custom-call | tf_op jit(solution)/shard_map/information/pallas_call | solution.py:271
  4.3 8.7 %all-gather = f32[16,72,128]{2,1,0:T(8,128)S(1)} all-gather(f32[8,72,128]{2,1,0:T(8,128)S(1)} %get-tuple-element.12), channel_id=2, replica_groups=mesh['z'=8,'x'=4,'y'=8,'c'=2] {'c'}, dimensions={0}, use_global_device_ids=true | all-gather | bytes 884736 | tf_op jit(solution)/shard_map/all_gather | solution.py:288
  13.1 15.0 %all_to_all.30 = f32[8,72,128]{2,1,0:T(8,128)S(1)} all-to-all(f32[8,72,128]{2,1,0:T(8,128)S(1)} %bitcast_add_fusion), channel_id=1, replica_groups=mesh['z'=8,'x'=4,'y'=8,'c'=2] {'y'}, dimensions={0} | all-to-all | bytes 589824 | tf_op jit(solution)/shard_map/all_to_all | solution.py:289
  28.1 0.0 copy-start.4
  28.1 0.0 copy-start.6
  28.1 0.0 copy-start.7
  28.2 13.4 %all_to_all.31 = f32[8,72,128]{2,1,0:T(8,128)S(1)} all-to-all(f32[8,72,128]{2,1,0:T(8,128)S(1)} %broadcast_in_dim.10), channel_id=1, replica_groups=mesh['z'=8,'x'=4,'y'=8,'c'=2] {'y'}, dimensions={0} | all-to-all | bytes 589824 | tf_op jit(solution)/shard_map/all_to_all | solution.py:250
  41.6 4.3 %all-gather.1.packed = f32[16,72,128]{2,1,0:T(8,128)S(1)} all-gather(f32[8,72,128]{2,1,0:T(8,128)S(1)} %all_to_all.31), channel_id=3, replica_groups=mesh['z'=8,'x'=4,'y'=8,'c'=2] {'c'}, dimensions={0}, use_global_device_ids=true | all-gather | bytes 884736 | tf_op jit(solution)/shard_map/all_gather | solution.py:291
  45.9 0.0 copy-done.4
  45.9 0.0 copy-done.6
  45.9 0.0 copy-done.7
  45.9 1.8 %block.1 = (f32[16,136,128]{2,1,0:T(8,128)S(1)}, f32[8,136,128]{2,1,0:T(8,128)S(1)}, f32[4,136,128]{2,1,0:T(8,128)S(1)}, f32[2,136,128]{2,1,0:T(8,128)S(1)}, f32[136,128]{1,0:T(8,128)S(1)}) custom-call(f32[16,72,128]{2,1,0:T(8,128)S(1)} %all-gather.1.packed, f32[1,128]{1,0:T(1,128)S(1)} %bitcast.22, f32[1,128]{1,0:T(1,128)S(1)} %bitcast.20, ...), custom_call_target="tpu_custom_call" | custom-call | tf_op jit(solution)/shard_map/block/pallas_call | solution.py:294
  47.8 8.8 %all_to_all.32 = f32[4,136,128]{2,1,0:T(8,128)S(1)} all-to-all(f32[4,136,128]{2,1,0:T(8,128)S(1)} %broadcast_in_dim.11), channel_id=1, replica_groups=mesh['z'=8,'x'=4,'y'=8,'c'=2] {'x'}, dimensions={0} | all-to-all | bytes 557056 | tf_op jit(solution)/shard_map/all_to_all | solution.py:250
  56.6 3.2 %all-gather.2 = f32[8,136,128]{2,1,0:T(8,128)S(1)} all-gather(f32[4,136,128]{2,1,0:T(8,128)S(1)} %all_to_all.32), channel_id=4, replica_groups=mesh['z'=8,'x'=4,'y'=8,'c'=2] {'c'}, dimensions={0}, use_global_device_ids=true | all-gather | bytes 835584 | tf_op jit(solution)/shard_map/all_gather | solution.py:303
  59.8 0.5 four.1
  60.3 27.4 %all_to_all.33 = f32[8,136,128]{2,1,0:T(8,128)S(1)} all-to-all(f32[8,136,128]{2,1,0:T(8,128)S(1)} %broadcast_in_dim.12), channel_id=1, replica_groups=mesh['z'=8,'x'=4,'y'=8,'c'=2] {'z'}, dimensions={0} | all-to-all | bytes 1114112 | tf_op jit(solution)/shard_map/all_to_all | solution.py:250
  87.7 0.0 copy-start
  87.7 0.0 copy-start.1
  87.7 0.0 copy-start.2
  87.7 0.0 copy-start.3
  87.7 0.0 copy-start.5
  87.8 3.7 %all-gather.3 = f32[1920,128]{1,0:T(8,128)S(1)} all-gather(f32[960,128]{1,0:T(8,128)S(1)} %slice.4), channel_id=5, replica_groups=mesh['z'=8,'x'=4,'y'=8,'c'=2] {'c'}, dimensions={0}, use_global_device_ids=true | all-gather | bytes 1474560 | tf_op jit(solution)/shard_map/all_gather | solution.py:314
  91.5 0.0 copy-done
  91.5 0.0 copy-done.1
  91.5 0.0 copy-done.2
  91.5 0.0 copy-done.3
  91.5 0.0 copy-done.5
  91.5 2.8 %final.1 = (f32[16,128]{1,0:T(8,128)}, f32[3,128]{1,0:T(4,128)S(1)}) custom-call(f32[2,960,128]{2,1,0:T(8,128)S(1)} %bitcast.13, f32[2,4,136,128]{3,2,1,0:T(8,128)S(1)} %bitcast.12, f32[16,136,128]{2,1,0:T(8,128)S(1)} %get-tuple-element.14.leaves, f32[8,136,128]{2,1,0:T(8,128)S(1)} %get-tuple-element.15.pairs, f32[4,136,128]{2,1,0:T(8,128)S(1)} %get-tuple-element.16.quads, ...), custom_call_target="tpu_custom_call" | custom-call | tf_op jit(solution)/shard_map/final/pallas_call | solution.py:319
  94.4 10.2 %all_to_all.34 = f32[16,3,128]{2,1,0:T(4,128)S(1)} all-to-all(f32[16,3,128]{2,1,0:T(4,128)S(1)} %broadcast_in_dim.13), channel_id=1, replica_groups=mesh['z'=8,'x'=4,'y'=8,'c'=2] {'y','c'}, dimensions={0} | all-to-all | bytes 49152 | tf_op jit(solution)/shard_map/all_to_all | solution.py:250
  104.6 11.8 %all_to_all.35.parts = f32[32,3,128]{2,1,0:T(4,128)S(1)} all-to-all(f32[32,3,128]{2,1,0:T(4,128)S(1)} %broadcast_in_dim.14), channel_id=1, replica_groups=mesh['z'=8,'x'=4,'y'=8,'c'=2] {'z','x'}, dimensions={0} | all-to-all | bytes 98304 | tf_op jit(solution)/shard_map/all_to_all | solution.py:250
  116.5 0.8 tail.1
  (9 shorter events, 0.2 us)
Async XLA Ops:
  28.1 17.8 %copy-start.4 = (f32[128]{0:T(128)S(1)}, f32[128]{0:T(128)}, u32[]{:S(2)}) copy-start(f32[128]{0:T(128)} %param.14) | copy-start | bytes 1540
  28.1 17.8 %copy-start.6 = (f32[128]{0:T(128)S(1)}, f32[128]{0:T(128)}, u32[]{:S(2)}) copy-start(f32[128]{0:T(128)} %param.13) | copy-start | bytes 1540
  28.1 17.8 %copy-start.7 = (f32[128]{0:T(128)S(1)}, f32[128]{0:T(128)}, u32[]{:S(2)}) copy-start(f32[128]{0:T(128)} %param.12) | copy-start | bytes 1540
  87.7 3.8 %copy-start = (bf16[1024,128]{1,0:T(8,128)(2,1)S(1)}, bf16[1024,128]{1,0:T(8,128)(2,1)}, u32[]{:S(2)}) copy-start(bf16[1024,128]{1,0:T(8,128)(2,1)} %loadings.1) | copy-start | bytes 786436
  87.7 3.8 %copy-start.1 = (s32[16,1024]{1,0:T(8,128)S(1)}, s32[16,1024]{1,0:T(8,128)}, u32[]{:S(2)}) copy-start(s32[16,1024]{1,0:T(8,128)} %present.1) | copy-start | bytes 196612
  87.7 3.8 %copy-start.2 = (bf16[16,1024]{1,0:T(8,128)(2,1)S(1)}, bf16[16,1024]{1,0:T(8,128)(2,1)}, u32[]{:S(2)}) copy-start(bf16[16,1024]{1,0:T(8,128)(2,1)} %readings.1) | copy-start | bytes 98308
  87.7 3.8 %copy-start.3 = (f32[1024]{0:T(1024)S(1)}, f32[1024]{0:T(1024)}, u32[]{:S(2)}) copy-start(f32[1024]{0:T(1024)} %param.11) | copy-start | bytes 12292
  87.7 3.8 %copy-start.5 = (s32[1024]{0:T(1024)S(1)}, s32[1024]{0:T(1024)}, u32[]{:S(2)}) copy-start(s32[1024]{0:T(1024)} %param.15) | copy-start | bytes 12292

commit v5 on v4

--- a/solution.py
+++ b/solution.py
@@ -9,7 +9,8 @@
 BINS = 20
 GROUPS = 16
 SERIES = ("y", "c")
-TM = ("z", "x")
+NEAR = ("zl", "x")
+TM = ("zh", *NEAR)
 F32 = jnp.float32
 BF16 = jnp.bfloat16
 VM = pl.BlockSpec(memory_space=pltpu.VMEM)
@@ -72,12 +73,7 @@
     copies[0].wait()
     copies[1].wait()
     load = loadings[...]
-    turned = jnp.transpose(load.astype(F32))
-    scaled_wide = turned * noise[...]
-    scaled = scaled_wide.astype(BF16)
-    turned = turned.astype(BF16)
-    columns = jnp.concatenate([load, jnp.transpose(scaled.astype(F32)).astype(BF16)], axis=0)
-    lines = jnp.concatenate([scaled, turned], axis=1)
+    scaled = (jnp.transpose(load.astype(F32)) * noise[...]).astype(BF16)
     copies[2].wait()
     seen[...] = present[...].astype(F32)
     copies[3].wait()
@@ -88,7 +84,7 @@
         first = (core if slot == 0 else 1 - core) * count
         for i in range(count):
             observed = seen[pl.ds(first + i, 1), :].astype(BF16)
-            inform = 0.5 * bdot(lines * jnp.concatenate([observed, observed], axis=1), columns)
+            inform = bdot(scaled * observed, load)
             folded = pltpu.roll(inform[half:], half, 1)
             out[i, :half] = jnp.where(lane >= row, inform[:half], folded)
             diagonal = jnp.sum(jnp.where(row_k == lane_k, inform, 0.0), axis=0, keepdims=True)
@@ -137,13 +133,15 @@
     half_total[...] = jnp.where(lax.axis_index("c") == 0, total[0], total[1])
 
 
-def four_kernel(blocks, smooth_rate, half_total):
+def near_kernel(low, high, smooth_rate, half_total):
     rate = smooth_rate[...]
-    short, long = jnp.exp(-16.0 * rate), jnp.exp(-32.0 * rate)
-    one = joined((blocks[0, 0], blocks[1, 0]), (blocks[0, 1], blocks[1, 1]), short)
-    two = joined((blocks[0, 2], blocks[1, 2]), (blocks[0, 3], blocks[1, 3]), short)
-    total = joined(one, two, long)
-    half_total[...] = jnp.where(lax.axis_index("c") == 0, total[0], total[1])
+    nodes = [(part[0, i], part[1, i]) for part in (low, high) for i in range(part.shape[1])]
+    hours = 16.0
+    while len(nodes) > 1:
+        fade = jnp.exp(-hours * rate)
+        nodes = [joined(nodes[i], nodes[i + 1], fade) for i in range(0, len(nodes), 2)]
+        hours = 2.0 * hours
+    half_total[...] = jnp.where(lax.axis_index("c") == 0, nodes[0][0], nodes[0][1])
 
 
 def applied(current, one):
@@ -157,10 +155,6 @@
     gives = []
     for i, (maps, given) in enumerate(nodes):
         found = jnp.where(i == own, current, found)
-        if maps.shape[0] < k:
-            gives.append(None)
-            current = current + maps[:1]
-            continue
         product = dot3(current, jnp.concatenate([maps[:k], given[:k]], axis=1))
         gives.append(product[:1, k:] + given[k : k + 1])
         current = product[:, :k] + maps[k : k + 1]
@@ -171,30 +165,26 @@
     found = following = after
     for i in reversed(range(len(gives))):
         found = jnp.where(i == own, following, found)
-        if gives[i] is not None:
-            following = gives[i] + fade * following
+        following = gives[i] + fade * following
     return found
 
 
 def final_kernel(
-    planes, blocks, leaves, pairs, quads, eighths, factor_rate, smooth_rate,
+    planes, low, high, leaves, pairs, quads, eighths, factor_rate, smooth_rate,
     readings, present, loadings, noise, regions, scale, smoothed, out,
 ):
     hours, _, k = leaves.shape
-    z, x = lax.axis_index("z"), lax.axis_index("x")
+    far, near = lax.axis_index("zh"), lax.axis_index(NEAR)
     decays = jnp.exp(-factor_rate[...])
     rate = smooth_rate[...]
     retain = jnp.exp(-rate)
-    tall = blocks.shape[2]
-    plane_nodes = [(planes[0, : tall - k], planes[1, : tall - k])]
-    for at in range(tall - k, planes.shape[1], tall):
-        plane_nodes.append((planes[0, at : at + tall], planes[1, at : at + tall]))
-    start, final, plane_gives = walked(plane_nodes, jnp.zeros((8, k), F32), z)
-    span = hours * blocks.shape[1]
-    behind_plane = followed(plane_gives, decays * final[:1], z, jnp.exp(-span * rate))
-    block_nodes = [(blocks[0, i], blocks[1, i]) for i in range(blocks.shape[1])]
-    start, _, block_gives = walked(block_nodes, start, x)
-    following = followed(block_gives, behind_plane, x, jnp.exp(-hours * rate))
+    plane_nodes = [(planes[0, i], planes[1, i]) for i in range(planes.shape[1])]
+    block_nodes = [(part[0, i], part[1, i]) for part in (low, high) for i in range(part.shape[1])]
+    start, final, plane_gives = walked(plane_nodes, jnp.zeros((8, k), F32), far)
+    span = hours * len(block_nodes)
+    behind_plane = followed(plane_gives, decays * final[:1], far, jnp.exp(-span * rate))
+    start, _, block_gives = walked(block_nodes, start, near)
+    following = followed(block_gives, behind_plane, near, jnp.exp(-hours * rate))
     after = {-1: start}
     after[7] = applied(start, eighths[0])
     after[3] = applied(start, quads[0])
@@ -220,9 +210,8 @@
     table = jnp.concatenate(rows, axis=0)
     slot, _ = iotas(128, probab.shape[1])
     member = (lax.rem(slot, GROUPS) == regions[...]).astype(F32).astype(BF16)
-    high, low = halves(table)
-    lowest = (table - high.astype(F32) - low.astype(F32)).astype(BF16)
-    wide = across(high, member) + (across(low, member) + across(lowest, member))
+    wide = across(jnp.concatenate(halves(table), axis=0), member)
+    wide = wide[:24] + wide[24:]
     brow, blane = iotas(24, 128)
     kept = jnp.where(lax.div(blane, GROUPS) == lax.rem(brow, 8), wide, 0.0) * scale[0]
     out[...] = jnp.concatenate(
@@ -232,17 +221,15 @@
 
 def tail_kernel(parts, out):
     total = jnp.sum(parts[...], axis=0)
-    slots = 128 // GROUPS
     group, lane = iotas(GROUPS, 128)
     slot, column = iotas(128, 128)
-    found = jnp.zeros((GROUPS, 128), F32)
-    for r in range(3):
-        spread = jnp.where(lax.rem(lane, GROUPS) == group, total[r : r + 1], 0.0)
-        chosen = (lax.div(slot, GROUPS) + slots * r == column).astype(F32).astype(BF16)
-        high, low = halves(spread)
-        lowest = (spread - high.astype(F32) - low.astype(F32)).astype(BF16)
-        found = found + (bdot(high, chosen) + (bdot(low, chosen) + bdot(lowest, chosen)))
-    out[...] = found[:, :BINS]
+    spread = jnp.concatenate(
+        [jnp.where(lax.rem(lane, GROUPS) == group, total[r : r + 1], 0.0) for r in range(3)], axis=1
+    )
+    first = lax.div(slot, GROUPS)
+    chosen = jnp.concatenate([(first + 8 * r == column).astype(F32) for r in range(3)], axis=0)
+    found = bdot(jnp.concatenate(halves(spread), axis=0), chosen.astype(BF16))
+    out[...] = (found[:GROUPS] + found[GROUPS:])[:, :BINS]
 
 
 def sent_to_all(shard, axis):
@@ -265,7 +252,7 @@
     noise = noise_precision.reshape(1, series)
     gain, factor, smooth = (a.reshape(1, k) for a in (update_gain, factor_rate, smooth_rate))
     core = lax.axis_index("c")
-    nz, nx, ny, cores = (lax.axis_size(a) for a in ("z", "x", "y", "c"))
+    blocks, ny, cores = (lax.axis_size(a) for a in (TM, "y", "c"))
     share = hours // cores
 
     kept, sent = pl.pallas_call(
@@ -300,31 +287,32 @@
         compiler_params=PARAMS,
         name="block",
     )(packed, gain, factor, smooth)
-    blocks = lax.all_gather(sent_to_all(half_total, "x"), "c")
+    parts = sent_to_all(half_total, NEAR)
+    middle = parts.shape[0] // 2
+    parts = [lax.all_gather(part, "c") for part in (parts[:middle], parts[middle:])]
 
     half_total = pl.pallas_call(
-        four_kernel,
+        near_kernel,
         out_shape=shape_of(tall, k),
-        in_specs=[VM] * 2,
+        in_specs=[VM] * 3,
         out_specs=VM,
         compiler_params=PARAMS,
-        name="four",
-    )(blocks, smooth)
-    half_planes = sent_to_all(half_total, "z").reshape(nz * tall, k)
-    planes = lax.all_gather(half_planes[k:], "c")
-
-    hours_all = hours * nz * nx
+        name="near",
+    )(*parts, smooth)
+    planes = lax.all_gather(sent_to_all(half_total, "zh"), "c")
+
+    hours_all = hours * blocks
     series_all = series * ny * cores
     scale = jnp.full((1,), BINS * GROUPS / (hours_all * series_all), F32)
     smoothed, local = pl.pallas_call(
         final_kernel,
         out_shape=[shape_of(hours, k), shape_of(3, 128)],
-        in_specs=[VM] * 13 + [SM],
+        in_specs=[VM] * 14 + [SM],
         out_specs=[VM] * 2,
         compiler_params=PARAMS,
         name="final",
     )(
-        planes, blocks, leaves, pairs, quads, eighths, factor, smooth,
+        planes, *parts, leaves, pairs, quads, eighths, factor, smooth,
         readings, present, loadings, noise, regions.reshape(1, series), scale,
     )
 
@@ -341,7 +329,7 @@
 
 
 def solution(mesh):
-    split = Mesh(mesh.devices.reshape(8, 4, 8, 2), ("z", "x", "y", "c"))
+    split = Mesh(mesh.devices.reshape(4, 2, 4, 8, 2), (*TM, *SERIES))
     in_specs = (P(TM, SERIES), P(TM, SERIES), P(SERIES, None), P(SERIES), P(), P(), P(), P(SERIES))
     out_specs = (P(TM, None), P())
     return jax.shard_map(body, mesh=split, in_specs=in_specs, out_specs=out_specs, check_vma=False)

time: 118 us -> 117 us (level)
    all_to_all x5, blocking collectives: 71.7 us -> 68.6 us  [sent_to_all(): lax.all_to_all(jnp.broadcast_to(shard[None], (count, *shard.shape)), axis...]
    all_gather x2 -> x3, blocking collectives: 6.88 us -> 9.88 us  [the longest x2 5.64 us: body(): lax.all_gather(part, 'c')]
where the time goes in v5:
time: 117 us; the launch traced here: 116 us
  blocking collectives  107 us (91%)
  Pallas kernels  8.83 us (8%)
    all_to_all x5, blocking collectives, sent_to_all(): lax.all_to_all(jnp.broadcast_to(shard[None], (count, *shard.shape)), axis...  68.6 us
    all_to_all x1, blocking collectives, body(): packed = lax.all_to_all(kept + arrived, 'y', 0, 0, tiled=True).sum(axis=0)  15 us
    all_gather x1, blocking collectives, body(): lax.all_gather(sent, 'c')  8.73 us
    all_gather x2, blocking collectives, body(): lax.all_gather(part, 'c')  5.64 us
    all_gather x1, blocking collectives, body(): packed = lax.all_gather(packed, 'c').reshape(hours, height, k)  4.33 us
    all_gather x1, blocking collectives, body(): planes = lax.all_gather(sent_to_all(half_total, 'zh'), 'c')  4.23 us
    pallas_call x1, Pallas kernels, body(): pl.pallas_call(final_kernel, out_shape=[shape_of(hours, k), shape_of(3, 1...  2.91 us
    pallas_call x1, Pallas kernels, body(): pl.pallas_call(information_kernel, out_shape=[shape_of(share, height, k)]...  2.51 us

profile of v5, /device:TPU:1, one launch (start us, length us, event | category | flops | bytes accessed | tf_op | source)
XLA Modules:
  0.0 116.5 jit_solution(15149474609482319612)
XLA Ops:
  0.6 2.5 %information.1 = (f32[8,72,128]{2,1,0:T(8,128)S(1)}, f32[8,72,128]{2,1,0:T(8,128)S(1)}) custom-call(bf16[16,1024]{1,0:T(8,128)(2,1)} %readings.1, s32[16,1024]{1,0:T(8,128)} %present.1, bf16[1024,128]{1,0:T(8,128)(2,1)} %loadings.1, f32[1,1024]{1,0:T(1,128)} %bitcast.16), custom_call_target="tpu_custom_call" | custom-call | tf_op jit(solution)/shard_map/information/pallas_call | solution.py:258
  3.1 8.7 %all-gather = f32[16,72,128]{2,1,0:T(8,128)S(1)} all-gather(f32[8,72,128]{2,1,0:T(8,128)S(1)} %get-tuple-element.12), channel_id=2, replica_groups=mesh['zh'=4,'zl'=2,'x'=4,'y'=8,'c'=2] {'c'}, dimensions={0}, use_global_device_ids=true | all-gather | bytes 884736 | tf_op jit(solution)/shard_map/all_gather | solution.py:275
  11.9 15.0 %all_to_all.30 = f32[8,72,128]{2,1,0:T(8,128)S(1)} all-to-all(f32[8,72,128]{2,1,0:T(8,128)S(1)} %bitcast_add_fusion), channel_id=1, replica_groups=mesh['zh'=4,'zl'=2,'x'=4,'y'=8,'c'=2] {'y'}, dimensions={0} | all-to-all | bytes 589824 | tf_op jit(solution)/shard_map/all_to_all | solution.py:276
  27.0 0.0 copy-start.4
  27.0 0.0 copy-start.6
  27.0 0.0 copy-start.7
  27.0 13.4 %all_to_all.31 = f32[8,72,128]{2,1,0:T(8,128)S(1)} all-to-all(f32[8,72,128]{2,1,0:T(8,128)S(1)} %broadcast_in_dim.10), channel_id=1, replica_groups=mesh['zh'=4,'zl'=2,'x'=4,'y'=8,'c'=2] {'y'}, dimensions={0} | all-to-all | bytes 589824 | tf_op jit(solution)/shard_map/all_to_all | solution.py:237
  40.4 4.3 %all-gather.1.packed = f32[16,72,128]{2,1,0:T(8,128)S(1)} all-gather(f32[8,72,128]{2,1,0:T(8,128)S(1)} %all_to_all.31), channel_id=3, replica_groups=mesh['zh'=4,'zl'=2,'x'=4,'y'=8,'c'=2] {'c'}, dimensions={0}, use_global_device_ids=true | all-gather | bytes 884736 | tf_op jit(solution)/shard_map/all_gather | solution.py:278
  44.8 0.0 copy-done.4
  44.8 0.0 copy-done.6
  44.8 0.0 copy-done.7
  44.8 1.8 %block.1 = (f32[16,136,128]{2,1,0:T(8,128)S(1)}, f32[8,136,128]{2,1,0:T(8,128)S(1)}, f32[4,136,128]{2,1,0:T(8,128)S(1)}, f32[2,136,128]{2,1,0:T(8,128)S(1)}, f32[136,128]{1,0:T(8,128)S(1)}) custom-call(f32[16,72,128]{2,1,0:T(8,128)S(1)} %all-gather.1.packed, f32[1,128]{1,0:T(1,128)S(1)} %bitcast.24, f32[1,128]{1,0:T(1,128)S(1)} %bitcast.22, ...), custom_call_target="tpu_custom_call" | custom-call | tf_op jit(solution)/shard_map/block/pallas_call | solution.py:281
  46.6 14.0 %all_to_all.32 = f32[8,136,128]{2,1,0:T(8,128)S(1)} all-to-all(f32[8,136,128]{2,1,0:T(8,128)S(1)} %broadcast_in_dim.11), channel_id=1, replica_groups=mesh['zh'=4,'zl'=2,'x'=4,'y'=8,'c'=2] {'zl','x'}, dimensions={0} | all-to-all | bytes 1114112 | tf_op jit(solution)/shard_map/all_to_all | solution.py:237
  60.7 3.4 %all-gather.3 = f32[8,136,128]{2,1,0:T(8,128)S(1)} all-gather(f32[4,136,128]{2,1,0:T(8,128)S(1)} %get-tuple-element.20), channel_id=5, replica_groups=mesh['zh'=4,'zl'=2,'x'=4,'y'=8,'c'=2] {'c'}, dimensions={0}, use_global_device_ids=true | all-gather | bytes 835584 | tf_op jit(solution)/shard_map/all_gather | solution.py:292
  64.1 2.2 %all-gather.2 = f32[8,136,128]{2,1,0:T(8,128)S(1)} all-gather(f32[4,136,128]{2,1,0:T(8,128)S(1)} %get-tuple-element.21), channel_id=4, replica_groups=mesh['zh'=4,'zl'=2,'x'=4,'y'=8,'c'=2] {'c'}, dimensions={0}, use_global_device_ids=true | all-gather | bytes 835584 | tf_op jit(solution)/shard_map/all_gather | solution.py:292
  66.3 0.8 near.1
  67.2 0.0 copy-start
  67.2 0.0 copy-start.1
  67.2 0.0 copy-start.2
  67.2 0.0 copy-start.3
  67.2 0.0 copy-start.5
  67.2 19.0 %all_to_all.33 = f32[4,136,128]{2,1,0:T(8,128)S(1)} all-to-all(f32[4,136,128]{2,1,0:T(8,128)S(1)} %broadcast_in_dim.12), channel_id=1, replica_groups=mesh['zh'=4,'zl'=2,'x'=4,'y'=8,'c'=2] {'zh'}, dimensions={0} | all-to-all | bytes 557056 | tf_op jit(solution)/shard_map/all_to_all | solution.py:237
  86.3 4.2 %all-gather.4 = f32[8,136,128]{2,1,0:T(8,128)S(1)} all-gather(f32[4,136,128]{2,1,0:T(8,128)S(1)} %all_to_all.33), channel_id=6, replica_groups=mesh['zh'=4,'zl'=2,'x'=4,'y'=8,'c'=2] {'c'}, dimensions={0}, use_global_device_ids=true | all-gather | bytes 835584 | tf_op jit(solution)/shard_map/all_gather | solution.py:302
  90.5 0.0 copy-done
  90.5 0.0 copy-done.1
  90.5 0.0 copy-done.2
  90.5 0.0 copy-done.3
  90.5 0.0 copy-done.5
  90.5 2.9 %final.1 = (f32[16,128]{1,0:T(8,128)}, f32[3,128]{1,0:T(4,128)S(1)}) custom-call(f32[2,4,136,128]{3,2,1,0:T(8,128)S(1)} %bitcast.15, f32[2,4,136,128]{3,2,1,0:T(8,128)S(1)} %bitcast.14, f32[2,4,136,128]{3,2,1,0:T(8,128)S(1)} %bitcast.12, f32[16,136,128]{2,1,0:T(8,128)S(1)} %get-tuple-element.14.leaves, f32[8,136,128]{2,1,0:T(8,128)S(1)} %get-tuple-element.15.pairs, ...), custom_call_target="tpu_custom_call" | custom-call | tf_op jit(solution)/shard_map/final/pallas_call | solution.py:307
  93.4 10.2 %all_to_all.34 = f32[16,3,128]{2,1,0:T(4,128)S(1)} all-to-all(f32[16,3,128]{2,1,0:T(4,128)S(1)} %broadcast_in_dim.13), channel_id=1, replica_groups=mesh['zh'=4,'zl'=2,'x'=4,'y'=8,'c'=2] {'y','c'}, dimensions={0} | all-to-all | bytes 49152 | tf_op jit(solution)/shard_map/all_to_all | solution.py:237
  103.7 12.0 %all_to_all.35.parts = f32[32,3,128]{2,1,0:T(4,128)S(1)} all-to-all(f32[32,3,128]{2,1,0:T(4,128)S(1)} %broadcast_in_dim.14), channel_id=1, replica_groups=mesh['zh'=4,'zl'=2,'x'=4,'y'=8,'c'=2] {'zh','zl','x'}, dimensions={0} | all-to-all | bytes 98304 | tf_op jit(solution)/shard_map/all_to_all | solution.py:237
  115.7 0.8 tail.1
  (9 shorter events, 0.2 us)
Async XLA Ops:
  27.0 17.8 %copy-start.4 = (f32[128]{0:T(128)S(1)}, f32[128]{0:T(128)}, u32[]{:S(2)}) copy-start(f32[128]{0:T(128)} %param.14) | copy-start | bytes 1540
  27.0 17.8 %copy-start.6 = (f32[128]{0:T(128)S(1)}, f32[128]{0:T(128)}, u32[]{:S(2)}) copy-start(f32[128]{0:T(128)} %param.13) | copy-start | bytes 1540
  27.0 17.8 %copy-start.7 = (f32[128]{0:T(128)S(1)}, f32[128]{0:T(128)}, u32[]{:S(2)}) copy-start(f32[128]{0:T(128)} %param.12) | copy-start | bytes 1540
  67.2 23.4 %copy-start = (bf16[1024,128]{1,0:T(8,128)(2,1)S(1)}, bf16[1024,128]{1,0:T(8,128)(2,1)}, u32[]{:S(2)}) copy-start(bf16[1024,128]{1,0:T(8,128)(2,1)} %loadings.1) | copy-start | bytes 786436
  67.2 23.3 %copy-start.1 = (s32[16,1024]{1,0:T(8,128)S(1)}, s32[16,1024]{1,0:T(8,128)}, u32[]{:S(2)}) copy-start(s32[16,1024]{1,0:T(8,128)} %present.1) | copy-start | bytes 196612
  67.2 23.3 %copy-start.2 = (bf16[16,1024]{1,0:T(8,128)(2,1)S(1)}, bf16[16,1024]{1,0:T(8,128)(2,1)}, u32[]{:S(2)}) copy-start(bf16[16,1024]{1,0:T(8,128)(2,1)} %readings.1) | copy-start | bytes 98308
  67.2 23.3 %copy-start.3 = (f32[1024]{0:T(1024)S(1)}, f32[1024]{0:T(1024)}, u32[]{:S(2)}) copy-start(f32[1024]{0:T(1024)} %param.11) | copy-start | bytes 12292
  67.2 23.3 %copy-start.5 = (s32[1024]{0:T(1024)S(1)}, s32[1024]{0:T(1024)}, u32[]{:S(2)}) copy-start(s32[1024]{0:T(1024)} %param.15) | copy-start | bytes 12292

commit v6 on v5

--- a/solution.py
+++ b/solution.py
@@ -94,7 +94,7 @@
 
 
 def block_kernel(
-    packed, gain, factor_rate, smooth_rate, leaves, pairs, quads, eighths, half_total,
+    packed, gain, factor_rate, smooth_rate, leaves, pairs, quads, eighths, sent,
     given1, given2, given4, given8,
 ):
     hours = packed.shape[0]
@@ -130,16 +130,33 @@
             )
         below, given = above, gives
     total = joined((below[0], given[0]), (below[1], given[1]), jnp.exp(-8.0 * rate))
-    half_total[...] = jnp.where(lax.axis_index("c") == 0, total[0], total[1])
-
-
-def near_kernel(low, high, smooth_rate, half_total):
+    rows = jnp.concatenate([total[0][k : k + 1], total[1][k : k + 1], jnp.zeros((6, k), F32)], axis=0)
+    first = lax.axis_index("c") == 0
+    sent[:k] = jnp.where(first, total[0][:k], total[1][:k])
+    sent[k : k + 8] = rows
+    sent[k + 8 :] = jnp.where(first, total[1][k - 8 : k], total[0][k - 8 : k])
+
+
+def block_node(parts, sides, i):
+    k = parts.shape[2]
+    first = lax.axis_index("c") == 0
+    own, other, rows = parts[i, k - 8 : k], parts[i, k + 8 :], parts[i, k : k + 8]
+    none = jnp.zeros((7, k), F32)
+    maps = [sides[0, i], jnp.where(first, own, other), rows[:1], none]
+    given = [sides[1, i], jnp.where(first, other, own), rows[1:2], none]
+    return jnp.concatenate(maps, axis=0), jnp.concatenate(given, axis=0)
+
+
+def near_kernel(parts, sides, smooth_rate, twos, fours, half_total):
     rate = smooth_rate[...]
-    nodes = [(part[0, i], part[1, i]) for part in (low, high) for i in range(part.shape[1])]
+    nodes = [block_node(parts, sides, i) for i in range(parts.shape[0])]
     hours = 16.0
-    while len(nodes) > 1:
+    for kept in (twos, fours, None):
         fade = jnp.exp(-hours * rate)
         nodes = [joined(nodes[i], nodes[i + 1], fade) for i in range(0, len(nodes), 2)]
+        if kept is not None:
+            for i, node in enumerate(nodes):
+                kept[0, i], kept[1, i] = node
         hours = 2.0 * hours
     half_total[...] = jnp.where(lax.axis_index("c") == 0, nodes[0][0], nodes[0][1])
 
@@ -149,15 +166,20 @@
     return dot3(current, one[:k]) + one[k : k + 1]
 
 
+def stepped(current, node):
+    maps, given = node
+    k = current.shape[1]
+    product = dot3(current, jnp.concatenate([maps[:k], given[:k]], axis=1))
+    return product[:, :k] + maps[k : k + 1], product[:1, k:] + given[k : k + 1]
+
+
 def walked(nodes, current, own):
-    k = current.shape[1]
     found = current
     gives = []
-    for i, (maps, given) in enumerate(nodes):
+    for i, node in enumerate(nodes):
         found = jnp.where(i == own, current, found)
-        product = dot3(current, jnp.concatenate([maps[:k], given[:k]], axis=1))
-        gives.append(product[:1, k:] + given[k : k + 1])
-        current = product[:, :k] + maps[k : k + 1]
+        current, give = stepped(current, node)
+        gives.append(give)
     return found, current, gives
 
 
@@ -169,8 +191,15 @@
     return found
 
 
+def narrowed(current, following, left, right, goes_right, fade):
+    middle = applied(current, left)
+    _, give = stepped(middle, right)
+    before = jnp.where(goes_right, middle, current)
+    return before, jnp.where(goes_right, following, give + fade * following)
+
+
 def final_kernel(
-    planes, low, high, leaves, pairs, quads, eighths, factor_rate, smooth_rate,
+    planes, fours, twos, parts, sides, leaves, pairs, quads, eighths, factor_rate, smooth_rate,
     readings, present, loadings, noise, regions, scale, smoothed, out,
 ):
     hours, _, k = leaves.shape
@@ -179,12 +208,21 @@
     rate = smooth_rate[...]
     retain = jnp.exp(-rate)
     plane_nodes = [(planes[0, i], planes[1, i]) for i in range(planes.shape[1])]
-    block_nodes = [(part[0, i], part[1, i]) for part in (low, high) for i in range(part.shape[1])]
     start, final, plane_gives = walked(plane_nodes, jnp.zeros((8, k), F32), far)
-    span = hours * len(block_nodes)
-    behind_plane = followed(plane_gives, decays * final[:1], far, jnp.exp(-span * rate))
-    start, _, block_gives = walked(block_nodes, start, near)
-    following = followed(block_gives, behind_plane, near, jnp.exp(-hours * rate))
+    count = parts.shape[0]
+    following = followed(
+        plane_gives, decays * final[:1], far, jnp.exp(-float(count * hours) * rate)
+    )
+    for part, size in ((fours, 4), (twos, 2), (None, 1)):
+        slot = lax.div(near, size)
+        first = slot - lax.rem(slot, 2)
+        if part is None:
+            left, right = (block_node(parts, sides, first + i) for i in (0, 1))
+        else:
+            left, right = ((part[0, first + i], part[1, first + i]) for i in (0, 1))
+        start, following = narrowed(
+            start, following, left[0], right, first < slot, jnp.exp(-float(size * hours) * rate)
+        )
     after = {-1: start}
     after[7] = applied(start, eighths[0])
     after[3] = applied(start, quads[0])
@@ -278,27 +316,31 @@
     packed = lax.all_gather(packed, "c").reshape(hours, height, k)
 
     nodes = [shape_of(hours // n, tall, k) for n in (1, 2, 4, 8)]
-    leaves, pairs, quads, eighths, half_total = pl.pallas_call(
+    leaves, pairs, quads, eighths, sent = pl.pallas_call(
         block_kernel,
-        out_shape=nodes + [shape_of(tall, k)],
+        out_shape=nodes + [shape_of(tall + 8, k)],
         in_specs=[VM] * 4,
         out_specs=[VM] * 5,
         scratch_shapes=[pltpu.VMEM((hours // n, tall, k), F32) for n in (1, 2, 4, 8)],
         compiler_params=PARAMS,
         name="block",
     )(packed, gain, factor, smooth)
-    parts = sent_to_all(half_total, NEAR)
-    middle = parts.shape[0] // 2
-    parts = [lax.all_gather(part, "c") for part in (parts[:middle], parts[middle:])]
-
-    half_total = pl.pallas_call(
+    parts = sent_to_all(sent, NEAR)
+    count = parts.shape[0]
+    sides = lax.all_gather(parts[:, : k - 8], "c")
+
+    twos, fours, half_total = pl.pallas_call(
         near_kernel,
-        out_shape=shape_of(tall, k),
+        out_shape=[
+            shape_of(2, count // 2, tall, k),
+            shape_of(2, count // 4, tall, k),
+            shape_of(tall, k),
+        ],
         in_specs=[VM] * 3,
-        out_specs=VM,
+        out_specs=[VM] * 3,
         compiler_params=PARAMS,
         name="near",
-    )(*parts, smooth)
+    )(parts, sides, smooth)
     planes = lax.all_gather(sent_to_all(half_total, "zh"), "c")
 
     hours_all = hours * blocks
@@ -307,12 +349,12 @@
     smoothed, local = pl.pallas_call(
         final_kernel,
         out_shape=[shape_of(hours, k), shape_of(3, 128)],
-        in_specs=[VM] * 14 + [SM],
+        in_specs=[VM] * 16 + [SM],
         out_specs=[VM] * 2,
         compiler_params=PARAMS,
         name="final",
     )(
-        planes, *parts, leaves, pairs, quads, eighths, factor, smooth,
+        planes, fours, twos, parts, sides, leaves, pairs, quads, eighths, factor, smooth,
         readings, present, loadings, noise, regions.reshape(1, series), scale,
     )
 

time: 117 us -> 115 us (0.983)
  blocking collectives: 107 us -> 105 us
    all_gather x2 -> x1, blocking collectives: 5.64 us -> 3.84 us  [body(): sides = lax.all_gather(parts[:, :k - 8], 'c')]
where the time goes in v6:
time: 115 us; the launch traced here: 114 us
  blocking collectives  105 us (91%)
  Pallas kernels  8.38 us (7%)
    all_to_all x5, blocking collectives, sent_to_all(): lax.all_to_all(jnp.broadcast_to(shard[None], (count, *shard.shape)), axis...  68.8 us
    all_to_all x1, blocking collectives, body(): packed = lax.all_to_all(kept + arrived, 'y', 0, 0, tiled=True).sum(axis=0)  15 us
    all_gather x1, blocking collectives, body(): lax.all_gather(sent, 'c')  8.73 us
    all_gather x1, blocking collectives, body(): packed = lax.all_gather(packed, 'c').reshape(hours, height, k)  4.33 us
    all_gather x1, blocking collectives, body(): planes = lax.all_gather(sent_to_all(half_total, 'zh'), 'c')  4.23 us
    all_gather x1, blocking collectives, body(): sides = lax.all_gather(parts[:, :k - 8], 'c')  3.84 us
    pallas_call x1, Pallas kernels, body(): pl.pallas_call(information_kernel, out_shape=[shape_of(share, height, k)]...  2.51 us
    pallas_call x1, Pallas kernels, body(): pl.pallas_call(final_kernel, out_shape=[shape_of(hours, k), shape_of(3, 1...  2.45 us

profile of v6, /device:TPU:1, one launch (start us, length us, event | category | flops | bytes accessed | tf_op | source)
XLA Modules:
  0.0 114.4 jit_solution(6440516415085945438)
XLA Ops:
  0.6 2.5 %information.1 = (f32[8,72,128]{2,1,0:T(8,128)S(1)}, f32[8,72,128]{2,1,0:T(8,128)S(1)}) custom-call(bf16[16,1024]{1,0:T(8,128)(2,1)} %readings.1, s32[16,1024]{1,0:T(8,128)} %present.1, bf16[1024,128]{1,0:T(8,128)(2,1)} %loadings.1, f32[1,1024]{1,0:T(1,128)} %bitcast.13), custom_call_target="tpu_custom_call" | custom-call | tf_op jit(solution)/shard_map/information/pallas_call | solution.py:296
  3.1 8.7 %all-gather = f32[16,72,128]{2,1,0:T(8,128)S(1)} all-gather(f32[8,72,128]{2,1,0:T(8,128)S(1)} %get-tuple-element.15), channel_id=2, replica_groups=mesh['zh'=4,'zl'=2,'x'=4,'y'=8,'c'=2] {'c'}, dimensions={0}, use_global_device_ids=true | all-gather | bytes 884736 | tf_op jit(solution)/shard_map/all_gather | solution.py:313
  11.9 15.0 %all_to_all.30 = f32[8,72,128]{2,1,0:T(8,128)S(1)} all-to-all(f32[8,72,128]{2,1,0:T(8,128)S(1)} %bitcast_add_fusion), channel_id=1, replica_groups=mesh['zh'=4,'zl'=2,'x'=4,'y'=8,'c'=2] {'y'}, dimensions={0} | all-to-all | bytes 589824 | tf_op jit(solution)/shard_map/all_to_all | solution.py:314
  27.0 0.0 copy-start.4
  27.0 0.0 copy-start.6
  27.0 0.0 copy-start.7
  27.0 13.4 %all_to_all.31 = f32[8,72,128]{2,1,0:T(8,128)S(1)} all-to-all(f32[8,72,128]{2,1,0:T(8,128)S(1)} %broadcast_in_dim.10), channel_id=1, replica_groups=mesh['zh'=4,'zl'=2,'x'=4,'y'=8,'c'=2] {'y'}, dimensions={0} | all-to-all | bytes 589824 | tf_op jit(solution)/shard_map/all_to_all | solution.py:275
  40.4 4.3 %all-gather.1.packed = f32[16,72,128]{2,1,0:T(8,128)S(1)} all-gather(f32[8,72,128]{2,1,0:T(8,128)S(1)} %all_to_all.31), channel_id=3, replica_groups=mesh['zh'=4,'zl'=2,'x'=4,'y'=8,'c'=2] {'c'}, dimensions={0}, use_global_device_ids=true | all-gather | bytes 884736 | tf_op jit(solution)/shard_map/all_gather | solution.py:316
  44.8 0.0 copy-done.4
  44.8 0.0 copy-done.6
  44.8 0.0 copy-done.7
  44.8 1.8 %block.1 = (f32[16,136,128]{2,1,0:T(8,128)S(1)}, f32[8,136,128]{2,1,0:T(8,128)S(1)}, f32[4,136,128]{2,1,0:T(8,128)S(1)}, f32[2,136,128]{2,1,0:T(8,128)S(1)}, f32[144,128]{1,0:T(8,128)S(1)}) custom-call(f32[16,72,128]{2,1,0:T(8,128)S(1)} %all-gather.1.packed, f32[1,128]{1,0:T(1,128)S(1)} %bitcast.21, f32[1,128]{1,0:T(1,128)S(1)} %bitcast.19, ...), custom_call_target="tpu_custom_call" | custom-call | tf_op jit(solution)/shard_map/block/pallas_call | solution.py:319
  46.6 14.2 %all_to_all.32.parts = f32[8,144,128]{2,1,0:T(8,128)S(1)} all-to-all(f32[8,144,128]{2,1,0:T(8,128)S(1)} %broadcast_in_dim.11), channel_id=1, replica_groups=mesh['zh'=4,'zl'=2,'x'=4,'y'=8,'c'=2] {'zl','x'}, dimensions={0} | all-to-all | bytes 1179648 | tf_op jit(solution)/shard_map/all_to_all | solution.py:275
  60.9 3.8 %all-gather.2 = f32[16,120,128]{2,1,0:T(8,128)S(1)} all-gather(f32[8,120,128]{2,1,0:T(8,128)S(1)} %slice.4), channel_id=4, replica_groups=mesh['zh'=4,'zl'=2,'x'=4,'y'=8,'c'=2] {'c'}, dimensions={0}, use_global_device_ids=true | all-gather | bytes 1474560 | tf_op jit(solution)/shard_map/all_gather | solution.py:330
  64.7 0.8 near.1
  65.5 0.0 copy-start
  65.5 0.0 copy-start.1
  65.6 0.0 copy-start.2
  65.6 0.0 copy-start.3
  65.6 0.0 copy-start.5
  65.6 19.0 %all_to_all.33 = f32[4,136,128]{2,1,0:T(8,128)S(1)} all-to-all(f32[4,136,128]{2,1,0:T(8,128)S(1)} %broadcast_in_dim.12), channel_id=1, replica_groups=mesh['zh'=4,'zl'=2,'x'=4,'y'=8,'c'=2] {'zh'}, dimensions={0} | all-to-all | bytes 557056 | tf_op jit(solution)/shard_map/all_to_all | solution.py:275
  84.7 4.2 %all-gather.3 = f32[8,136,128]{2,1,0:T(8,128)S(1)} all-gather(f32[4,136,128]{2,1,0:T(8,128)S(1)} %all_to_all.33), channel_id=5, replica_groups=mesh['zh'=4,'zl'=2,'x'=4,'y'=8,'c'=2] {'c'}, dimensions={0}, use_global_device_ids=true | all-gather | bytes 835584 | tf_op jit(solution)/shard_map/all_gather | solution.py:344
  88.9 0.0 copy-done
  88.9 0.0 copy-done.1
  88.9 0.0 copy-done.2
  88.9 0.0 copy-done.3
  88.9 0.0 copy-done.5
  88.9 2.5 %final.1 = (f32[16,128]{1,0:T(8,128)}, f32[3,128]{1,0:T(4,128)S(1)}) custom-call(f32[2,4,136,128]{3,2,1,0:T(8,128)S(1)} %bitcast.12, f32[2,2,136,128]{3,2,1,0:T(8,128)S(1)} %get-tuple-element.18.fours, f32[2,4,136,128]{3,2,1,0:T(8,128)S(1)} %get-tuple-element.19.twos, f32[8,144,128]{2,1,0:T(8,128)S(1)} %all_to_all.32.parts, f32[2,8,120,128]{3,2,1,0:T(8,128)S(1)} %bitcast.11, ...), custom_call_target="tpu_custom_call" | custom-call | tf_op jit(solution)/shard_map/final/pallas_call | solution.py:349
  91.4 10.2 %all_to_all.34 = f32[16,3,128]{2,1,0:T(4,128)S(1)} all-to-all(f32[16,3,128]{2,1,0:T(4,128)S(1)} %broadcast_in_dim.13), channel_id=1, replica_groups=mesh['zh'=4,'zl'=2,'x'=4,'y'=8,'c'=2] {'y','c'}, dimensions={0} | all-to-all | bytes 49152 | tf_op jit(solution)/shard_map/all_to_all | solution.py:275
  101.6 12.0 %all_to_all.35.parts = f32[32,3,128]{2,1,0:T(4,128)S(1)} all-to-all(f32[32,3,128]{2,1,0:T(4,128)S(1)} %broadcast_in_dim.14), channel_id=1, replica_groups=mesh['zh'=4,'zl'=2,'x'=4,'y'=8,'c'=2] {'zh','zl','x'}, dimensions={0} | all-to-all | bytes 98304 | tf_op jit(solution)/shard_map/all_to_all | solution.py:275
  113.6 0.8 tail.1
  (9 shorter events, 0.2 us)
Async XLA Ops:
  27.0 17.8 %copy-start.4 = (f32[128]{0:T(128)S(1)}, f32[128]{0:T(128)}, u32[]{:S(2)}) copy-start(f32[128]{0:T(128)} %param.14) | copy-start | bytes 1540
  27.0 17.8 %copy-start.6 = (f32[128]{0:T(128)S(1)}, f32[128]{0:T(128)}, u32[]{:S(2)}) copy-start(f32[128]{0:T(128)} %param.13) | copy-start | bytes 1540
  27.0 17.8 %copy-start.7 = (f32[128]{0:T(128)S(1)}, f32[128]{0:T(128)}, u32[]{:S(2)}) copy-start(f32[128]{0:T(128)} %param.12) | copy-start | bytes 1540
  65.5 23.4 %copy-start = (bf16[1024,128]{1,0:T(8,128)(2,1)S(1)}, bf16[1024,128]{1,0:T(8,128)(2,1)}, u32[]{:S(2)}) copy-start(bf16[1024,128]{1,0:T(8,128)(2,1)} %loadings.1) | copy-start | bytes 786436
  65.5 23.3 %copy-start.1 = (s32[16,1024]{1,0:T(8,128)S(1)}, s32[16,1024]{1,0:T(8,128)}, u32[]{:S(2)}) copy-start(s32[16,1024]{1,0:T(8,128)} %present.1) | copy-start | bytes 196612
  65.6 23.3 %copy-start.2 = (bf16[16,1024]{1,0:T(8,128)(2,1)S(1)}, bf16[16,1024]{1,0:T(8,128)(2,1)}, u32[]{:S(2)}) copy-start(bf16[16,1024]{1,0:T(8,128)(2,1)} %readings.1) | copy-start | bytes 98308
  65.6 23.3 %copy-start.3 = (f32[1024]{0:T(1024)S(1)}, f32[1024]{0:T(1024)}, u32[]{:S(2)}) copy-start(f32[1024]{0:T(1024)} %param.11) | copy-start | bytes 12292
  65.6 23.3 %copy-start.5 = (s32[1024]{0:T(1024)S(1)}, s32[1024]{0:T(1024)}, u32[]{:S(2)}) copy-start(s32[1024]{0:T(1024)} %param.15) | copy-start | bytes 12292

commit v7 on v6

--- a/solution.py
+++ b/solution.py
@@ -88,8 +88,8 @@
             folded = pltpu.roll(inform[half:], half, 1)
             out[i, :half] = jnp.where(lane >= row, inform[:half], folded)
             diagonal = jnp.sum(jnp.where(row_k == lane_k, inform, 0.0), axis=0, keepdims=True)
-            out[i, half:] = jnp.concatenate(
-                [diagonal, scores[pl.ds(first + i, 1), :], jnp.zeros((6, k), F32)], axis=0
+            out[i, half : half + 2] = jnp.concatenate(
+                [diagonal, scores[pl.ds(first + i, 1), :]], axis=0
             )
 
 
@@ -130,17 +130,16 @@
             )
         below, given = above, gives
     total = joined((below[0], given[0]), (below[1], given[1]), jnp.exp(-8.0 * rate))
-    rows = jnp.concatenate([total[0][k : k + 1], total[1][k : k + 1], jnp.zeros((6, k), F32)], axis=0)
     first = lax.axis_index("c") == 0
     sent[:k] = jnp.where(first, total[0][:k], total[1][:k])
-    sent[k : k + 8] = rows
-    sent[k + 8 :] = jnp.where(first, total[1][k - 8 : k], total[0][k - 8 : k])
+    sent[k : k + 8] = jnp.where(first, total[1][k - 8 : k], total[0][k - 8 : k])
+    sent[k + 8 :] = jnp.concatenate([total[0][k : k + 1], total[1][k : k + 1]], axis=0)
 
 
 def block_node(parts, sides, i):
     k = parts.shape[2]
     first = lax.axis_index("c") == 0
-    own, other, rows = parts[i, k - 8 : k], parts[i, k + 8 :], parts[i, k : k + 8]
+    own, other, rows = parts[i, k - 8 : k], parts[i, k : k + 8], parts[i, k + 8 :]
     none = jnp.zeros((7, k), F32)
     maps = [sides[0, i], jnp.where(first, own, other), rows[:1], none]
     given = [sides[1, i], jnp.where(first, other, own), rows[1:2], none]
@@ -158,7 +157,7 @@
             for i, node in enumerate(nodes):
                 kept[0, i], kept[1, i] = node
         hours = 2.0 * hours
-    half_total[...] = jnp.where(lax.axis_index("c") == 0, nodes[0][0], nodes[0][1])
+    half_total[...] = jnp.where(lax.axis_index("c") == 0, *nodes[0])[: half_total.shape[0]]
 
 
 def applied(current, one):
@@ -286,7 +285,8 @@
 ):
     hours, series = readings.shape
     k = loadings.shape[1]
-    height, tall = k // 2 + 8, k + 8
+    height, tall = k // 2 + 2, k + 8
+    padded = -(-height // 8) * 8
     noise = noise_precision.reshape(1, series)
     gain, factor, smooth = (a.reshape(1, k) for a in (update_gain, factor_rate, smooth_rate))
     core = lax.axis_index("c")
@@ -295,7 +295,7 @@
 
     kept, sent = pl.pallas_call(
         information_kernel,
-        out_shape=[shape_of(share, height, k)] * 2,
+        out_shape=[shape_of(share, height, k), shape_of(share, padded, k)],
         in_specs=[HB] * 4,
         out_specs=[VM] * 2,
         scratch_shapes=[
@@ -311,14 +311,14 @@
         name="information",
     )(*(pltpu.with_memory_space_constraint(a, pltpu.HBM) for a in (readings, present, loadings, noise)))
     arrived = lax.dynamic_index_in_dim(lax.all_gather(sent, "c"), 1 - core, 0, keepdims=False)
-    packed = lax.all_to_all(kept + arrived, "y", 0, 0, tiled=True).sum(axis=0)
-    packed = sent_to_all(packed, "y")
-    packed = lax.all_gather(packed, "c").reshape(hours, height, k)
+    packed = lax.all_to_all(kept + arrived[:, :height], "y", 0, 0, tiled=True).sum(axis=0)
+    packed = jnp.pad(sent_to_all(packed, "y"), ((0, 0), (0, padded - height), (0, 0)))
+    packed = lax.all_gather(packed, "c").reshape(hours, padded, k)
 
     nodes = [shape_of(hours // n, tall, k) for n in (1, 2, 4, 8)]
     leaves, pairs, quads, eighths, sent = pl.pallas_call(
         block_kernel,
-        out_shape=nodes + [shape_of(tall + 8, k)],
+        out_shape=nodes + [shape_of(k + 10, k)],
         in_specs=[VM] * 4,
         out_specs=[VM] * 5,
         scratch_shapes=[pltpu.VMEM((hours // n, tall, k), F32) for n in (1, 2, 4, 8)],
@@ -334,7 +334,7 @@
         out_shape=[
             shape_of(2, count // 2, tall, k),
             shape_of(2, count // 4, tall, k),
-            shape_of(tall, k),
+            shape_of(k + 1, k),
         ],
         in_specs=[VM] * 3,
         out_specs=[VM] * 3,

time: 115 us -> 115 us (level)
  no operation moved by 1% of the time
where the time goes in v7:
time: 115 us
  blocking collectives  105 us (91%)
  Pallas kernels  8.39 us (7%)
    all_to_all x5, blocking collectives, sent_to_all(): lax.all_to_all(jnp.broadcast_to(shard[None], (count, *shard.shape)), axis...  68.9 us
    all_to_all x1, blocking collectives, body(): lax.all_to_all(kept + arrived[:, :height], 'y', 0, 0, tiled=True)  15 us
    all_gather x1, blocking collectives, body(): lax.all_gather(sent, 'c')  8.73 us
    all_gather x1, blocking collectives, body(): packed = lax.all_gather(packed, 'c').reshape(hours, padded, k)  4.34 us
    all_gather x1, blocking collectives, body(): planes = lax.all_gather(sent_to_all(half_total, 'zh'), 'c')  4.23 us
    all_gather x1, blocking collectives, body(): sides = lax.all_gather(parts[:, :k - 8], 'c')  3.84 us
    pallas_call x1, Pallas kernels, body(): pl.pallas_call(information_kernel, out_shape=[shape_of(share, height, k),...  2.51 us
    pallas_call x1, Pallas kernels, body(): pl.pallas_call(final_kernel, out_shape=[shape_of(hours, k), shape_of(3, 1...  2.45 us

profile of v7, /device:TPU:1, one launch (start us, length us, event | category | flops | bytes accessed | tf_op | source)
XLA Modules:
  0.0 114.6 jit_solution(6108094914316820417)
XLA Ops:
  0.6 2.5 %information.1 = (f32[8,66,128]{2,1,0:T(8,128)S(1)}, f32[8,72,128]{2,1,0:T(8,128)S(1)}) custom-call(bf16[16,1024]{1,0:T(8,128)(2,1)} %readings.1, s32[16,1024]{1,0:T(8,128)} %present.1, bf16[1024,128]{1,0:T(8,128)(2,1)} %loadings.1, f32[1,1024]{1,0:T(1,128)} %bitcast.13), custom_call_target="tpu_custom_call" | custom-call | tf_op jit(solution)/shard_map/information/pallas_call | solution.py:296
  3.1 8.7 %all-gather = f32[16,72,128]{2,1,0:T(8,128)S(1)} all-gather(f32[8,72,128]{2,1,0:T(8,128)S(1)} %get-tuple-element.15), channel_id=2, replica_groups=mesh['zh'=4,'zl'=2,'x'=4,'y'=8,'c'=2] {'c'}, dimensions={0}, use_global_device_ids=true | all-gather | bytes 884736 | tf_op jit(solution)/shard_map/all_gather | solution.py:313
  11.9 15.0 %all_to_all.30 = f32[8,66,128]{2,1,0:T(8,128)S(1)} all-to-all(f32[8,66,128]{2,1,0:T(8,128)S(1)} %slice_add_fusion), channel_id=1, replica_groups=mesh['zh'=4,'zl'=2,'x'=4,'y'=8,'c'=2] {'y'}, dimensions={0} | all-to-all | bytes 540672 | tf_op jit(solution)/shard_map/all_to_all | solution.py:314
  27.0 0.0 copy-start.4
  27.1 0.0 copy-start.6
  27.1 0.0 copy-start.7
  27.1 13.5 %all_to_all.31 = f32[8,66,128]{2,1,0:T(8,128)S(1)} all-to-all(f32[8,66,128]{2,1,0:T(8,128)S(1)} %broadcast_in_dim.10), channel_id=1, replica_groups=mesh['zh'=4,'zl'=2,'x'=4,'y'=8,'c'=2] {'y'}, dimensions={0} | all-to-all | bytes 540672 | tf_op jit(solution)/shard_map/all_to_all | solution.py:274
  40.6 4.3 %all-gather.1.packed = f32[16,72,128]{2,1,0:T(8,128)S(1)} all-gather(f32[8,72,128]{2,1,0:T(8,128)S(1)} %pad.4), channel_id=3, replica_groups=mesh['zh'=4,'zl'=2,'x'=4,'y'=8,'c'=2] {'c'}, dimensions={0}, use_global_device_ids=true | all-gather | bytes 884736 | tf_op jit(solution)/shard_map/all_gather | solution.py:316
  45.0 0.0 copy-done.4
  45.0 0.0 copy-done.6
  45.0 0.0 copy-done.7
  45.0 1.8 %block.1 = (f32[16,136,128]{2,1,0:T(8,128)S(1)}, f32[8,136,128]{2,1,0:T(8,128)S(1)}, f32[4,136,128]{2,1,0:T(8,128)S(1)}, f32[2,136,128]{2,1,0:T(8,128)S(1)}, f32[138,128]{1,0:T(8,128)S(1)}) custom-call(f32[16,72,128]{2,1,0:T(8,128)S(1)} %all-gather.1.packed, f32[1,128]{1,0:T(1,128)S(1)} %bitcast.21, f32[1,128]{1,0:T(1,128)S(1)} %bitcast.19, ...), custom_call_target="tpu_custom_call" | custom-call | tf_op jit(solution)/shard_map/block/pallas_call | solution.py:319
  46.9 14.2 %all_to_all.32.parts = f32[8,138,128]{2,1,0:T(8,128)S(1)} all-to-all(f32[8,138,128]{2,1,0:T(8,128)S(1)} %broadcast_in_dim.11), channel_id=1, replica_groups=mesh['zh'=4,'zl'=2,'x'=4,'y'=8,'c'=2] {'zl','x'}, dimensions={0} | all-to-all | bytes 1130496 | tf_op jit(solution)/shard_map/all_to_all | solution.py:274
  61.1 3.8 %all-gather.2 = f32[16,120,128]{2,1,0:T(8,128)S(1)} all-gather(f32[8,120,128]{2,1,0:T(8,128)S(1)} %slice.9), channel_id=4, replica_groups=mesh['zh'=4,'zl'=2,'x'=4,'y'=8,'c'=2] {'c'}, dimensions={0}, use_global_device_ids=true | all-gather | bytes 1474560 | tf_op jit(solution)/shard_map/all_gather | solution.py:330
  64.9 0.8 near.1
  65.8 0.0 copy-start
  65.8 0.0 copy-start.1
  65.8 0.0 copy-start.2
  65.8 0.0 copy-start.3
  65.8 0.0 copy-start.5
  65.8 19.0 %all_to_all.33 = f32[4,129,128]{2,1,0:T(8,128)S(1)} all-to-all(f32[4,129,128]{2,1,0:T(8,128)S(1)} %broadcast_in_dim.12), channel_id=1, replica_groups=mesh['zh'=4,'zl'=2,'x'=4,'y'=8,'c'=2] {'zh'}, dimensions={0} | all-to-all | bytes 528384 | tf_op jit(solution)/shard_map/all_to_all | solution.py:274
  84.9 4.2 %all-gather.3 = f32[8,129,128]{2,1,0:T(8,128)S(1)} all-gather(f32[4,129,128]{2,1,0:T(8,128)S(1)} %all_to_all.33), channel_id=5, replica_groups=mesh['zh'=4,'zl'=2,'x'=4,'y'=8,'c'=2] {'c'}, dimensions={0}, use_global_device_ids=true | all-gather | bytes 792576 | tf_op jit(solution)/shard_map/all_gather | solution.py:344
  89.1 0.0 copy-done
  89.1 0.0 copy-done.1
  89.1 0.0 copy-done.2
  89.1 0.0 copy-done.3
  89.1 0.0 copy-done.5
  89.1 2.5 %final.1 = (f32[16,128]{1,0:T(8,128)}, f32[3,128]{1,0:T(4,128)S(1)}) custom-call(f32[2,4,129,128]{3,2,1,0:T(8,128)S(1)} %bitcast.12, f32[2,2,136,128]{3,2,1,0:T(8,128)S(1)} %get-tuple-element.18.fours, f32[2,4,136,128]{3,2,1,0:T(8,128)S(1)} %get-tuple-element.19.twos, f32[8,138,128]{2,1,0:T(8,128)S(1)} %all_to_all.32.parts, f32[2,8,120,128]{3,2,1,0:T(8,128)S(1)} %bitcast.11, ...), custom_call_target="tpu_custom_call" | custom-call | tf_op jit(solution)/shard_map/final/pallas_call | solution.py:349
  91.6 10.2 %all_to_all.34 = f32[16,3,128]{2,1,0:T(4,128)S(1)} all-to-all(f32[16,3,128]{2,1,0:T(4,128)S(1)} %broadcast_in_dim.13), channel_id=1, replica_groups=mesh['zh'=4,'zl'=2,'x'=4,'y'=8,'c'=2] {'y','c'}, dimensions={0} | all-to-all | bytes 49152 | tf_op jit(solution)/shard_map/all_to_all | solution.py:274
  101.9 12.0 %all_to_all.35.parts = f32[32,3,128]{2,1,0:T(4,128)S(1)} all-to-all(f32[32,3,128]{2,1,0:T(4,128)S(1)} %broadcast_in_dim.14), channel_id=1, replica_groups=mesh['zh'=4,'zl'=2,'x'=4,'y'=8,'c'=2] {'zh','zl','x'}, dimensions={0} | all-to-all | bytes 98304 | tf_op jit(solution)/shard_map/all_to_all | solution.py:274
  113.8 0.8 tail.1
  (11 shorter events, 0.3 us)
Async XLA Ops:
  27.0 18.0 %copy-start.4 = (f32[128]{0:T(128)S(1)}, f32[128]{0:T(128)}, u32[]{:S(2)}) copy-start(f32[128]{0:T(128)} %param.14) | copy-start | bytes 1540
  27.1 17.9 %copy-start.6 = (f32[128]{0:T(128)S(1)}, f32[128]{0:T(128)}, u32[]{:S(2)}) copy-start(f32[128]{0:T(128)} %param.13) | copy-start | bytes 1540
  27.1 17.9 %copy-start.7 = (f32[128]{0:T(128)S(1)}, f32[128]{0:T(128)}, u32[]{:S(2)}) copy-start(f32[128]{0:T(128)} %param.12) | copy-start | bytes 1540
  65.8 23.4 %copy-start = (bf16[1024,128]{1,0:T(8,128)(2,1)S(1)}, bf16[1024,128]{1,0:T(8,128)(2,1)}, u32[]{:S(2)}) copy-start(bf16[1024,128]{1,0:T(8,128)(2,1)} %loadings.1) | copy-start | bytes 786436
  65.8 23.3 %copy-start.1 = (s32[16,1024]{1,0:T(8,128)S(1)}, s32[16,1024]{1,0:T(8,128)}, u32[]{:S(2)}) copy-start(s32[16,1024]{1,0:T(8,128)} %present.1) | copy-start | bytes 196612
  65.8 23.3 %copy-start.2 = (bf16[16,1024]{1,0:T(8,128)(2,1)S(1)}, bf16[16,1024]{1,0:T(8,128)(2,1)}, u32[]{:S(2)}) copy-start(bf16[16,1024]{1,0:T(8,128)(2,1)} %readings.1) | copy-start | bytes 98308
  65.8 23.3 %copy-start.3 = (f32[1024]{0:T(1024)S(1)}, f32[1024]{0:T(1024)}, u32[]{:S(2)}) copy-start(f32[1024]{0:T(1024)} %param.11) | copy-start | bytes 12292
  65.8 23.3 %copy-start.5 = (s32[1024]{0:T(1024)S(1)}, s32[1024]{0:T(1024)}, u32[]{:S(2)}) copy-start(s32[1024]{0:T(1024)} %param.15) | copy-start | bytes 12292

commit v8 on v7

--- a/solution.py
+++ b/solution.py
@@ -10,7 +10,7 @@
 GROUPS = 16
 SERIES = ("y", "c")
 NEAR = ("zl", "x")
-TM = ("zh", *NEAR)
+TM = ("za", "zb", *NEAR)
 F32 = jnp.float32
 BF16 = jnp.bfloat16
 VM = pl.BlockSpec(memory_space=pltpu.VMEM)
@@ -160,6 +160,22 @@
     half_total[...] = jnp.where(lax.axis_index("c") == 0, *nodes[0])[: half_total.shape[0]]
 
 
+def far_pair(pair):
+    return [(pair[2 * i], pair[2 * i + 1]) for i in (0, 1)]
+
+
+def half_kernel(pair, factor_rate, smooth_rate, sent):
+    k = smooth_rate.shape[1]
+    share = sent.shape[0] - 8
+    rate = smooth_rate[...]
+    none = jnp.zeros((7, k), F32)
+    nodes = [[jnp.concatenate([part, none], axis=0) for part in node] for node in far_pair(pair)]
+    maps, gives = joined(*nodes, jnp.exp(-128.0 * rate))
+    gives = gives + jnp.exp(-256.0 * rate - factor_rate[...]) * maps
+    sent[:share] = jnp.where(lax.axis_index("c") == 0, gives[:share], gives[share:k])
+    sent[share:] = jnp.concatenate([maps[k : k + 1], gives[k : k + 1], none[:6]], axis=0)
+
+
 def applied(current, one):
     k = one.shape[1]
     return dot3(current, one[:k]) + one[k : k + 1]
@@ -198,19 +214,26 @@
 
 
 def final_kernel(
-    planes, fours, twos, parts, sides, leaves, pairs, quads, eighths, factor_rate, smooth_rate,
+    pair, halves_sent, fours, twos, parts, sides, leaves, pairs, quads, eighths, factor_rate, smooth_rate,
     readings, present, loadings, noise, regions, scale, smoothed, out,
 ):
     hours, _, k = leaves.shape
-    far, near = lax.axis_index("zh"), lax.axis_index(NEAR)
+    upper, far, near = (lax.axis_index(a) for a in ("za", "zb", NEAR))
     decays = jnp.exp(-factor_rate[...])
     rate = smooth_rate[...]
     retain = jnp.exp(-rate)
-    plane_nodes = [(planes[0, i], planes[1, i]) for i in range(planes.shape[1])]
-    start, final, plane_gives = walked(plane_nodes, jnp.zeros((8, k), F32), far)
+    share = halves_sent.shape[1] - 8
+    middle = jnp.broadcast_to(halves_sent[0, share : share + 1], (8, k))
+    later = jnp.concatenate([halves_sent[2, :share], halves_sent[3, :share]], axis=0)
+    behind = (dot3(middle, later) + halves_sent[2, share + 1 : share + 2])[:1]
+    start = jnp.where(upper == 0, 0.0, middle)
+    start, final, far_gives = walked(far_pair(pair), start, far)
     count = parts.shape[0]
     following = followed(
-        plane_gives, decays * final[:1], far, jnp.exp(-float(count * hours) * rate)
+        far_gives,
+        jnp.where(upper == 0, behind, decays * final[:1]),
+        far,
+        jnp.exp(-float(count * hours) * rate),
     )
     for part, size in ((fours, 4), (twos, 2), (None, 1)):
         slot = lax.div(near, size)
@@ -341,7 +364,16 @@
         compiler_params=PARAMS,
         name="near",
     )(parts, sides, smooth)
-    planes = lax.all_gather(sent_to_all(half_total, "zh"), "c")
+    pair = lax.all_gather(half_total, ("zb", "c"))
+    half_sent = pl.pallas_call(
+        half_kernel,
+        out_shape=shape_of(k // 2 + 8, k),
+        in_specs=[VM] * 3,
+        out_specs=VM,
+        compiler_params=PARAMS,
+        name="half",
+    )(pair, factor, smooth)
+    halves_sent = lax.all_gather(half_sent, ("za", "c"))
 
     hours_all = hours * blocks
     series_all = series * ny * cores
@@ -349,12 +381,12 @@
     smoothed, local = pl.pallas_call(
         final_kernel,
         out_shape=[shape_of(hours, k), shape_of(3, 128)],
-        in_specs=[VM] * 16 + [SM],
+        in_specs=[VM] * 17 + [SM],
         out_specs=[VM] * 2,
         compiler_params=PARAMS,
         name="final",
     )(
-        planes, fours, twos, parts, sides, leaves, pairs, quads, eighths, factor, smooth,
+        pair, halves_sent, fours, twos, parts, sides, leaves, pairs, quads, eighths, factor, smooth,
         readings, present, loadings, noise, regions.reshape(1, series), scale,
     )
 
@@ -371,7 +403,7 @@
 
 
 def solution(mesh):
-    split = Mesh(mesh.devices.reshape(4, 2, 4, 8, 2), (*TM, *SERIES))
+    split = Mesh(mesh.devices.reshape(2, 2, 2, 4, 8, 2), (*TM, *SERIES))
     in_specs = (P(TM, SERIES), P(TM, SERIES), P(SERIES, None), P(SERIES), P(), P(), P(), P(SERIES))
     out_specs = (P(TM, None), P())
     return jax.shard_map(body, mesh=split, in_specs=in_specs, out_specs=out_specs, check_vma=False)

time: 115 us -> 116 us (level)
    all_gather x1 -> x2, blocking collectives: 4.23 us -> 20.3 us  [the longest x1 10.2 us: body(): pair = lax.all_gather(half_total, ('zb', 'c'))]
    all_to_all x5 -> x4, blocking collectives: 68.9 us -> 53.9 us  [sent_to_all(): lax.all_to_all(jnp.broadcast_to(shard[None], (count, *shard.shape)), axis...]
where the time goes in v8:
time: 116 us
  blocking collectives  106 us (91%)
  Pallas kernels  8.37 us (7%)
    all_to_all x4, blocking collectives, sent_to_all(): lax.all_to_all(jnp.broadcast_to(shard[None], (count, *shard.shape)), axis...  53.9 us
    all_to_all x1, blocking collectives, body(): lax.all_to_all(kept + arrived[:, :height], 'y', 0, 0, tiled=True)  15 us
    all_gather x1, blocking collectives, body(): pair = lax.all_gather(half_total, ('zb', 'c'))  10.2 us
    all_gather x1, blocking collectives, body(): halves_sent = lax.all_gather(half_sent, ('za', 'c'))  10.1 us
    all_gather x1, blocking collectives, body(): lax.all_gather(sent, 'c')  8.73 us
    all_gather x1, blocking collectives, body(): packed = lax.all_gather(packed, 'c').reshape(hours, padded, k)  4.34 us
    all_gather x1, blocking collectives, body(): sides = lax.all_gather(parts[:, :k - 8], 'c')  3.84 us
    pallas_call x1, Pallas kernels, body(): pl.pallas_call(information_kernel, out_shape=[shape_of(share, height, k),...  2.51 us

profile of v8, /device:TPU:1, one launch (start us, length us, event | category | flops | bytes accessed | tf_op | source)
XLA Modules:
  0.0 115.6 jit_solution(3208438649906571733)
XLA Ops:
  0.6 2.5 %information.1 = (f32[8,66,128]{2,1,0:T(8,128)S(1)}, f32[8,72,128]{2,1,0:T(8,128)S(1)}) custom-call(bf16[16,1024]{1,0:T(8,128)(2,1)} %readings.1, s32[16,1024]{1,0:T(8,128)} %present.1, bf16[1024,128]{1,0:T(8,128)(2,1)} %loadings.1, f32[1,1024]{1,0:T(1,128)} %bitcast.15), custom_call_target="tpu_custom_call" | custom-call | tf_op jit(solution)/shard_map/information/pallas_call | solution.py:319
  3.1 8.7 %all-gather = f32[16,72,128]{2,1,0:T(8,128)S(1)} all-gather(f32[8,72,128]{2,1,0:T(8,128)S(1)} %get-tuple-element.15), channel_id=2, replica_groups=mesh['za'=2,'zb'=2,'zl'=2,'x'=4,'y'=8,'c'=2] {'c'}, dimensions={0}, use_global_device_ids=true | all-gather | bytes 884736 | tf_op jit(solution)/shard_map/all_gather | solution.py:336
  11.9 15.0 %all_to_all.25 = f32[8,66,128]{2,1,0:T(8,128)S(1)} all-to-all(f32[8,66,128]{2,1,0:T(8,128)S(1)} %slice_add_fusion), channel_id=1, replica_groups=mesh['za'=2,'zb'=2,'zl'=2,'x'=4,'y'=8,'c'=2] {'y'}, dimensions={0} | all-to-all | bytes 540672 | tf_op jit(solution)/shard_map/all_to_all | solution.py:337
  27.0 0.0 copy-start.4
  27.1 0.0 copy-start.5
  27.1 0.0 copy-start.7
  27.1 13.5 %all_to_all.26 = f32[8,66,128]{2,1,0:T(8,128)S(1)} all-to-all(f32[8,66,128]{2,1,0:T(8,128)S(1)} %broadcast_in_dim.8), channel_id=1, replica_groups=mesh['za'=2,'zb'=2,'zl'=2,'x'=4,'y'=8,'c'=2] {'y'}, dimensions={0} | all-to-all | bytes 540672 | tf_op jit(solution)/shard_map/all_to_all | solution.py:297
  40.6 4.3 %all-gather.1.packed = f32[16,72,128]{2,1,0:T(8,128)S(1)} all-gather(f32[8,72,128]{2,1,0:T(8,128)S(1)} %pad.4), channel_id=3, replica_groups=mesh['za'=2,'zb'=2,'zl'=2,'x'=4,'y'=8,'c'=2] {'c'}, dimensions={0}, use_global_device_ids=true | all-gather | bytes 884736 | tf_op jit(solution)/shard_map/all_gather | solution.py:339
  45.0 0.0 copy-done.4
  45.0 0.0 copy-done.5
  45.0 0.0 copy-done.7
  45.0 1.8 %block.1 = (f32[16,136,128]{2,1,0:T(8,128)S(1)}, f32[8,136,128]{2,1,0:T(8,128)S(1)}, f32[4,136,128]{2,1,0:T(8,128)S(1)}, f32[2,136,128]{2,1,0:T(8,128)S(1)}, f32[138,128]{1,0:T(8,128)S(1)}) custom-call(f32[16,72,128]{2,1,0:T(8,128)S(1)} %all-gather.1.packed, f32[1,128]{1,0:T(1,128)S(1)} %bitcast.25, f32[1,128]{1,0:T(1,128)S(1)} %bitcast.21, ...), custom_call_target="tpu_custom_call" | custom-call | tf_op jit(solution)/shard_map/block/pallas_call | solution.py:342
  46.9 14.2 %all_to_all.27.parts = f32[8,138,128]{2,1,0:T(8,128)S(1)} all-to-all(f32[8,138,128]{2,1,0:T(8,128)S(1)} %broadcast_in_dim.9), channel_id=1, replica_groups=mesh['za'=2,'zb'=2,'zl'=2,'x'=4,'y'=8,'c'=2] {'zl','x'}, dimensions={0} | all-to-all | bytes 1130496 | tf_op jit(solution)/shard_map/all_to_all | solution.py:297
  61.1 3.8 %all-gather.2 = f32[16,120,128]{2,1,0:T(8,128)S(1)} all-gather(f32[8,120,128]{2,1,0:T(8,128)S(1)} %slice.9), channel_id=4, replica_groups=mesh['za'=2,'zb'=2,'zl'=2,'x'=4,'y'=8,'c'=2] {'c'}, dimensions={0}, use_global_device_ids=true | all-gather | bytes 1474560 | tf_op jit(solution)/shard_map/all_gather | solution.py:353
  64.9 0.0 copy-start
  64.9 0.0 copy-start.1
  64.9 0.0 copy-start.2
  64.9 0.0 copy-start.3
  64.9 0.0 copy-start.6
  64.9 0.8 near.1
  65.8 10.2 %all-gather.5.pair = f32[4,129,128]{2,1,0:T(8,128)S(1)} all-gather(f32[1,129,128]{2,1,0:T(8,128)S(1)} %bitcast.14), channel_id=5, replica_groups=mesh['za'=2,'zb'=2,'zl'=2,'x'=4,'y'=8,'c'=2] {'zb','c'}, dimensions={0}, use_global_device_ids=true | all-gather | bytes 330240 | tf_op jit(solution)/shard_map/all_gather | solution.py:367
  76.0 0.2 half.1
  76.2 10.1 %all-gather.4 = f32[288,128]{1,0:T(8,128)S(1)} all-gather(f32[72,128]{1,0:T(8,128)S(1)} %half.1), channel_id=6, replica_groups=mesh['za'=2,'zb'=2,'zl'=2,'x'=4,'y'=8,'c'=2] {'za','c'}, dimensions={0}, use_global_device_ids=true | all-gather | bytes 184320 | tf_op jit(solution)/shard_map/all_gather | solution.py:376
  86.3 0.0 copy-done
  86.3 0.0 copy-done.1
  86.3 0.0 copy-done.2
  86.3 0.0 copy-done.3
  86.3 0.0 copy-done.6
  86.3 2.2 %final.1 = (f32[16,128]{1,0:T(8,128)}, f32[3,128]{1,0:T(4,128)S(1)}) custom-call(f32[4,129,128]{2,1,0:T(8,128)S(1)} %all-gather.5.pair, f32[4,72,128]{2,1,0:T(8,128)S(1)} %bitcast.13, f32[2,2,136,128]{3,2,1,0:T(8,128)S(1)} %get-tuple-element.18.fours, f32[2,4,136,128]{3,2,1,0:T(8,128)S(1)} %get-tuple-element.19.twos, f32[8,138,128]{2,1,0:T(8,128)S(1)} %all_to_all.27.parts, ...), custom_call_target="tpu_custom_call" | custom-call | tf_op jit(solution)/shard_map/final/pallas_call | solution.py:381
  88.6 10.0 %all_to_all.28 = f32[16,3,128]{2,1,0:T(4,128)S(1)} all-to-all(f32[16,3,128]{2,1,0:T(4,128)S(1)} %broadcast_in_dim.10), channel_id=1, replica_groups=mesh['za'=2,'zb'=2,'zl'=2,'x'=4,'y'=8,'c'=2] {'y','c'}, dimensions={0} | all-to-all | bytes 49152 | tf_op jit(solution)/shard_map/all_to_all | solution.py:297
  98.6 16.2 %all_to_all.29.parts = f32[32,3,128]{2,1,0:T(4,128)S(1)} all-to-all(f32[32,3,128]{2,1,0:T(4,128)S(1)} %broadcast_in_dim.11), channel_id=1, replica_groups=mesh['za'=2,'zb'=2,'zl'=2,'x'=4,'y'=8,'c'=2] {'za','zb','zl','x'}, dimensions={0} | all-to-all | bytes 98304 | tf_op jit(solution)/shard_map/all_to_all | solution.py:297
  114.8 0.8 tail.1
  (10 shorter events, 0.2 us)
Async XLA Ops:
  27.0 18.0 %copy-start.4 = (f32[128]{0:T(128)S(1)}, f32[128]{0:T(128)}, u32[]{:S(2)}) copy-start(f32[128]{0:T(128)} %param.14) | copy-start | bytes 1540
  27.1 17.9 %copy-start.5 = (f32[128]{0:T(128)S(1)}, f32[128]{0:T(128)}, u32[]{:S(2)}) copy-start(f32[128]{0:T(128)} %param.13) | copy-start | bytes 1540
  27.1 17.9 %copy-start.7 = (f32[128]{0:T(128)S(1)}, f32[128]{0:T(128)}, u32[]{:S(2)}) copy-start(f32[128]{0:T(128)} %param.12) | copy-start | bytes 1540
  64.9 21.4 %copy-start = (bf16[1024,128]{1,0:T(8,128)(2,1)S(1)}, bf16[1024,128]{1,0:T(8,128)(2,1)}, u32[]{:S(2)}) copy-start(bf16[1024,128]{1,0:T(8,128)(2,1)} %loadings.1) | copy-start | bytes 786436
  64.9 21.4 %copy-start.1 = (s32[16,1024]{1,0:T(8,128)S(1)}, s32[16,1024]{1,0:T(8,128)}, u32[]{:S(2)}) copy-start(s32[16,1024]{1,0:T(8,128)} %present.1) | copy-start | bytes 196612
  64.9 21.4 %copy-start.2 = (bf16[16,1024]{1,0:T(8,128)(2,1)S(1)}, bf16[16,1024]{1,0:T(8,128)(2,1)}, u32[]{:S(2)}) copy-start(bf16[16,1024]{1,0:T(8,128)(2,1)} %readings.1) | copy-start | bytes 98308
  64.9 21.4 %copy-start.3 = (f32[1024]{0:T(1024)S(1)}, f32[1024]{0:T(1024)}, u32[]{:S(2)}) copy-start(f32[1024]{0:T(1024)} %param.11) | copy-start | bytes 12292
  64.9 21.4 %copy-start.6 = (s32[1024]{0:T(1024)S(1)}, s32[1024]{0:T(1024)}, u32[]{:S(2)}) copy-start(s32[1024]{0:T(1024)} %param.15) | copy-start | bytes 12292

commit v9 on v7

--- a/solution.py
+++ b/solution.py
@@ -94,8 +94,7 @@
 
 
 def block_kernel(
-    packed, gain, factor_rate, smooth_rate, leaves, pairs, quads, eighths, sent,
-    given1, given2, given4, given8,
+    packed, gain, factor_rate, smooth_rate, leaves, pairs, quads, eighths, sent
 ):
     hours = packed.shape[0]
     k = packed.shape[2]
@@ -109,7 +108,9 @@
     row_k, lane_k = iotas(k, k)
     on_diag = row_k == lane_k
     identity = on_diag.astype(F32)
-    for h in range(hours):
+    levels = {1: leaves, 2: pairs, 4: quads, 8: eighths}
+
+    def leaf(h):
         page = packed[h]
         top = page[:half]
         upper = jnp.where(lane >= row, top, 0.0)
@@ -118,18 +119,22 @@
         inform = jnp.where(on_diag, page[half : half + 1], part + jnp.transpose(part))
         matrix = (identity - inform * gain_row) * decay_col
         shift = gain_row * page[half + 1 : half + 2]
-        one = jnp.concatenate([matrix, shift, jnp.zeros((7, k), F32)], axis=0)
-        leaves[h] = one
-        given1[h] = one * weight
-    below, given = leaves, given1
-    for span, above, gives in ((1, pairs, given2), (2, quads, given4), (4, eighths, given8)):
-        fade = jnp.exp(-span * rate)
-        for i in range(hours // (2 * span)):
-            above[i], gives[i] = joined(
-                (below[2 * i], given[2 * i]), (below[2 * i + 1], given[2 * i + 1]), fade
+        maps = jnp.concatenate([matrix, shift, jnp.zeros((7, k), F32)], axis=0)
+        return maps, maps * weight
+
+    def grown(at, span):
+        if span == 1:
+            node = leaf(at)
+        else:
+            middle = span // 2
+            node = joined(
+                grown(at, middle), grown(at + middle, middle), jnp.exp(-float(middle) * rate)
             )
-        below, given = above, gives
-    total = joined((below[0], given[0]), (below[1], given[1]), jnp.exp(-8.0 * rate))
+        if span in levels:
+            levels[span][at // span] = node[0]
+        return node
+
+    total = grown(0, hours)
     first = lax.axis_index("c") == 0
     sent[:k] = jnp.where(first, total[0][:k], total[1][:k])
     sent[k : k + 8] = jnp.where(first, total[1][k - 8 : k], total[0][k - 8 : k])
@@ -321,7 +326,6 @@
         out_shape=nodes + [shape_of(k + 10, k)],
         in_specs=[VM] * 4,
         out_specs=[VM] * 5,
-        scratch_shapes=[pltpu.VMEM((hours // n, tall, k), F32) for n in (1, 2, 4, 8)],
         compiler_params=PARAMS,
         name="block",
     )(packed, gain, factor, smooth)

time: 115 us -> 115 us (level)
  no operation moved by 1% of the time
where the time goes in v9:
time: 115 us
  blocking collectives  105 us (91%)
  Pallas kernels  8.88 us (8%)
    all_to_all x5, blocking collectives, sent_to_all(): lax.all_to_all(jnp.broadcast_to(shard[None], (count, *shard.shape)), axis...  69 us
    all_to_all x1, blocking collectives, body(): lax.all_to_all(kept + arrived[:, :height], 'y', 0, 0, tiled=True)  15 us
    all_gather x1, blocking collectives, body(): lax.all_gather(sent, 'c')  8.73 us
    all_gather x1, blocking collectives, body(): packed = lax.all_gather(packed, 'c').reshape(hours, padded, k)  4.34 us
    all_gather x1, blocking collectives, body(): planes = lax.all_gather(sent_to_all(half_total, 'zh'), 'c')  4.23 us
    all_gather x1, blocking collectives, body(): sides = lax.all_gather(parts[:, :k - 8], 'c')  3.84 us
    pallas_call x1, Pallas kernels, body(): pl.pallas_call(information_kernel, out_shape=[shape_of(share, height, k),...  2.51 us
    pallas_call x1, Pallas kernels, body(): pl.pallas_call(final_kernel, out_shape=[shape_of(hours, k), shape_of(3, 1...  2.45 us

profile of v9, /device:TPU:1, one launch (start us, length us, event | category | flops | bytes accessed | tf_op | source)
XLA Modules:
  0.0 115.1 jit_solution(1718079213721996176)
XLA Ops:
  0.6 2.5 %information.1 = (f32[8,66,128]{2,1,0:T(8,128)S(1)}, f32[8,72,128]{2,1,0:T(8,128)S(1)}) custom-call(bf16[16,1024]{1,0:T(8,128)(2,1)} %readings.1, s32[16,1024]{1,0:T(8,128)} %present.1, bf16[1024,128]{1,0:T(8,128)(2,1)} %loadings.1, f32[1,1024]{1,0:T(1,128)} %bitcast.13), custom_call_target="tpu_custom_call" | custom-call | tf_op jit(solution)/shard_map/information/pallas_call | solution.py:301
  3.1 8.7 %all-gather = f32[16,72,128]{2,1,0:T(8,128)S(1)} all-gather(f32[8,72,128]{2,1,0:T(8,128)S(1)} %get-tuple-element.15), channel_id=2, replica_groups=mesh['zh'=4,'zl'=2,'x'=4,'y'=8,'c'=2] {'c'}, dimensions={0}, use_global_device_ids=true | all-gather | bytes 884736 | tf_op jit(solution)/shard_map/all_gather | solution.py:318
  11.9 15.0 %all_to_all.30 = f32[8,66,128]{2,1,0:T(8,128)S(1)} all-to-all(f32[8,66,128]{2,1,0:T(8,128)S(1)} %slice_add_fusion), channel_id=1, replica_groups=mesh['zh'=4,'zl'=2,'x'=4,'y'=8,'c'=2] {'y'}, dimensions={0} | all-to-all | bytes 540672 | tf_op jit(solution)/shard_map/all_to_all | solution.py:319
  27.0 0.0 copy-start.4
  27.1 0.0 copy-start.6
  27.1 0.0 copy-start.7
  27.1 13.5 %all_to_all.31 = f32[8,66,128]{2,1,0:T(8,128)S(1)} all-to-all(f32[8,66,128]{2,1,0:T(8,128)S(1)} %broadcast_in_dim.10), channel_id=1, replica_groups=mesh['zh'=4,'zl'=2,'x'=4,'y'=8,'c'=2] {'y'}, dimensions={0} | all-to-all | bytes 540672 | tf_op jit(solution)/shard_map/all_to_all | solution.py:279
  40.6 4.3 %all-gather.1.packed = f32[16,72,128]{2,1,0:T(8,128)S(1)} all-gather(f32[8,72,128]{2,1,0:T(8,128)S(1)} %pad.4), channel_id=3, replica_groups=mesh['zh'=4,'zl'=2,'x'=4,'y'=8,'c'=2] {'c'}, dimensions={0}, use_global_device_ids=true | all-gather | bytes 884736 | tf_op jit(solution)/shard_map/all_gather | solution.py:321
  45.0 0.0 copy-done.4
  45.0 0.0 copy-done.6
  45.0 0.0 copy-done.7
  45.0 2.3 %block.1 = (f32[16,136,128]{2,1,0:T(8,128)S(1)}, f32[8,136,128]{2,1,0:T(8,128)S(1)}, f32[4,136,128]{2,1,0:T(8,128)S(1)}, f32[2,136,128]{2,1,0:T(8,128)S(1)}, f32[138,128]{1,0:T(8,128)S(1)}) custom-call(f32[16,72,128]{2,1,0:T(8,128)S(1)} %all-gather.1.packed, f32[1,128]{1,0:T(1,128)S(1)} %bitcast.21, f32[1,128]{1,0:T(1,128)S(1)} %bitcast.19, ...), custom_call_target="tpu_custom_call" | custom-call | tf_op jit(solution)/shard_map/block/pallas_call | solution.py:324
  47.4 14.2 %all_to_all.32.parts = f32[8,138,128]{2,1,0:T(8,128)S(1)} all-to-all(f32[8,138,128]{2,1,0:T(8,128)S(1)} %broadcast_in_dim.11), channel_id=1, replica_groups=mesh['zh'=4,'zl'=2,'x'=4,'y'=8,'c'=2] {'zl','x'}, dimensions={0} | all-to-all | bytes 1130496 | tf_op jit(solution)/shard_map/all_to_all | solution.py:279
  61.6 3.8 %all-gather.2 = f32[16,120,128]{2,1,0:T(8,128)S(1)} all-gather(f32[8,120,128]{2,1,0:T(8,128)S(1)} %slice.9), channel_id=4, replica_groups=mesh['zh'=4,'zl'=2,'x'=4,'y'=8,'c'=2] {'c'}, dimensions={0}, use_global_device_ids=true | all-gather | bytes 1474560 | tf_op jit(solution)/shard_map/all_gather | solution.py:334
  65.4 0.8 near.1
  66.3 0.0 copy-start
  66.3 0.0 copy-start.1
  66.3 0.0 copy-start.2
  66.3 0.0 copy-start.3
  66.3 0.0 copy-start.5
  66.4 19.0 %all_to_all.33 = f32[4,129,128]{2,1,0:T(8,128)S(1)} all-to-all(f32[4,129,128]{2,1,0:T(8,128)S(1)} %broadcast_in_dim.12), channel_id=1, replica_groups=mesh['zh'=4,'zl'=2,'x'=4,'y'=8,'c'=2] {'zh'}, dimensions={0} | all-to-all | bytes 528384 | tf_op jit(solution)/shard_map/all_to_all | solution.py:279
  85.4 4.2 %all-gather.3 = f32[8,129,128]{2,1,0:T(8,128)S(1)} all-gather(f32[4,129,128]{2,1,0:T(8,128)S(1)} %all_to_all.33), channel_id=5, replica_groups=mesh['zh'=4,'zl'=2,'x'=4,'y'=8,'c'=2] {'c'}, dimensions={0}, use_global_device_ids=true | all-gather | bytes 792576 | tf_op jit(solution)/shard_map/all_gather | solution.py:348
  89.6 0.0 copy-done
  89.6 0.0 copy-done.1
  89.6 0.0 copy-done.2
  89.6 0.0 copy-done.3
  89.6 0.0 copy-done.5
  89.6 2.5 %final.1 = (f32[16,128]{1,0:T(8,128)}, f32[3,128]{1,0:T(4,128)S(1)}) custom-call(f32[2,4,129,128]{3,2,1,0:T(8,128)S(1)} %bitcast.12, f32[2,2,136,128]{3,2,1,0:T(8,128)S(1)} %get-tuple-element.18.fours, f32[2,4,136,128]{3,2,1,0:T(8,128)S(1)} %get-tuple-element.19.twos, f32[8,138,128]{2,1,0:T(8,128)S(1)} %all_to_all.32.parts, f32[2,8,120,128]{3,2,1,0:T(8,128)S(1)} %bitcast.11, ...), custom_call_target="tpu_custom_call" | custom-call | tf_op jit(solution)/shard_map/final/pallas_call | solution.py:353
  92.1 10.2 %all_to_all.34 = f32[16,3,128]{2,1,0:T(4,128)S(1)} all-to-all(f32[16,3,128]{2,1,0:T(4,128)S(1)} %broadcast_in_dim.13), channel_id=1, replica_groups=mesh['zh'=4,'zl'=2,'x'=4,'y'=8,'c'=2] {'y','c'}, dimensions={0} | all-to-all | bytes 49152 | tf_op jit(solution)/shard_map/all_to_all | solution.py:279
  102.4 12.0 %all_to_all.35.parts = f32[32,3,128]{2,1,0:T(4,128)S(1)} all-to-all(f32[32,3,128]{2,1,0:T(4,128)S(1)} %broadcast_in_dim.14), channel_id=1, replica_groups=mesh['zh'=4,'zl'=2,'x'=4,'y'=8,'c'=2] {'zh','zl','x'}, dimensions={0} | all-to-all | bytes 98304 | tf_op jit(solution)/shard_map/all_to_all | solution.py:279
  114.3 0.8 tail.1
  (11 shorter events, 0.3 us)
Async XLA Ops:
  27.0 18.0 %copy-start.4 = (f32[128]{0:T(128)S(1)}, f32[128]{0:T(128)}, u32[]{:S(2)}) copy-start(f32[128]{0:T(128)} %param.14) | copy-start | bytes 1540
  27.1 17.9 %copy-start.6 = (f32[128]{0:T(128)S(1)}, f32[128]{0:T(128)}, u32[]{:S(2)}) copy-start(f32[128]{0:T(128)} %param.13) | copy-start | bytes 1540
  27.1 17.9 %copy-start.7 = (f32[128]{0:T(128)S(1)}, f32[128]{0:T(128)}, u32[]{:S(2)}) copy-start(f32[128]{0:T(128)} %param.12) | copy-start | bytes 1540
  66.3 23.4 %copy-start = (bf16[1024,128]{1,0:T(8,128)(2,1)S(1)}, bf16[1024,128]{1,0:T(8,128)(2,1)}, u32[]{:S(2)}) copy-start(bf16[1024,128]{1,0:T(8,128)(2,1)} %loadings.1) | copy-start | bytes 786436
  66.3 23.3 %copy-start.1 = (s32[16,1024]{1,0:T(8,128)S(1)}, s32[16,1024]{1,0:T(8,128)}, u32[]{:S(2)}) copy-start(s32[16,1024]{1,0:T(8,128)} %present.1) | copy-start | bytes 196612
  66.3 23.3 %copy-start.2 = (bf16[16,1024]{1,0:T(8,128)(2,1)S(1)}, bf16[16,1024]{1,0:T(8,128)(2,1)}, u32[]{:S(2)}) copy-start(bf16[16,1024]{1,0:T(8,128)(2,1)} %readings.1) | copy-start | bytes 98308
  66.3 23.3 %copy-start.3 = (f32[1024]{0:T(1024)S(1)}, f32[1024]{0:T(1024)}, u32[]{:S(2)}) copy-start(f32[1024]{0:T(1024)} %param.11) | copy-start | bytes 12292
  66.3 23.3 %copy-start.5 = (s32[1024]{0:T(1024)S(1)}, s32[1024]{0:T(1024)}, u32[]{:S(2)}) copy-start(s32[1024]{0:T(1024)} %param.15) | copy-start | bytes 12292

commit v10 on v7

--- a/solution.py
+++ b/solution.py
@@ -121,8 +121,12 @@
         one = jnp.concatenate([matrix, shift, jnp.zeros((7, k), F32)], axis=0)
         leaves[h] = one
         given1[h] = one * weight
-    below, given = leaves, given1
-    for span, above, gives in ((1, pairs, given2), (2, quads, given4), (4, eighths, given8)):
+        if h % 2:
+            pairs[h // 2], given2[h // 2] = joined(
+                (leaves[h - 1], given1[h - 1]), (leaves[h], given1[h]), jnp.exp(-rate)
+            )
+    below, given = pairs, given2
+    for span, above, gives in ((2, quads, given4), (4, eighths, given8)):
         fade = jnp.exp(-span * rate)
         for i in range(hours // (2 * span)):
             above[i], gives[i] = joined(
@@ -238,21 +242,21 @@
     fitted = across(smoothed[...].astype(BF16), loadings[...])
     standard = (readings[...].astype(F32) - fitted) * jnp.sqrt(noise[...])
     probab = 0.5 * (1.0 + lax.erf(standard * 0.7071067811865476))
-    seen = present[...].astype(F32)
+    place = jnp.where(present[...] > 0, float(BINS) * probab, -8.0)
     rows = []
     for b in range(BINS):
-        kernel = jnp.maximum(0.0, 1.0 - BINS * jnp.abs(probab - (b + 0.5) / BINS))
-        rows.append(jnp.sum(seen * kernel, axis=0, keepdims=True))
-    rows.append(jnp.zeros((4, probab.shape[1]), F32))
+        kernel = jnp.maximum(0.0, 1.0 - jnp.abs(place - (b + 0.5)))
+        rows.append(sum(kernel[at : at + 8] for at in range(0, hours, 8)))
     table = jnp.concatenate(rows, axis=0)
     slot, _ = iotas(128, probab.shape[1])
     member = (lax.rem(slot, GROUPS) == regions[...]).astype(F32).astype(BF16)
     wide = across(jnp.concatenate(halves(table), axis=0), member)
-    wide = wide[:24] + wide[24:]
-    brow, blane = iotas(24, 128)
-    kept = jnp.where(lax.div(blane, GROUPS) == lax.rem(brow, 8), wide, 0.0) * scale[0]
+    wide = wide[: 8 * BINS] + wide[8 * BINS :]
+    brow, blane = iotas(8 * BINS, 128)
+    kept = jnp.where(lax.div(blane, GROUPS) == lax.rem(lax.div(brow, 8), 8), wide, 0.0) * scale[0]
     out[...] = jnp.concatenate(
-        [jnp.sum(kept[8 * r : 8 * r + 8], axis=0, keepdims=True) for r in range(3)], axis=0
+        [jnp.sum(kept[at : at + 64], axis=0, keepdims=True) for at in range(0, 8 * BINS, 64)],
+        axis=0,
     )
 
 

time: 115 us -> 115 us (level)
  no operation moved by 1% of the time
where the time goes in v10:
time: 115 us; the launch traced here: 114 us
  blocking collectives  105 us (91%)
  Pallas kernels  8.2 us (7%)
    all_to_all x5, blocking collectives, sent_to_all(): lax.all_to_all(jnp.broadcast_to(shard[None], (count, *shard.shape)), axis...  69 us
    all_to_all x1, blocking collectives, body(): lax.all_to_all(kept + arrived[:, :height], 'y', 0, 0, tiled=True)  15 us
    all_gather x1, blocking collectives, body(): lax.all_gather(sent, 'c')  8.73 us
    all_gather x1, blocking collectives, body(): packed = lax.all_gather(packed, 'c').reshape(hours, padded, k)  4.34 us
    all_gather x1, blocking collectives, body(): planes = lax.all_gather(sent_to_all(half_total, 'zh'), 'c')  4.23 us
    all_gather x1, blocking collectives, body(): sides = lax.all_gather(parts[:, :k - 8], 'c')  3.84 us
    pallas_call x1, Pallas kernels, body(): pl.pallas_call(information_kernel, out_shape=[shape_of(share, height, k),...  2.51 us

profile of v10, /device:TPU:1, one launch (start us, length us, event | category | flops | bytes accessed | tf_op | source)
XLA Modules:
  0.0 114.4 jit_solution(7491317250540390568)
XLA Ops:
  0.6 2.5 %information.1 = (f32[8,66,128]{2,1,0:T(8,128)S(1)}, f32[8,72,128]{2,1,0:T(8,128)S(1)}) custom-call(bf16[16,1024]{1,0:T(8,128)(2,1)} %readings.1, s32[16,1024]{1,0:T(8,128)} %present.1, bf16[1024,128]{1,0:T(8,128)(2,1)} %loadings.1, f32[1,1024]{1,0:T(1,128)} %bitcast.13), custom_call_target="tpu_custom_call" | custom-call | tf_op jit(solution)/shard_map/information/pallas_call | solution.py:300
  3.1 8.7 %all-gather = f32[16,72,128]{2,1,0:T(8,128)S(1)} all-gather(f32[8,72,128]{2,1,0:T(8,128)S(1)} %get-tuple-element.15), channel_id=2, replica_groups=mesh['zh'=4,'zl'=2,'x'=4,'y'=8,'c'=2] {'c'}, dimensions={0}, use_global_device_ids=true | all-gather | bytes 884736 | tf_op jit(solution)/shard_map/all_gather | solution.py:317
  11.9 15.0 %all_to_all.30 = f32[8,66,128]{2,1,0:T(8,128)S(1)} all-to-all(f32[8,66,128]{2,1,0:T(8,128)S(1)} %slice_add_fusion), channel_id=1, replica_groups=mesh['zh'=4,'zl'=2,'x'=4,'y'=8,'c'=2] {'y'}, dimensions={0} | all-to-all | bytes 540672 | tf_op jit(solution)/shard_map/all_to_all | solution.py:318
  27.0 0.0 copy-start.4
  27.1 0.0 copy-start.6
  27.1 0.0 copy-start.7
  27.1 13.5 %all_to_all.31 = f32[8,66,128]{2,1,0:T(8,128)S(1)} all-to-all(f32[8,66,128]{2,1,0:T(8,128)S(1)} %broadcast_in_dim.10), channel_id=1, replica_groups=mesh['zh'=4,'zl'=2,'x'=4,'y'=8,'c'=2] {'y'}, dimensions={0} | all-to-all | bytes 540672 | tf_op jit(solution)/shard_map/all_to_all | solution.py:278
  40.6 4.3 %all-gather.1.packed = f32[16,72,128]{2,1,0:T(8,128)S(1)} all-gather(f32[8,72,128]{2,1,0:T(8,128)S(1)} %pad.4), channel_id=3, replica_groups=mesh['zh'=4,'zl'=2,'x'=4,'y'=8,'c'=2] {'c'}, dimensions={0}, use_global_device_ids=true | all-gather | bytes 884736 | tf_op jit(solution)/shard_map/all_gather | solution.py:320
  45.0 0.0 copy-done.4
  45.0 0.0 copy-done.6
  45.0 0.0 copy-done.7
  45.0 1.8 %block.1 = (f32[16,136,128]{2,1,0:T(8,128)S(1)}, f32[8,136,128]{2,1,0:T(8,128)S(1)}, f32[4,136,128]{2,1,0:T(8,128)S(1)}, f32[2,136,128]{2,1,0:T(8,128)S(1)}, f32[138,128]{1,0:T(8,128)S(1)}) custom-call(f32[16,72,128]{2,1,0:T(8,128)S(1)} %all-gather.1.packed, f32[1,128]{1,0:T(1,128)S(1)} %bitcast.21, f32[1,128]{1,0:T(1,128)S(1)} %bitcast.19, ...), custom_call_target="tpu_custom_call" | custom-call | tf_op jit(solution)/shard_map/block/pallas_call | solution.py:323
  46.9 14.2 %all_to_all.32.parts = f32[8,138,128]{2,1,0:T(8,128)S(1)} all-to-all(f32[8,138,128]{2,1,0:T(8,128)S(1)} %broadcast_in_dim.11), channel_id=1, replica_groups=mesh['zh'=4,'zl'=2,'x'=4,'y'=8,'c'=2] {'zl','x'}, dimensions={0} | all-to-all | bytes 1130496 | tf_op jit(solution)/shard_map/all_to_all | solution.py:278
  61.1 3.8 %all-gather.2 = f32[16,120,128]{2,1,0:T(8,128)S(1)} all-gather(f32[8,120,128]{2,1,0:T(8,128)S(1)} %slice.9), channel_id=4, replica_groups=mesh['zh'=4,'zl'=2,'x'=4,'y'=8,'c'=2] {'c'}, dimensions={0}, use_global_device_ids=true | all-gather | bytes 1474560 | tf_op jit(solution)/shard_map/all_gather | solution.py:334
  64.9 0.8 near.1
  65.8 0.0 copy-start
  65.8 0.0 copy-start.1
  65.8 0.0 copy-start.2
  65.8 0.0 copy-start.3
  65.8 0.0 copy-start.5
  65.9 19.0 %all_to_all.33 = f32[4,129,128]{2,1,0:T(8,128)S(1)} all-to-all(f32[4,129,128]{2,1,0:T(8,128)S(1)} %broadcast_in_dim.12), channel_id=1, replica_groups=mesh['zh'=4,'zl'=2,'x'=4,'y'=8,'c'=2] {'zh'}, dimensions={0} | all-to-all | bytes 528384 | tf_op jit(solution)/shard_map/all_to_all | solution.py:278
  84.9 4.2 %all-gather.3 = f32[8,129,128]{2,1,0:T(8,128)S(1)} all-gather(f32[4,129,128]{2,1,0:T(8,128)S(1)} %all_to_all.33), channel_id=5, replica_groups=mesh['zh'=4,'zl'=2,'x'=4,'y'=8,'c'=2] {'c'}, dimensions={0}, use_global_device_ids=true | all-gather | bytes 792576 | tf_op jit(solution)/shard_map/all_gather | solution.py:348
  89.1 0.0 copy-done
  89.1 0.0 copy-done.1
  89.1 0.0 copy-done.2
  89.1 0.0 copy-done.3
  89.1 0.0 copy-done.5
  89.1 2.3 %final.1 = (f32[16,128]{1,0:T(8,128)}, f32[3,128]{1,0:T(4,128)S(1)}) custom-call(f32[2,4,129,128]{3,2,1,0:T(8,128)S(1)} %bitcast.12, f32[2,2,136,128]{3,2,1,0:T(8,128)S(1)} %get-tuple-element.18.fours, f32[2,4,136,128]{3,2,1,0:T(8,128)S(1)} %get-tuple-element.19.twos, f32[8,138,128]{2,1,0:T(8,128)S(1)} %all_to_all.32.parts, f32[2,8,120,128]{3,2,1,0:T(8,128)S(1)} %bitcast.11, ...), custom_call_target="tpu_custom_call" | custom-call | tf_op jit(solution)/shard_map/final/pallas_call | solution.py:353
  91.4 10.2 %all_to_all.34 = f32[16,3,128]{2,1,0:T(4,128)S(1)} all-to-all(f32[16,3,128]{2,1,0:T(4,128)S(1)} %broadcast_in_dim.13), channel_id=1, replica_groups=mesh['zh'=4,'zl'=2,'x'=4,'y'=8,'c'=2] {'y','c'}, dimensions={0} | all-to-all | bytes 49152 | tf_op jit(solution)/shard_map/all_to_all | solution.py:278
  101.7 12.0 %all_to_all.35.parts = f32[32,3,128]{2,1,0:T(4,128)S(1)} all-to-all(f32[32,3,128]{2,1,0:T(4,128)S(1)} %broadcast_in_dim.14), channel_id=1, replica_groups=mesh['zh'=4,'zl'=2,'x'=4,'y'=8,'c'=2] {'zh','zl','x'}, dimensions={0} | all-to-all | bytes 98304 | tf_op jit(solution)/shard_map/all_to_all | solution.py:278
  113.7 0.8 tail.1
  (11 shorter events, 0.3 us)
Async XLA Ops:
  27.0 18.0 %copy-start.4 = (f32[128]{0:T(128)S(1)}, f32[128]{0:T(128)}, u32[]{:S(2)}) copy-start(f32[128]{0:T(128)} %param.14) | copy-start | bytes 1540
  27.1 17.9 %copy-start.6 = (f32[128]{0:T(128)S(1)}, f32[128]{0:T(128)}, u32[]{:S(2)}) copy-start(f32[128]{0:T(128)} %param.13) | copy-start | bytes 1540
  27.1 17.9 %copy-start.7 = (f32[128]{0:T(128)S(1)}, f32[128]{0:T(128)}, u32[]{:S(2)}) copy-start(f32[128]{0:T(128)} %param.12) | copy-start | bytes 1540
  65.8 23.4 %copy-start = (bf16[1024,128]{1,0:T(8,128)(2,1)S(1)}, bf16[1024,128]{1,0:T(8,128)(2,1)}, u32[]{:S(2)}) copy-start(bf16[1024,128]{1,0:T(8,128)(2,1)} %loadings.1) | copy-start | bytes 786436
  65.8 23.3 %copy-start.1 = (s32[16,1024]{1,0:T(8,128)S(1)}, s32[16,1024]{1,0:T(8,128)}, u32[]{:S(2)}) copy-start(s32[16,1024]{1,0:T(8,128)} %present.1) | copy-start | bytes 196612
  65.8 23.3 %copy-start.2 = (bf16[16,1024]{1,0:T(8,128)(2,1)S(1)}, bf16[16,1024]{1,0:T(8,128)(2,1)}, u32[]{:S(2)}) copy-start(bf16[16,1024]{1,0:T(8,128)(2,1)} %readings.1) | copy-start | bytes 98308
  65.8 23.3 %copy-start.3 = (f32[1024]{0:T(1024)S(1)}, f32[1024]{0:T(1024)}, u32[]{:S(2)}) copy-start(f32[1024]{0:T(1024)} %param.11) | copy-start | bytes 12292
  65.8 23.3 %copy-start.5 = (s32[1024]{0:T(1024)S(1)}, s32[1024]{0:T(1024)}, u32[]{:S(2)}) copy-start(s32[1024]{0:T(1024)} %param.15) | copy-start | bytes 12292

commit v11 on v10

--- a/solution.py
+++ b/solution.py
@@ -58,8 +58,10 @@
     readings_hbm, present_hbm, loadings_hbm, noise_hbm, kept, sent,
     readings, present, loadings, noise, seen, scores, sems,
 ):
+    quarter = loadings.shape[0] // 4
+    spans = [pl.ds(i * quarter, quarter) for i in range(4)]
     pairs = (
-        (loadings_hbm, loadings),
+        *((loadings_hbm.at[span], loadings.at[span]) for span in spans),
         (noise_hbm, noise),
         (present_hbm, present),
         (readings_hbm, readings),
@@ -70,13 +72,13 @@
     core = lax.axis_index("c")
     count, _, k = kept.shape
     half = k // 2
-    copies[0].wait()
-    copies[1].wait()
+    for copy in copies[:5]:
+        copy.wait()
     load = loadings[...]
-    scaled = (jnp.transpose(load.astype(F32)) * noise[...]).astype(BF16)
-    copies[2].wait()
+    scaled = (jnp.transpose(load).astype(F32) * noise[...]).astype(BF16)
+    copies[5].wait()
     seen[...] = present[...].astype(F32)
-    copies[3].wait()
+    copies[6].wait()
     scores[...] = across(readings[...] * seen[...].astype(BF16), scaled)
     row, lane = iotas(half, k)
     row_k, lane_k = iotas(k, k)
@@ -309,7 +311,7 @@
             pltpu.VMEM((1, series), F32),
             pltpu.VMEM((hours, series), F32),
             pltpu.VMEM((hours, k), F32),
-            pltpu.SemaphoreType.DMA((4,)),
+            pltpu.SemaphoreType.DMA((7,)),
         ],
         compiler_params=PARAMS,
         name="information",

time: 115 us -> 115 us (level)
  no operation moved by 1% of the time
where the time goes in v11:
time: 115 us; the launch traced here: 114 us
  blocking collectives  105 us (91%)
  Pallas kernels  8.21 us (7%)
    all_to_all x5, blocking collectives, sent_to_all(): lax.all_to_all(jnp.broadcast_to(shard[None], (count, *shard.shape)), axis...  69 us
    all_to_all x1, blocking collectives, body(): lax.all_to_all(kept + arrived[:, :height], 'y', 0, 0, tiled=True)  15 us
    all_gather x1, blocking collectives, body(): lax.all_gather(sent, 'c')  8.73 us
    all_gather x1, blocking collectives, body(): packed = lax.all_gather(packed, 'c').reshape(hours, padded, k)  4.34 us
    all_gather x1, blocking collectives, body(): planes = lax.all_gather(sent_to_all(half_total, 'zh'), 'c')  4.23 us
    all_gather x1, blocking collectives, body(): sides = lax.all_gather(parts[:, :k - 8], 'c')  3.84 us
    pallas_call x1, Pallas kernels, body(): pl.pallas_call(information_kernel, out_shape=[shape_of(share, height, k),...  2.51 us

profile of v11, /device:TPU:1, one launch (start us, length us, event | category | flops | bytes accessed | tf_op | source)
XLA Modules:
  0.0 114.4 jit_solution(7400875720719959942)
XLA Ops:
  0.6 2.5 %information.1 = (f32[8,66,128]{2,1,0:T(8,128)S(1)}, f32[8,72,128]{2,1,0:T(8,128)S(1)}) custom-call(bf16[16,1024]{1,0:T(8,128)(2,1)} %readings.1, s32[16,1024]{1,0:T(8,128)} %present.1, bf16[1024,128]{1,0:T(8,128)(2,1)} %loadings.1, f32[1,1024]{1,0:T(1,128)} %bitcast.13), custom_call_target="tpu_custom_call" | custom-call | tf_op jit(solution)/shard_map/information/pallas_call | solution.py:302
  3.1 8.7 %all-gather = f32[16,72,128]{2,1,0:T(8,128)S(1)} all-gather(f32[8,72,128]{2,1,0:T(8,128)S(1)} %get-tuple-element.15), channel_id=2, replica_groups=mesh['zh'=4,'zl'=2,'x'=4,'y'=8,'c'=2] {'c'}, dimensions={0}, use_global_device_ids=true | all-gather | bytes 884736 | tf_op jit(solution)/shard_map/all_gather | solution.py:319
  11.9 15.0 %all_to_all.30 = f32[8,66,128]{2,1,0:T(8,128)S(1)} all-to-all(f32[8,66,128]{2,1,0:T(8,128)S(1)} %slice_add_fusion), channel_id=1, replica_groups=mesh['zh'=4,'zl'=2,'x'=4,'y'=8,'c'=2] {'y'}, dimensions={0} | all-to-all | bytes 540672 | tf_op jit(solution)/shard_map/all_to_all | solution.py:320
  27.0 0.0 copy-start.4
  27.1 0.0 copy-start.6
  27.1 0.0 copy-start.7
  27.1 13.5 %all_to_all.31 = f32[8,66,128]{2,1,0:T(8,128)S(1)} all-to-all(f32[8,66,128]{2,1,0:T(8,128)S(1)} %broadcast_in_dim.10), channel_id=1, replica_groups=mesh['zh'=4,'zl'=2,'x'=4,'y'=8,'c'=2] {'y'}, dimensions={0} | all-to-all | bytes 540672 | tf_op jit(solution)/shard_map/all_to_all | solution.py:280
  40.6 4.3 %all-gather.1.packed = f32[16,72,128]{2,1,0:T(8,128)S(1)} all-gather(f32[8,72,128]{2,1,0:T(8,128)S(1)} %pad.4), channel_id=3, replica_groups=mesh['zh'=4,'zl'=2,'x'=4,'y'=8,'c'=2] {'c'}, dimensions={0}, use_global_device_ids=true | all-gather | bytes 884736 | tf_op jit(solution)/shard_map/all_gather | solution.py:322
  45.0 0.0 copy-done.4
  45.0 0.0 copy-done.6
  45.0 0.0 copy-done.7
  45.0 1.8 %block.1 = (f32[16,136,128]{2,1,0:T(8,128)S(1)}, f32[8,136,128]{2,1,0:T(8,128)S(1)}, f32[4,136,128]{2,1,0:T(8,128)S(1)}, f32[2,136,128]{2,1,0:T(8,128)S(1)}, f32[138,128]{1,0:T(8,128)S(1)}) custom-call(f32[16,72,128]{2,1,0:T(8,128)S(1)} %all-gather.1.packed, f32[1,128]{1,0:T(1,128)S(1)} %bitcast.21, f32[1,128]{1,0:T(1,128)S(1)} %bitcast.19, ...), custom_call_target="tpu_custom_call" | custom-call | tf_op jit(solution)/shard_map/block/pallas_call | solution.py:325
  46.9 14.2 %all_to_all.32.parts = f32[8,138,128]{2,1,0:T(8,128)S(1)} all-to-all(f32[8,138,128]{2,1,0:T(8,128)S(1)} %broadcast_in_dim.11), channel_id=1, replica_groups=mesh['zh'=4,'zl'=2,'x'=4,'y'=8,'c'=2] {'zl','x'}, dimensions={0} | all-to-all | bytes 1130496 | tf_op jit(solution)/shard_map/all_to_all | solution.py:280
  61.1 3.8 %all-gather.2 = f32[16,120,128]{2,1,0:T(8,128)S(1)} all-gather(f32[8,120,128]{2,1,0:T(8,128)S(1)} %slice.9), channel_id=4, replica_groups=mesh['zh'=4,'zl'=2,'x'=4,'y'=8,'c'=2] {'c'}, dimensions={0}, use_global_device_ids=true | all-gather | bytes 1474560 | tf_op jit(solution)/shard_map/all_gather | solution.py:336
  64.9 0.8 near.1
  65.8 0.0 copy-start
  65.8 0.0 copy-start.1
  65.8 0.0 copy-start.2
  65.8 0.0 copy-start.3
  65.8 0.0 copy-start.5
  65.8 19.0 %all_to_all.33 = f32[4,129,128]{2,1,0:T(8,128)S(1)} all-to-all(f32[4,129,128]{2,1,0:T(8,128)S(1)} %broadcast_in_dim.12), channel_id=1, replica_groups=mesh['zh'=4,'zl'=2,'x'=4,'y'=8,'c'=2] {'zh'}, dimensions={0} | all-to-all | bytes 528384 | tf_op jit(solution)/shard_map/all_to_all | solution.py:280
  84.9 4.2 %all-gather.3 = f32[8,129,128]{2,1,0:T(8,128)S(1)} all-gather(f32[4,129,128]{2,1,0:T(8,128)S(1)} %all_to_all.33), channel_id=5, replica_groups=mesh['zh'=4,'zl'=2,'x'=4,'y'=8,'c'=2] {'c'}, dimensions={0}, use_global_device_ids=true | all-gather | bytes 792576 | tf_op jit(solution)/shard_map/all_gather | solution.py:350
  89.1 0.0 copy-done
  89.1 0.0 copy-done.1
  89.1 0.0 copy-done.2
  89.1 0.0 copy-done.3
  89.1 0.0 copy-done.5
  89.1 2.3 %final.1 = (f32[16,128]{1,0:T(8,128)}, f32[3,128]{1,0:T(4,128)S(1)}) custom-call(f32[2,4,129,128]{3,2,1,0:T(8,128)S(1)} %bitcast.12, f32[2,2,136,128]{3,2,1,0:T(8,128)S(1)} %get-tuple-element.18.fours, f32[2,4,136,128]{3,2,1,0:T(8,128)S(1)} %get-tuple-element.19.twos, f32[8,138,128]{2,1,0:T(8,128)S(1)} %all_to_all.32.parts, f32[2,8,120,128]{3,2,1,0:T(8,128)S(1)} %bitcast.11, ...), custom_call_target="tpu_custom_call" | custom-call | tf_op jit(solution)/shard_map/final/pallas_call | solution.py:355
  91.4 10.2 %all_to_all.34 = f32[16,3,128]{2,1,0:T(4,128)S(1)} all-to-all(f32[16,3,128]{2,1,0:T(4,128)S(1)} %broadcast_in_dim.13), channel_id=1, replica_groups=mesh['zh'=4,'zl'=2,'x'=4,'y'=8,'c'=2] {'y','c'}, dimensions={0} | all-to-all | bytes 49152 | tf_op jit(solution)/shard_map/all_to_all | solution.py:280
  101.7 12.0 %all_to_all.35.parts = f32[32,3,128]{2,1,0:T(4,128)S(1)} all-to-all(f32[32,3,128]{2,1,0:T(4,128)S(1)} %broadcast_in_dim.14), channel_id=1, replica_groups=mesh['zh'=4,'zl'=2,'x'=4,'y'=8,'c'=2] {'zh','zl','x'}, dimensions={0} | all-to-all | bytes 98304 | tf_op jit(solution)/shard_map/all_to_all | solution.py:280
  113.7 0.8 tail.1
  (11 shorter events, 0.3 us)
Async XLA Ops:
  27.0 18.0 %copy-start.4 = (f32[128]{0:T(128)S(1)}, f32[128]{0:T(128)}, u32[]{:S(2)}) copy-start(f32[128]{0:T(128)} %param.14) | copy-start | bytes 1540
  27.1 17.9 %copy-start.6 = (f32[128]{0:T(128)S(1)}, f32[128]{0:T(128)}, u32[]{:S(2)}) copy-start(f32[128]{0:T(128)} %param.13) | copy-start | bytes 1540
  27.1 17.9 %copy-start.7 = (f32[128]{0:T(128)S(1)}, f32[128]{0:T(128)}, u32[]{:S(2)}) copy-start(f32[128]{0:T(128)} %param.12) | copy-start | bytes 1540
  65.8 23.4 %copy-start = (bf16[1024,128]{1,0:T(8,128)(2,1)S(1)}, bf16[1024,128]{1,0:T(8,128)(2,1)}, u32[]{:S(2)}) copy-start(bf16[1024,128]{1,0:T(8,128)(2,1)} %loadings.1) | copy-start | bytes 786436
  65.8 23.3 %copy-start.1 = (s32[16,1024]{1,0:T(8,128)S(1)}, s32[16,1024]{1,0:T(8,128)}, u32[]{:S(2)}) copy-start(s32[16,1024]{1,0:T(8,128)} %present.1) | copy-start | bytes 196612
  65.8 23.3 %copy-start.2 = (bf16[16,1024]{1,0:T(8,128)(2,1)S(1)}, bf16[16,1024]{1,0:T(8,128)(2,1)}, u32[]{:S(2)}) copy-start(bf16[16,1024]{1,0:T(8,128)(2,1)} %readings.1) | copy-start | bytes 98308
  65.8 23.3 %copy-start.3 = (f32[1024]{0:T(1024)S(1)}, f32[1024]{0:T(1024)}, u32[]{:S(2)}) copy-start(f32[1024]{0:T(1024)} %param.11) | copy-start | bytes 12292
  65.8 23.3 %copy-start.5 = (s32[1024]{0:T(1024)S(1)}, s32[1024]{0:T(1024)}, u32[]{:S(2)}) copy-start(s32[1024]{0:T(1024)} %param.15) | copy-start | bytes 12292

commit v12 on v10

--- a/solution.py
+++ b/solution.py
@@ -362,7 +362,7 @@
         readings, present, loadings, noise, regions.reshape(1, series), scale,
     )
 
-    local = sent_to_all(local, SERIES).sum(axis=0)
+    local = sent_to_all(local, ("zl", *SERIES)).sum(axis=0)
     histogram = pl.pallas_call(
         tail_kernel,
         out_shape=shape_of(GROUPS, BINS),
@@ -370,7 +370,7 @@
         out_specs=VM,
         compiler_params=PARAMS,
         name="tail",
-    )(sent_to_all(local, TM))
+    )(sent_to_all(local, ("zh", "x")))
     return (smoothed, histogram)
 
 

time: 115 us -> 116 us (level)
  no operation moved by 1% of the time
where the time goes in v12:
time: 116 us; the launch traced here: 115 us
  blocking collectives  106 us (91%)
  Pallas kernels  8.19 us (7%)
    all_to_all x5, blocking collectives, sent_to_all(): lax.all_to_all(jnp.broadcast_to(shard[None], (count, *shard.shape)), axis...  69.7 us
    all_to_all x1, blocking collectives, body(): lax.all_to_all(kept + arrived[:, :height], 'y', 0, 0, tiled=True)  15 us
    all_gather x1, blocking collectives, body(): lax.all_gather(sent, 'c')  8.73 us
    all_gather x1, blocking collectives, body(): packed = lax.all_gather(packed, 'c').reshape(hours, padded, k)  4.34 us
    all_gather x1, blocking collectives, body(): planes = lax.all_gather(sent_to_all(half_total, 'zh'), 'c')  4.23 us
    all_gather x1, blocking collectives, body(): sides = lax.all_gather(parts[:, :k - 8], 'c')  3.84 us
    pallas_call x1, Pallas kernels, body(): pl.pallas_call(information_kernel, out_shape=[shape_of(share, height, k),...  2.51 us

profile of v12, /device:TPU:1, one launch (start us, length us, event | category | flops | bytes accessed | tf_op | source)
XLA Modules:
  0.0 115.2 jit_solution(4721046631696265300)
XLA Ops:
  0.6 2.5 %information.1 = (f32[8,66,128]{2,1,0:T(8,128)S(1)}, f32[8,72,128]{2,1,0:T(8,128)S(1)}) custom-call(bf16[16,1024]{1,0:T(8,128)(2,1)} %readings.1, s32[16,1024]{1,0:T(8,128)} %present.1, bf16[1024,128]{1,0:T(8,128)(2,1)} %loadings.1, f32[1,1024]{1,0:T(1,128)} %bitcast.13), custom_call_target="tpu_custom_call" | custom-call | tf_op jit(solution)/shard_map/information/pallas_call | solution.py:300
  3.1 8.7 %all-gather = f32[16,72,128]{2,1,0:T(8,128)S(1)} all-gather(f32[8,72,128]{2,1,0:T(8,128)S(1)} %get-tuple-element.15), channel_id=2, replica_groups=mesh['zh'=4,'zl'=2,'x'=4,'y'=8,'c'=2] {'c'}, dimensions={0}, use_global_device_ids=true | all-gather | bytes 884736 | tf_op jit(solution)/shard_map/all_gather | solution.py:317
  11.9 15.0 %all_to_all.30 = f32[8,66,128]{2,1,0:T(8,128)S(1)} all-to-all(f32[8,66,128]{2,1,0:T(8,128)S(1)} %slice_add_fusion), channel_id=1, replica_groups=mesh['zh'=4,'zl'=2,'x'=4,'y'=8,'c'=2] {'y'}, dimensions={0} | all-to-all | bytes 540672 | tf_op jit(solution)/shard_map/all_to_all | solution.py:318
  27.0 0.0 copy-start.4
  27.1 0.0 copy-start.6
  27.1 0.0 copy-start.7
  27.1 13.5 %all_to_all.31 = f32[8,66,128]{2,1,0:T(8,128)S(1)} all-to-all(f32[8,66,128]{2,1,0:T(8,128)S(1)} %broadcast_in_dim.10), channel_id=1, replica_groups=mesh['zh'=4,'zl'=2,'x'=4,'y'=8,'c'=2] {'y'}, dimensions={0} | all-to-all | bytes 540672 | tf_op jit(solution)/shard_map/all_to_all | solution.py:278
  40.6 4.3 %all-gather.1.packed = f32[16,72,128]{2,1,0:T(8,128)S(1)} all-gather(f32[8,72,128]{2,1,0:T(8,128)S(1)} %pad.4), channel_id=3, replica_groups=mesh['zh'=4,'zl'=2,'x'=4,'y'=8,'c'=2] {'c'}, dimensions={0}, use_global_device_ids=true | all-gather | bytes 884736 | tf_op jit(solution)/shard_map/all_gather | solution.py:320
  45.0 0.0 copy-done.4
  45.0 0.0 copy-done.6
  45.0 0.0 copy-done.7
  45.0 1.8 %block.1 = (f32[16,136,128]{2,1,0:T(8,128)S(1)}, f32[8,136,128]{2,1,0:T(8,128)S(1)}, f32[4,136,128]{2,1,0:T(8,128)S(1)}, f32[2,136,128]{2,1,0:T(8,128)S(1)}, f32[138,128]{1,0:T(8,128)S(1)}) custom-call(f32[16,72,128]{2,1,0:T(8,128)S(1)} %all-gather.1.packed, f32[1,128]{1,0:T(1,128)S(1)} %bitcast.21, f32[1,128]{1,0:T(1,128)S(1)} %bitcast.19, ...), custom_call_target="tpu_custom_call" | custom-call | tf_op jit(solution)/shard_map/block/pallas_call | solution.py:323
  46.9 14.2 %all_to_all.32.parts = f32[8,138,128]{2,1,0:T(8,128)S(1)} all-to-all(f32[8,138,128]{2,1,0:T(8,128)S(1)} %broadcast_in_dim.11), channel_id=1, replica_groups=mesh['zh'=4,'zl'=2,'x'=4,'y'=8,'c'=2] {'zl','x'}, dimensions={0} | all-to-all | bytes 1130496 | tf_op jit(solution)/shard_map/all_to_all | solution.py:278
  61.1 3.8 %all-gather.2 = f32[16,120,128]{2,1,0:T(8,128)S(1)} all-gather(f32[8,120,128]{2,1,0:T(8,128)S(1)} %slice.9), channel_id=4, replica_groups=mesh['zh'=4,'zl'=2,'x'=4,'y'=8,'c'=2] {'c'}, dimensions={0}, use_global_device_ids=true | all-gather | bytes 1474560 | tf_op jit(solution)/shard_map/all_gather | solution.py:334
  64.9 0.8 near.1
  65.8 0.0 copy-start
  65.8 0.0 copy-start.1
  65.8 0.0 copy-start.2
  65.8 0.0 copy-start.3
  65.8 0.0 copy-start.5
  65.9 19.0 %all_to_all.33 = f32[4,129,128]{2,1,0:T(8,128)S(1)} all-to-all(f32[4,129,128]{2,1,0:T(8,128)S(1)} %broadcast_in_dim.12), channel_id=1, replica_groups=mesh['zh'=4,'zl'=2,'x'=4,'y'=8,'c'=2] {'zh'}, dimensions={0} | all-to-all | bytes 528384 | tf_op jit(solution)/shard_map/all_to_all | solution.py:278
  84.9 4.2 %all-gather.3 = f32[8,129,128]{2,1,0:T(8,128)S(1)} all-gather(f32[4,129,128]{2,1,0:T(8,128)S(1)} %all_to_all.33), channel_id=5, replica_groups=mesh['zh'=4,'zl'=2,'x'=4,'y'=8,'c'=2] {'c'}, dimensions={0}, use_global_device_ids=true | all-gather | bytes 792576 | tf_op jit(solution)/shard_map/all_gather | solution.py:348
  89.1 0.0 copy-done
  89.1 0.0 copy-done.1
  89.1 0.0 copy-done.2
  89.1 0.0 copy-done.3
  89.1 0.0 copy-done.5
  89.1 2.3 %final.1 = (f32[16,128]{1,0:T(8,128)}, f32[3,128]{1,0:T(4,128)S(1)}) custom-call(f32[2,4,129,128]{3,2,1,0:T(8,128)S(1)} %bitcast.12, f32[2,2,136,128]{3,2,1,0:T(8,128)S(1)} %get-tuple-element.18.fours, f32[2,4,136,128]{3,2,1,0:T(8,128)S(1)} %get-tuple-element.19.twos, f32[8,138,128]{2,1,0:T(8,128)S(1)} %all_to_all.32.parts, f32[2,8,120,128]{3,2,1,0:T(8,128)S(1)} %bitcast.11, ...), custom_call_target="tpu_custom_call" | custom-call | tf_op jit(solution)/shard_map/final/pallas_call | solution.py:353
  91.4 11.2 %all_to_all.34 = f32[32,3,128]{2,1,0:T(4,128)S(1)} all-to-all(f32[32,3,128]{2,1,0:T(4,128)S(1)} %broadcast_in_dim.13), channel_id=1, replica_groups=mesh['zh'=4,'zl'=2,'x'=4,'y'=8,'c'=2] {'zl','y','c'}, dimensions={0} | all-to-all | bytes 98304 | tf_op jit(solution)/shard_map/all_to_all | solution.py:278
  102.7 11.7 %all_to_all.35.parts = f32[16,3,128]{2,1,0:T(4,128)S(1)} all-to-all(f32[16,3,128]{2,1,0:T(4,128)S(1)} %broadcast_in_dim.14), channel_id=1, replica_groups=mesh['zh'=4,'zl'=2,'x'=4,'y'=8,'c'=2] {'zh','x'}, dimensions={0} | all-to-all | bytes 49152 | tf_op jit(solution)/shard_map/all_to_all | solution.py:278
  114.4 0.8 tail.1
  (11 shorter events, 0.3 us)
Async XLA Ops:
  27.0 18.0 %copy-start.4 = (f32[128]{0:T(128)S(1)}, f32[128]{0:T(128)}, u32[]{:S(2)}) copy-start(f32[128]{0:T(128)} %param.14) | copy-start | bytes 1540
  27.1 17.9 %copy-start.6 = (f32[128]{0:T(128)S(1)}, f32[128]{0:T(128)}, u32[]{:S(2)}) copy-start(f32[128]{0:T(128)} %param.13) | copy-start | bytes 1540
  27.1 17.9 %copy-start.7 = (f32[128]{0:T(128)S(1)}, f32[128]{0:T(128)}, u32[]{:S(2)}) copy-start(f32[128]{0:T(128)} %param.12) | copy-start | bytes 1540
  65.8 23.4 %copy-start = (bf16[1024,128]{1,0:T(8,128)(2,1)S(1)}, bf16[1024,128]{1,0:T(8,128)(2,1)}, u32[]{:S(2)}) copy-start(bf16[1024,128]{1,0:T(8,128)(2,1)} %loadings.1) | copy-start | bytes 786436
  65.8 23.3 %copy-start.1 = (s32[16,1024]{1,0:T(8,128)S(1)}, s32[16,1024]{1,0:T(8,128)}, u32[]{:S(2)}) copy-start(s32[16,1024]{1,0:T(8,128)} %present.1) | copy-start | bytes 196612
  65.8 23.3 %copy-start.2 = (bf16[16,1024]{1,0:T(8,128)(2,1)S(1)}, bf16[16,1024]{1,0:T(8,128)(2,1)}, u32[]{:S(2)}) copy-start(bf16[16,1024]{1,0:T(8,128)(2,1)} %readings.1) | copy-start | bytes 98308
  65.8 23.3 %copy-start.3 = (f32[1024]{0:T(1024)S(1)}, f32[1024]{0:T(1024)}, u32[]{:S(2)}) copy-start(f32[1024]{0:T(1024)} %param.11) | copy-start | bytes 12292
  65.8 23.3 %copy-start.5 = (s32[1024]{0:T(1024)S(1)}, s32[1024]{0:T(1024)}, u32[]{:S(2)}) copy-start(s32[1024]{0:T(1024)} %param.15) | copy-start | bytes 12292

commit v13 on v12

--- a/solution.py
+++ b/solution.py
@@ -362,7 +362,7 @@
         readings, present, loadings, noise, regions.reshape(1, series), scale,
     )
 
-    local = sent_to_all(local, ("zl", *SERIES)).sum(axis=0)
+    local = sent_to_all(local, TM).sum(axis=0)
     histogram = pl.pallas_call(
         tail_kernel,
         out_shape=shape_of(GROUPS, BINS),
@@ -370,7 +370,7 @@
         out_specs=VM,
         compiler_params=PARAMS,
         name="tail",
-    )(sent_to_all(local, ("zh", "x")))
+    )(sent_to_all(local, SERIES))
     return (smoothed, histogram)
 
 

time: 116 us -> 116 us (level)
  no operation moved by 1% of the time
where the time goes in v13:
time: 116 us
  blocking collectives  107 us (92%)
  Pallas kernels  8.19 us (7%)
    all_to_all x5, blocking collectives, sent_to_all(): lax.all_to_all(jnp.broadcast_to(shard[None], (count, *shard.shape)), axis...  70.4 us
    all_to_all x1, blocking collectives, body(): lax.all_to_all(kept + arrived[:, :height], 'y', 0, 0, tiled=True)  15 us
    all_gather x1, blocking collectives, body(): lax.all_gather(sent, 'c')  8.73 us
    all_gather x1, blocking collectives, body(): packed = lax.all_gather(packed, 'c').reshape(hours, padded, k)  4.34 us
    all_gather x1, blocking collectives, body(): planes = lax.all_gather(sent_to_all(half_total, 'zh'), 'c')  4.23 us
    all_gather x1, blocking collectives, body(): sides = lax.all_gather(parts[:, :k - 8], 'c')  3.84 us
    pallas_call x1, Pallas kernels, body(): pl.pallas_call(information_kernel, out_shape=[shape_of(share, height, k),...  2.51 us

profile of v13, /device:TPU:1, one launch (start us, length us, event | category | flops | bytes accessed | tf_op | source)
XLA Modules:
  0.0 115.9 jit_solution(880008059676243298)
XLA Ops:
  0.6 2.5 %information.1 = (f32[8,66,128]{2,1,0:T(8,128)S(1)}, f32[8,72,128]{2,1,0:T(8,128)S(1)}) custom-call(bf16[16,1024]{1,0:T(8,128)(2,1)} %readings.1, s32[16,1024]{1,0:T(8,128)} %present.1, bf16[1024,128]{1,0:T(8,128)(2,1)} %loadings.1, f32[1,1024]{1,0:T(1,128)} %bitcast.13), custom_call_target="tpu_custom_call" | custom-call | tf_op jit(solution)/shard_map/information/pallas_call | solution.py:300
  3.1 8.7 %all-gather = f32[16,72,128]{2,1,0:T(8,128)S(1)} all-gather(f32[8,72,128]{2,1,0:T(8,128)S(1)} %get-tuple-element.15), channel_id=2, replica_groups=mesh['zh'=4,'zl'=2,'x'=4,'y'=8,'c'=2] {'c'}, dimensions={0}, use_global_device_ids=true | all-gather | bytes 884736 | tf_op jit(solution)/shard_map/all_gather | solution.py:317
  11.9 15.0 %all_to_all.30 = f32[8,66,128]{2,1,0:T(8,128)S(1)} all-to-all(f32[8,66,128]{2,1,0:T(8,128)S(1)} %slice_add_fusion), channel_id=1, replica_groups=mesh['zh'=4,'zl'=2,'x'=4,'y'=8,'c'=2] {'y'}, dimensions={0} | all-to-all | bytes 540672 | tf_op jit(solution)/shard_map/all_to_all | solution.py:318
  27.0 0.0 copy-start.4
  27.1 0.0 copy-start.6
  27.1 0.0 copy-start.7
  27.1 13.5 %all_to_all.31 = f32[8,66,128]{2,1,0:T(8,128)S(1)} all-to-all(f32[8,66,128]{2,1,0:T(8,128)S(1)} %broadcast_in_dim.10), channel_id=1, replica_groups=mesh['zh'=4,'zl'=2,'x'=4,'y'=8,'c'=2] {'y'}, dimensions={0} | all-to-all | bytes 540672 | tf_op jit(solution)/shard_map/all_to_all | solution.py:278
  40.6 4.3 %all-gather.1.packed = f32[16,72,128]{2,1,0:T(8,128)S(1)} all-gather(f32[8,72,128]{2,1,0:T(8,128)S(1)} %pad.4), channel_id=3, replica_groups=mesh['zh'=4,'zl'=2,'x'=4,'y'=8,'c'=2] {'c'}, dimensions={0}, use_global_device_ids=true | all-gather | bytes 884736 | tf_op jit(solution)/shard_map/all_gather | solution.py:320
  45.0 0.0 copy-done.4
  45.0 0.0 copy-done.6
  45.0 0.0 copy-done.7
  45.0 1.8 %block.1 = (f32[16,136,128]{2,1,0:T(8,128)S(1)}, f32[8,136,128]{2,1,0:T(8,128)S(1)}, f32[4,136,128]{2,1,0:T(8,128)S(1)}, f32[2,136,128]{2,1,0:T(8,128)S(1)}, f32[138,128]{1,0:T(8,128)S(1)}) custom-call(f32[16,72,128]{2,1,0:T(8,128)S(1)} %all-gather.1.packed, f32[1,128]{1,0:T(1,128)S(1)} %bitcast.21, f32[1,128]{1,0:T(1,128)S(1)} %bitcast.19, ...), custom_call_target="tpu_custom_call" | custom-call | tf_op jit(solution)/shard_map/block/pallas_call | solution.py:323
  46.9 14.2 %all_to_all.32.parts = f32[8,138,128]{2,1,0:T(8,128)S(1)} all-to-all(f32[8,138,128]{2,1,0:T(8,128)S(1)} %broadcast_in_dim.11), channel_id=1, replica_groups=mesh['zh'=4,'zl'=2,'x'=4,'y'=8,'c'=2] {'zl','x'}, dimensions={0} | all-to-all | bytes 1130496 | tf_op jit(solution)/shard_map/all_to_all | solution.py:278
  61.1 3.8 %all-gather.2 = f32[16,120,128]{2,1,0:T(8,128)S(1)} all-gather(f32[8,120,128]{2,1,0:T(8,128)S(1)} %slice.9), channel_id=4, replica_groups=mesh['zh'=4,'zl'=2,'x'=4,'y'=8,'c'=2] {'c'}, dimensions={0}, use_global_device_ids=true | all-gather | bytes 1474560 | tf_op jit(solution)/shard_map/all_gather | solution.py:334
  64.9 0.8 near.1
  65.8 0.0 copy-start
  65.8 0.0 copy-start.1
  65.8 0.0 copy-start.2
  65.8 0.0 copy-start.3
  65.8 0.0 copy-start.5
  65.9 19.0 %all_to_all.33 = f32[4,129,128]{2,1,0:T(8,128)S(1)} all-to-all(f32[4,129,128]{2,1,0:T(8,128)S(1)} %broadcast_in_dim.12), channel_id=1, replica_groups=mesh['zh'=4,'zl'=2,'x'=4,'y'=8,'c'=2] {'zh'}, dimensions={0} | all-to-all | bytes 528384 | tf_op jit(solution)/shard_map/all_to_all | solution.py:278
  84.9 4.2 %all-gather.3 = f32[8,129,128]{2,1,0:T(8,128)S(1)} all-gather(f32[4,129,128]{2,1,0:T(8,128)S(1)} %all_to_all.33), channel_id=5, replica_groups=mesh['zh'=4,'zl'=2,'x'=4,'y'=8,'c'=2] {'c'}, dimensions={0}, use_global_device_ids=true | all-gather | bytes 792576 | tf_op jit(solution)/shard_map/all_gather | solution.py:348
  89.1 0.0 copy-done
  89.1 0.0 copy-done.1
  89.1 0.0 copy-done.2
  89.1 0.0 copy-done.3
  89.1 0.0 copy-done.5
  89.1 2.3 %final.1 = (f32[16,128]{1,0:T(8,128)}, f32[3,128]{1,0:T(4,128)S(1)}) custom-call(f32[2,4,129,128]{3,2,1,0:T(8,128)S(1)} %bitcast.12, f32[2,2,136,128]{3,2,1,0:T(8,128)S(1)} %get-tuple-element.18.fours, f32[2,4,136,128]{3,2,1,0:T(8,128)S(1)} %get-tuple-element.19.twos, f32[8,138,128]{2,1,0:T(8,128)S(1)} %all_to_all.32.parts, f32[2,8,120,128]{3,2,1,0:T(8,128)S(1)} %bitcast.11, ...), custom_call_target="tpu_custom_call" | custom-call | tf_op jit(solution)/shard_map/final/pallas_call | solution.py:353
  91.4 12.0 %all_to_all.34 = f32[32,3,128]{2,1,0:T(4,128)S(1)} all-to-all(f32[32,3,128]{2,1,0:T(4,128)S(1)} %broadcast_in_dim.13), channel_id=1, replica_groups=mesh['zh'=4,'zl'=2,'x'=4,'y'=8,'c'=2] {'zh','zl','x'}, dimensions={0} | all-to-all | bytes 98304 | tf_op jit(solution)/shard_map/all_to_all | solution.py:278
  103.5 11.7 %all_to_all.35.parts = f32[16,3,128]{2,1,0:T(4,128)S(1)} all-to-all(f32[16,3,128]{2,1,0:T(4,128)S(1)} %broadcast_in_dim.14), channel_id=1, replica_groups=mesh['zh'=4,'zl'=2,'x'=4,'y'=8,'c'=2] {'y','c'}, dimensions={0} | all-to-all | bytes 49152 | tf_op jit(solution)/shard_map/all_to_all | solution.py:278
  115.1 0.8 tail.1
  (11 shorter events, 0.3 us)
Async XLA Ops:
  27.0 18.0 %copy-start.4 = (f32[128]{0:T(128)S(1)}, f32[128]{0:T(128)}, u32[]{:S(2)}) copy-start(f32[128]{0:T(128)} %param.14) | copy-start | bytes 1540
  27.1 17.9 %copy-start.6 = (f32[128]{0:T(128)S(1)}, f32[128]{0:T(128)}, u32[]{:S(2)}) copy-start(f32[128]{0:T(128)} %param.13) | copy-start | bytes 1540
  27.1 17.9 %copy-start.7 = (f32[128]{0:T(128)S(1)}, f32[128]{0:T(128)}, u32[]{:S(2)}) copy-start(f32[128]{0:T(128)} %param.12) | copy-start | bytes 1540
  65.8 23.4 %copy-start = (bf16[1024,128]{1,0:T(8,128)(2,1)S(1)}, bf16[1024,128]{1,0:T(8,128)(2,1)}, u32[]{:S(2)}) copy-start(bf16[1024,128]{1,0:T(8,128)(2,1)} %loadings.1) | copy-start | bytes 786436
  65.8 23.3 %copy-start.1 = (s32[16,1024]{1,0:T(8,128)S(1)}, s32[16,1024]{1,0:T(8,128)}, u32[]{:S(2)}) copy-start(s32[16,1024]{1,0:T(8,128)} %present.1) | copy-start | bytes 196612
  65.8 23.3 %copy-start.2 = (bf16[16,1024]{1,0:T(8,128)(2,1)S(1)}, bf16[16,1024]{1,0:T(8,128)(2,1)}, u32[]{:S(2)}) copy-start(bf16[16,1024]{1,0:T(8,128)(2,1)} %readings.1) | copy-start | bytes 98308
  65.8 23.3 %copy-start.3 = (f32[1024]{0:T(1024)S(1)}, f32[1024]{0:T(1024)}, u32[]{:S(2)}) copy-start(f32[1024]{0:T(1024)} %param.11) | copy-start | bytes 12292
  65.8 23.3 %copy-start.5 = (s32[1024]{0:T(1024)S(1)}, s32[1024]{0:T(1024)}, u32[]{:S(2)}) copy-start(s32[1024]{0:T(1024)} %param.15) | copy-start | bytes 12292
